TPU v7x, 256 devices: a whole 4x4x8 slice. The times are simulated.
256 devices in a mesh: samp: 16 (over z_hi, x), row: 4 (over y), col: 4 (over z_lo, core).
Axes of the slice: x: 4, y: 4, z: 8 (z_hi: 4, z_lo: 2; z = z_hi * 2 + z_lo), core: 2. Of those that a mesh axis runs over, the one named last changes fastest.
Arguments:
- pair_in: bfloat16 [128, 512, 512], P(None, 'row', 'col'), may hold values from -6 to 6
- token_act: bfloat16 [48, 512, 768], P('samp', 'row', 'col'), may hold values from -6 to 6
- single: bfloat16 [512, 384], P('row'), may hold values from -6 to 6
- noise_sigma: float32 [48], P('samp'), may hold values from 0.05 to 80
- token_mask: int32 [512], P('row'), may hold values 0 or 1
- tri_weight: bfloat16 [5, 128, 128], replicated, may hold values from -0.5 to 0.5
- out_weight: bfloat16 [128, 128], replicated, may hold values from -0.5 to 0.5
- bias_weight: bfloat16 [2, 128, 16], replicated, may hold values from -2 to 2
- time_weight: bfloat16 [256, 384], replicated, may hold values from -0.375 to 0.375
- mod_weight: bfloat16 [2, 6, 384, 768], P(None, None, None, 'col'), may hold values from -0.3125 to 0.3125
- query_weight: bfloat16 [2, 768, 768], P(None, None, 'col'), may hold values from -2 to 2
- key_weight: bfloat16 [2, 768, 768], P(None, None, 'col'), may hold values from -2 to 2
- value_gate_weight: bfloat16 [2, 2, 768, 768], P(None, None, None, 'col'), may hold values from -0.21875 to 0.21875
- attn_out_weight: bfloat16 [2, 768, 768], P(None, 'col'), may hold values from -0.21875 to 0.21875
- up_weight: bfloat16 [2, 2, 768, 1536], P(None, None, None, 'col'), may hold values from -0.21875 to 0.21875
- down_weight: bfloat16 [2, 1536, 768], P(None, 'col'), may hold values from -0.15625 to 0.15625
Outputs:
- pair_out: bfloat16 [128, 512, 512], P('samp', 'row', 'col')
- denoised: bfloat16 [48, 512, 768], P('samp', 'row', 'col')
Inputs may be any that keep to these rules, and one draw needn't show every extreme that they name: `token_mask`: 1 marks a token that queries attend to, 0 one that is left out.
All inputs are finite; a program needn't handle non-finite values. No bound on the sum of `token_mask` on one device may be relied on, other than what follows from the above.
Results may differ from a plain program's by a relative error of at most 0.019.
Values may be sent and summed in bfloat16 or wider, within the bound.
No kernel may reach another device: no remote copies, remote signals or barrier semaphores. Data moves between devices by JAX's collectives and lax.ppermute only.
A program may use at most 128 MiB of HBM per device.

v0:
```python
import math

import jax
import jax.numpy as jnp
from jax import lax
from jax.experimental import pallas as pl
from jax.experimental.pallas import tpu as pltpu
from jax.sharding import PartitionSpec as P

DA = 768
HEAD_DIM = 48
TEMB = 256


EPS = 1e-05
MASK_FILL = 1000000000.0
MIB = 1024 * 1024
CLAIM = 56
MASK_ROWS = 16


def channel_norm(values, axis):
    mean_value = jnp.mean(values, axis=axis, keepdims=True)
    centred = values - mean_value
    spread = jnp.mean(centred * centred, axis=axis, keepdims=True)
    return centred * lax.rsqrt(spread + EPS)


def swap(value, axis, flip):
    size = lax.axis_size(axis)
    return lax.ppermute(value, axis, [(k, k ^ flip) for k in range(size)])


def swap_all(value, axis):
    return [value] + [swap(value, axis, flip) for flip in range(1, lax.axis_size(axis))]


def local_call(kernel, out_shape, in_specs, args, scratch, flops, name, mib=CLAIM):
    moved = sum(a.size * a.dtype.itemsize for a in args)
    return pl.pallas_call(
        kernel,
        grid=(1,),
        out_shape=out_shape,
        in_specs=in_specs,
        out_specs=jax.tree.map(lambda o: whole(o.shape), out_shape),
        scratch_shapes=scratch,
        compiler_params=pltpu.CompilerParams(vmem_limit_bytes=mib * MIB),
        cost_estimate=pl.CostEstimate(flops=flops, bytes_accessed=moved, transcendentals=0),
        name=name,
    )(*args)


def whole(shape):
    return pl.BlockSpec(tuple(shape), lambda i: (0,) * len(shape))


def layer_block(shape, at, layer):
    block = tuple(1 if d == at else n for d, n in enumerate(shape))
    return pl.BlockSpec(block, lambda i: tuple(layer if d == at else 0 for d in range(len(shape))))


SCALAR = pl.BlockSpec(memory_space=pltpu.SMEM)
UNREAD = pl.BlockSpec(memory_space=pl.ANY)


def after(value, others):
    def kernel(*refs):
        refs[-1][...] = refs[0][...]

    return local_call(
        kernel,
        jax.ShapeDtypeStruct(value.shape, value.dtype),
        [whole(value.shape)] + [UNREAD] * len(others),
        [value, *others],
        [],
        0,
        "after",
    )


def stack_gathered(gathered, full):
    parts, samples, width, tokens = gathered.shape
    for k in range(parts):
        for s in range(samples):
            full[k * width : (k + 1) * width, s * tokens : (s + 1) * tokens] = gathered[k, s]


def stack_normed(gathered, shared, full, gain_at):
    parts, samples, width, tokens = gathered.shape
    for s in range(samples):
        value = jnp.concatenate([gathered[k, s] for k in range(parts)], 0).astype(jnp.float32)
        normed = channel_norm(value, 0)
        for k in range(parts):
            gain, shift = shared[k, gain_at, s], shared[k, gain_at + 1, s]
            piece = normed[k * width : (k + 1) * width]
            full[k * width : (k + 1) * width, s * tokens : (s + 1) * tokens] = (
                gain.astype(jnp.float32) * piece + shift.astype(jnp.float32)
            ).astype(jnp.bfloat16)


def fill(blocks, full, gain_at):
    if len(blocks) == 2:
        stack_normed(blocks[0], blocks[1], full, gain_at)
    else:
        stack_gathered(blocks[0], full)


def project_kernel(count, *refs):
    blocks = refs[:count]
    query_w, key_w, value_gate_w, mask, queries, gates, both, full = refs[count:]
    fill(blocks, full, 0)
    samples, width, tokens = queries.shape

    def times(weight):
        return jnp.dot(weight, full[...], preferred_element_type=jnp.float32).astype(jnp.bfloat16)

    query, gate = times(query_w[0]), times(value_gate_w[0, 1])
    key, value = times(key_w[0]), times(value_gate_w[0, 0])
    for s in range(samples):
        at = slice(s * tokens, (s + 1) * tokens)
        queries[s] = query[:, at]
        gates[s] = gate[:, at]
        both[2 * s * width : (2 * s + 1) * width] = key[:, at]
        both[(2 * s + 1) * width : (2 * s + 2) * width] = value[:, at]
    both[2 * samples * width :] = jnp.broadcast_to(mask[...], (MASK_ROWS, tokens))


def project(blocks, query_w, key_w, value_gate_w, mask, layer):
    samples, width, tokens = blocks[0].shape[-3:]
    small = jax.ShapeDtypeStruct((samples, width, tokens), jnp.bfloat16)
    joint = jax.ShapeDtypeStruct((2 * samples * width + MASK_ROWS, tokens), jnp.bfloat16)
    depth = query_w.shape[2]
    return local_call(
        lambda *refs: project_kernel(len(blocks), *refs),
        (small, small, joint),
        [whole(b.shape) for b in blocks]
        + [
            layer_block(query_w.shape, 0, layer),
            layer_block(key_w.shape, 0, layer),
            layer_block(value_gate_w.shape, 0, layer),
            whole(mask.shape),
        ],
        [*blocks, query_w, key_w, value_gate_w, mask],
        [pltpu.VMEM((depth, samples * tokens), jnp.bfloat16)],
        8 * depth * width * samples * tokens,
        "project",
    )


def transition_kernel(count, me_ref, *refs):
    blocks = refs[:count]
    up, down, own, parts, full, total = refs[count:]
    me = me_ref[0]
    fill(blocks, full, 2)
    samples, width, tokens = own.shape
    over_rows = (((0,), (0,)), ((), ()))
    swish = lax.dot_general(up[0, 0], full[...], over_rows, preferred_element_type=jnp.float32)
    linear = lax.dot_general(up[0, 1], full[...], over_rows, preferred_element_type=jnp.float32)
    hidden = (swish / (1.0 + jnp.exp(-swish)) * linear).astype(jnp.bfloat16)
    total[...] = lax.dot_general(down[0], hidden, over_rows, preferred_element_type=jnp.float32)
    for k in range(parts.shape[0] + 1):
        start = pl.multiple_of((me ^ k) * width, width)
        for s in range(samples):
            piece = total[pl.ds(start, width), s * tokens : (s + 1) * tokens]
            if k == 0:
                own[s] = piece
            else:
                parts[k - 1, s] = piece.astype(jnp.bfloat16)


def transition(blocks, me, up, down, layer, col_size):
    samples, width, tokens = blocks[0].shape[-3:]
    depth, hidden = up.shape[2:]
    return local_call(
        lambda *refs: transition_kernel(len(blocks), *refs),
        (
            jax.ShapeDtypeStruct((samples, width, tokens), jnp.float32),
            jax.ShapeDtypeStruct((col_size - 1, samples, width, tokens), jnp.bfloat16),
        ),
        [SCALAR]
        + [whole(b.shape) for b in blocks]
        + [layer_block(up.shape, 0, layer), layer_block(down.shape, 0, layer)],
        [me, *blocks, up, down],
        [
            pltpu.VMEM((depth, samples * tokens), jnp.bfloat16),
            pltpu.VMEM((depth, samples * tokens), jnp.float32),
        ],
        6 * depth * hidden * samples * tokens,
        "transition",
    )


def attention_kernel(me_ref, queries, gates, kv0, kv1, kv2, kv3, bias, *refs):
    out = refs[-1]
    pieces = (kv0, kv1, kv2, kv3)
    me = me_ref[0]
    samples, width, tokens = queries.shape
    heads = bias.shape[2]
    scale = 1.0 / math.sqrt(HEAD_DIM)
    lane = lax.broadcasted_iota(jnp.int32, (tokens, width), 1) // HEAD_DIM
    masks = jnp.concatenate(
        [kv[2 * samples * width : 2 * samples * width + 1].astype(jnp.float32) for kv in pieces], 1
    )
    mask_add = (masks - 1.0) * MASK_FILL
    for s in range(samples):
        query = jnp.transpose(queries[s].astype(jnp.float32))
        key = jnp.concatenate([kv[2 * s * width : (2 * s + 1) * width] for kv in pieces], 1)
        value = jnp.concatenate([kv[(2 * s + 1) * width : (2 * s + 2) * width] for kv in pieces], 1)
        kept = jnp.zeros((tokens, width), jnp.float32)
        for h in range(heads):
            mine = lane == h
            scores = jnp.dot(
                jnp.where(mine, query, 0.0).astype(jnp.bfloat16),
                key,
                preferred_element_type=jnp.float32,
            )
            added = jnp.concatenate(
                [
                    bias[:, me ^ k, h].astype(jnp.float32).reshape(tokens, tokens)
                    for k in range(len(pieces))
                ],
                1,
            )
            scores = scores * scale + added + mask_add
            exps = jnp.exp(scores - jnp.max(scores, axis=1, keepdims=True))
            total = jnp.sum(exps, axis=1, keepdims=True)
            product = lax.dot_general(
                exps.astype(jnp.bfloat16),
                value,
                (((1,), (1,)), ((), ())),
                preferred_element_type=jnp.float32,
            )
            kept = jnp.where(mine, product / total, kept)
        gate = jax.nn.sigmoid(gates[s].astype(jnp.float32))
        out[s] = (gate * jnp.transpose(kept)).astype(jnp.bfloat16)


def attention(me, queries, gates, pieces, bias, others):
    samples, width, tokens = queries.shape
    args = [me, queries, gates, *pieces, bias]
    return local_call(
        attention_kernel,
        jax.ShapeDtypeStruct(queries.shape, jnp.bfloat16),
        [SCALAR] + [whole(a.shape) for a in args[1:]] + [UNREAD] * len(others),
        args + others,
        [],
        4 * samples * bias.shape[2] * tokens * tokens * len(pieces) * width,
        "attention",
    )


def finish_kernel(attended, out_w, own, came0, came1, came2, gate_a, gate_t, state, full):
    stack_gathered(attended, full)
    samples, width, tokens = own.shape
    total = jnp.zeros((width, samples * tokens), jnp.float32)
    for k in range(attended.shape[0]):
        total = total + lax.dot_general(
            out_w[k, 0],
            full[k * width : (k + 1) * width],
            (((0,), (0,)), ((), ())),
            preferred_element_type=jnp.float32,
        )
    for s in range(samples):
        trans = own[s]
        for came in (came0, came1, came2):
            trans = trans + came[s].astype(jnp.float32)
        branch = total[:, s * tokens : (s + 1) * tokens]
        value = gate_a[0, s] * branch + gate_t[0, s] * trans
        state[s] = value.astype(state.dtype)


def finish(attended, out_w, own, came, mods, layer, gate_at, out_type):
    samples, width, tokens = own.shape
    parts = attended.shape[0]

    def mod_block(m):
        return pl.BlockSpec((1,) + own.shape, lambda i: (m, 0, 0, 0))

    return local_call(
        finish_kernel,
        jax.ShapeDtypeStruct(own.shape, out_type),
        [whole(attended.shape), layer_block(out_w.shape, 1, layer), whole(own.shape)]
        + [whole(c.shape) for c in came]
        + [mod_block(gate_at), mod_block(gate_at + 1)],
        [attended, out_w, own, *came, mods, mods],
        [pltpu.VMEM((parts * width, samples * tokens), jnp.bfloat16)],
        2 * parts * width * width * samples * tokens,
        "finish",
    )


def modulate_kernel(single, shift, mod_w, own, shared, normed):
    samples, width, tokens = own.shape[1:]
    layers, count = mod_w.shape[:2]
    for s in range(samples):
        condition = single[...].astype(jnp.float32) + shift[s : s + 1, :]
        normed[s * tokens : (s + 1) * tokens] = channel_norm(condition, 1).astype(jnp.bfloat16)
    kept = 0
    for layer in range(layers):
        for m in range(count):
            made = lax.dot_general(
                mod_w[layer, m],
                normed[...],
                (((1,), (1,)), ((), ())),
                preferred_element_type=jnp.float32,
            )
            if m not in (1, 3):
                made = jax.nn.sigmoid(made)
            for s in range(samples):
                piece = made[:, s * tokens : (s + 1) * tokens]
                if layer > 0 and m < 4:
                    shared[m, s] = piece.astype(jnp.bfloat16)
                else:
                    own[kept, s] = piece
            kept += layer == 0 or m >= 4


def modulate(single, shift, mod_w):
    layers, count, width, depth = mod_w.shape
    tokens, samples = single.shape[0], shift.shape[0]
    return local_call(
        modulate_kernel,
        (
            jax.ShapeDtypeStruct((count + 2, samples, width, tokens), jnp.float32),
            jax.ShapeDtypeStruct((4, samples, width, tokens), jnp.bfloat16),
        ),
        [whole(single.shape), whole(shift.shape), whole(mod_w.shape)],
        [single, shift, mod_w],
        [pltpu.VMEM((samples * tokens, depth), jnp.bfloat16)],
        2 * layers * count * width * depth * samples * tokens,
        "modulate",
    )


def triangle_kernel(came, *refs):
    out = refs[-1]
    rows, cols, _, keys = came.shape
    half = 8 * out.shape[0]

    def joined(at):
        return jnp.concatenate(
            [jnp.concatenate([came[r, c, at] for c in range(cols)], 1) for r in range(rows)], 0
        )

    sums = lax.dot_general(
        joined(slice(0, half)),
        joined(slice(half, half + keys)),
        (((1,), (1,)), ((), ())),
        preferred_element_type=jnp.float32,
    )
    groups = half // 8
    upper = lax.broadcasted_iota(jnp.int32, (groups, 8, keys), 1) < 4
    for r in range(rows):
        for c in range(0, cols, 2):
            one, two = (
                sums[r * half : (r + 1) * half, k * keys : (k + 1) * keys].reshape(groups, 8, keys)
                for k in (c, c + 1)
            )
            even = jnp.where(upper, one, pltpu.roll(two, 4, 1))
            odd = jnp.where(upper, pltpu.roll(one, 4, 1), two)
            out[:, 0, r, c // 2] = even.astype(jnp.bfloat16)
            out[:, 1, r, c // 2] = odd.astype(jnp.bfloat16)


def triangle_sums(came, others):
    rows, cols, height, keys = came.shape
    half = height - keys
    left = rows * half
    return local_call(
        triangle_kernel,
        jax.ShapeDtypeStruct((half // 8, 2, rows, cols // 2, 8, keys), jnp.bfloat16),
        [whole(came.shape)] + [UNREAD] * len(others),
        [came, *others],
        [],
        2 * left * rows * keys * cols * keys,
        "triangle_sums",
    )


def pair_project_kernel(me_ref, pair, tri, out, weight, normed, left, right):
    step = pl.program_id(0)
    channels, rows, keys = pair.shape
    height = rows * pl.num_programs(0)
    share = weight.shape[0] // 4
    halves = out.shape[0] // share
    part = out.shape[1] - keys
    group = 8 // halves

    @pl.when(step == 0)
    def _():
        mine = lax.broadcasted_iota(jnp.int32, (share, channels), 0) + me_ref[0] * share
        pick = mine == lax.broadcasted_iota(jnp.int32, (share, channels), 1)
        for p in range(4):
            weight[p * share : (p + 1) * share] = lax.dot_general(
                pick.astype(jnp.bfloat16),
                tri[p],
                (((1,), (1,)), ((), ())),
                preferred_element_type=jnp.float32,
            )

    value = pair[...].astype(jnp.float32)
    normed[...] = channel_norm(value, 0).reshape(channels * rows, keys)
    weights = weight[...].astype(jnp.bfloat16)
    for i in range(0, rows, 2):
        two = [normed[pl.ds(i + e, channels, stride=rows), :] for e in (0, 1)]
        made = jnp.dot(
            weights, jnp.concatenate(two, 1).astype(jnp.bfloat16), preferred_element_type=jnp.float32
        )
        made_left = jax.nn.sigmoid(made[:share]) * made[share : 2 * share]
        made_right = jax.nn.sigmoid(made[2 * share : 3 * share]) * made[3 * share :]
        for e in (0, 1):
            row, at = i + e, slice(e * keys, (e + 1) * keys)
            right[pl.ds(step * rows + row, share, stride=keys), :] = made_right[:, at]
            place = (row % 8) // group * part + row // 8 * group + row % group
            place = step * (rows // 8 * group) + place
            left[pl.ds(place, share, stride=keys), :] = made_left[:, at]

    @pl.when(step == pl.num_programs(0) - 1)
    def _():
        for c in range(share):
            whole_right = right[c * keys : (c + 1) * keys].astype(jnp.bfloat16)
            for h in range(halves):
                start = c * keys + h * part
                out[c * halves + h, :part] = left[start : start + part].astype(jnp.bfloat16)
                out[c * halves + h, part:] = whole_right


def pair_project(pair_in, tri_weight, me, group, samp_size):
    channels, height, keys = pair_in.shape
    share = channels // samp_size
    part = height // (group // share)
    rows = 16
    out = jax.ShapeDtypeStruct((group, part + height, keys), jnp.bfloat16)
    return pl.pallas_call(
        pair_project_kernel,
        grid=(height // rows,),
        out_shape=out,
        in_specs=[
            SCALAR,
            pl.BlockSpec((channels, rows, keys), lambda i: (0, i, 0)),
            whole(tri_weight.shape),
        ],
        out_specs=whole(out.shape),
        scratch_shapes=[
            pltpu.VMEM((4 * share, channels), jnp.float32),
            pltpu.VMEM((channels * rows, keys), jnp.float32),
            pltpu.VMEM((share * height, keys), jnp.float32),
            pltpu.VMEM((share * height, keys), jnp.float32),
        ],
        compiler_params=pltpu.CompilerParams(vmem_limit_bytes=CLAIM * MIB),
        cost_estimate=pl.CostEstimate(
            flops=8 * share * channels * height * keys,
            bytes_accessed=2 * pair_in.size,
            transcendentals=0,
        ),
        name="pair_project",
    )(me, pair_in, tri_weight)


def pair_update_kernel(came, own, gate_w, out_w, bias_w, *refs):
    back, bias0, bias1, rows_a, rows_b, rows_c = refs[-6:]
    channels, count, keys = came.shape
    over_rows = (((0,), (0,)), ((), ()))

    def by_channel(value, rows):
        rows[...] = value.astype(jnp.float32).reshape(channels * count, keys)
        return jnp.concatenate([rows[pl.ds(u, channels, stride=count), :] for u in range(count)], 1)

    def normed(value):
        return channel_norm(value, 0).astype(jnp.bfloat16)

    pair = by_channel(own[...], rows_a)
    sums = by_channel(came[...], rows_b)
    gate = lax.dot_general(gate_w[0], normed(pair), over_rows, preferred_element_type=jnp.float32)
    update = lax.dot_general(out_w[...], normed(sums), over_rows, preferred_element_type=jnp.float32)
    new = (pair + jax.nn.sigmoid(gate) * update).astype(jnp.bfloat16).astype(jnp.float32)
    bias = jnp.dot(bias_w[...], normed(new), preferred_element_type=jnp.float32)
    for u in range(count):
        at = slice(u * keys, (u + 1) * keys)
        rows_b[pl.ds(u, channels, stride=count), :] = new[:, at]
        rows_c[pl.ds(u, bias.shape[0], stride=count), :] = bias[:, at]
    back[...] = rows_b[...].reshape(channels, count, keys).astype(jnp.bfloat16)
    both = rows_c[...].reshape((2,) + bias0.shape[1:]).astype(jnp.bfloat16)
    for k in range(bias0.shape[0]):
        bias0[k] = both[0]
        bias1[k] = both[1]


def pair_update(came, own, tri_weight, out_weight, bias_w, samp_size, col_size, others):
    channels, count, keys = came.shape
    heads = bias_w.shape[0] // 2
    message = jax.ShapeDtypeStruct(
        (samp_size, col_size, heads // col_size, count, keys), jnp.bfloat16
    )
    return local_call(
        pair_update_kernel,
        (jax.ShapeDtypeStruct(came.shape, jnp.bfloat16), message, message),
        [
            whole(came.shape),
            whole(own.shape),
            layer_block(tri_weight.shape, 0, 4),
            whole(out_weight.shape),
            whole(bias_w.shape),
        ]
        + [UNREAD] * len(others),
        [came, own, tri_weight, out_weight, bias_w, *others],
        [
            pltpu.VMEM((channels * count, keys), jnp.float32),
            pltpu.VMEM((channels * count, keys), jnp.float32),
            pltpu.VMEM((bias_w.shape[0] * count, keys), jnp.float32),
        ],
        6 * channels * channels * count * keys,
        "pair_update",
    )


def pair_rows_kernel(came, out):
    for c in range(came.shape[1]):
        rows = [came[k, c].astype(jnp.float32) for k in range(came.shape[0])]
        out[c] = jnp.concatenate(rows, 0).astype(jnp.bfloat16)


def pair_rows_joined(came):
    parts, share, count, keys = came.shape
    return local_call(
        pair_rows_kernel,
        jax.ShapeDtypeStruct((share, parts * count, keys), jnp.bfloat16),
        [whole(came.shape)],
        [came],
        [],
        0,
        "pair_rows",
    )


def body(
    pair_in,
    token_act,
    single,
    noise_sigma,
    token_mask,
    tri_weight,
    out_weight,
    bias_weight,
    time_weight,
    mod_weight,
    query_weight,
    key_weight,
    value_gate_weight,
    attn_out_weight,
    up_weight,
    down_weight,
):
    channels, pair_rows, pair_cols = pair_in.shape
    samp_size, row_size, col_size = (lax.axis_size(name) for name in ("samp", "row", "col"))
    group = row_size * col_size
    share = channels // samp_size
    halves = group // share
    half_rows = pair_rows // halves
    cell_rows = half_rows // samp_size
    own_rows = halves * cell_rows
    samp_at = jnp.reshape(lax.axis_index("samp"), (1,))
    row_at = jnp.reshape(lax.axis_index("row"), (1,))
    col_at = jnp.reshape(lax.axis_index("col"), (1,))
    blocks, _, head_count = bias_weight.shape

    state = jnp.swapaxes(token_act, 1, 2).astype(jnp.float32)
    samples, width, row_count = state.shape
    query_w = jnp.swapaxes(query_weight, 1, 2)
    key_w = jnp.swapaxes(key_weight, 1, 2)
    value_gate_w = jnp.swapaxes(value_gate_weight, 2, 3)
    mod_w = jnp.swapaxes(mod_weight, 2, 3)
    out_w = attn_out_weight.reshape(blocks, width, col_size, width)
    out_w = lax.all_to_all(jnp.transpose(out_w, (2, 0, 1, 3)), "col", 0, 0, tiled=True)
    half_count = TEMB // 2
    frequency = jnp.exp(jnp.arange(half_count, dtype=jnp.float32) * (math.log(100.0) / half_count))
    angles = (jnp.log(noise_sigma) * 0.25)[:, None] * frequency[None, :]
    time_embed = jnp.concatenate([jnp.cos(angles), jnp.sin(angles)], 1).astype(jnp.bfloat16)
    time_shift = jnp.dot(time_embed, time_weight, preferred_element_type=jnp.float32)
    mods, shared = modulate(single, time_shift, mod_w)
    shared = lax.all_gather(shared, "col", axis=0)
    mask_row = token_mask.astype(jnp.bfloat16)[None]

    sums = jnp.stack([jnp.sum(state, 1), jnp.sum(state * state, 1)])
    sums = sum(swap_all(sums, "col"))
    mean_value = sums[0] / DA
    scale = lax.rsqrt(sums[1] / DA - mean_value * mean_value + EPS)
    normed = (state - mean_value[:, None, :]) * scale[:, None, :]
    attn_local = (mods[0] * normed + mods[1]).astype(jnp.bfloat16)
    trans_local = (mods[2] * normed + mods[3]).astype(jnp.bfloat16)
    attn_full = lax.all_gather(attn_local, "col", axis=0)
    queries, gates, both = project([attn_full], query_w, key_w, value_gate_w, mask_row, 0)
    pieces = swap_all(both, "row")
    trans_full = lax.all_gather(trans_local, "col", axis=0)
    own, parts = transition([trans_full], col_at, up_weight, down_weight, 0, col_size)
    trans_came = [swap(parts[k - 1], "col", k) for k in range(1, col_size)]

    to_send = pair_project(pair_in, tri_weight, samp_at, group, samp_size)
    came = lax.all_to_all(to_send, ("row", "col"), 0, 0, tiled=True)
    came = came.reshape(row_size, col_size, half_rows + pair_rows, pair_cols)
    triangle = triangle_sums(came, [attn_full, out_w])
    triangle = triangle.reshape(samp_size * group, cell_rows, pair_cols)
    triangle = lax.all_to_all(triangle, ("samp", "row", "col"), 0, 0, tiled=True)
    triangle = triangle.reshape(channels, own_rows, pair_cols)

    own_pair = lax.dynamic_slice_in_dim(pair_in, samp_at[0] * own_rows, own_rows, 1)
    bias_w = jnp.swapaxes(bias_weight, 1, 2).reshape(blocks * head_count, channels)
    pair_out, *biases = pair_update(
        triangle, own_pair, tri_weight, out_weight, bias_w, samp_size, col_size, [both, own]
    )

    def spread_bias(part):
        shape = part.shape
        part = part.reshape((samp_size * col_size,) + shape[2:])
        return lax.all_to_all(part, ("samp", "col"), 0, 0, tiled=True).reshape(shape)

    biases = [spread_bias(part) for part in biases]

    for layer in range(blocks):
        if layer > 0:
            queries, gates, both = project(
                [state, shared], query_w, key_w, value_gate_w, mask_row, layer
            )
            own, parts = transition([state, shared], col_at, up_weight, down_weight, layer, col_size)
            pieces = swap_all(both, "row")
            trans_came = [swap(parts[k - 1], "col", k) for k in range(1, col_size)]
            pair_back = lax.all_to_all(
                after(pair_out, [both]).reshape(samp_size, share, own_rows, pair_cols),
                "samp",
                0,
                0,
                tiled=True,
            )
            pair_back = pair_rows_joined(pair_back)
        attended = attention(
            row_at, queries, gates, pieces, biases[layer], [pair_back] if layer > 0 else []
        )
        attended = lax.all_gather(attended, "col", axis=0)
        state = finish(
            attended, out_w, own, trans_came, mods, layer, 4 + 2 * layer, jnp.bfloat16
        )
        if layer < blocks - 1:
            state = lax.all_gather(state, "col", axis=0)
    return (pair_back, jnp.swapaxes(state, 1, 2))


def solution(mesh):
    placed = (
        P(None, "row", "col"),
        P("samp", "row", "col"),
        P("row", None),
        P("samp"),
        P("row"),
        P(),
        P(),
        P(),
        P(),
        P(None, None, None, "col"),
        P(None, None, "col"),
        P(None, None, "col"),
        P(None, None, None, "col"),
        P(None, "col", None),
        P(None, None, None, "col"),
        P(None, "col", None),
    )
    return jax.shard_map(
        body,
        mesh=mesh,
        in_specs=placed,
        out_specs=(P("samp", "row", "col"), P("samp", "row", "col")),
        check_vma=False,
    )
```

profile of v0, /device:TPU:1, one launch (start us, length us, event | category | flops | bytes accessed | tf_op | source)
XLA Modules:
  0.0 240.5 jit_solution(3609069543424423684)
XLA Ops:
  7.2 2.3 reshape.72
  9.5 1.0 copy.21
  10.5 6.7 %all-to-all-start.1 = ((bf16[4,2,192,192]{3,2,1,0:T(8,128)(2,1)}), bf16[4,2,192,192]{3,2,1,0:T(8,128)(2,1)S(1)}, u32[]{:S(2)}, u32[]{:S(2)}) async-start(bf16[4,2,192,192]{3,2,1,0:T(8,128)(2,1)} %bitcast.84), calls=%async_computation.1 | async-start | bytes 1572864 | tf_op jit(solution)/shard_map/all_to_all | solution.py:574
  17.2 0.1 fusion.5
  17.3 0.7 fusion.12.shift
  18.1 4.6 %modulate.1 = (f32[8,3,192,128]{3,2,1,0:T(8,128)}, bf16[4,3,192,128]{3,2,1,0:T(8,128)(2,1)}) custom-call(bf16[128,384]{1,0:T(8,128)(2,1)} %single.1, f32[3,384]{1,0:T(4,128)} %fusion.12.shift, bf16[2,6,192,384]{3,2,1,0:T(8,128)(2,1)} %bitcast.112), custom_call_target="tpu_custom_call" | custom-call | flops 679477248 | bytes 1872384 | tf_op jit(solution)/shard_map/modulate/pallas_call | solution.py:40
  22.8 9.8 %pair_project.1 = bf16[16,192,128]{2,1,0:T(8,128)(2,1)} custom-call(s32[1]{0:T(128)} %bitcast.me_ref, bf16[128,128,128]{2,1,0:T(8,128)(2,1)} %pair.1, bf16[5,128,128]{2,1,0:T(8,128)(2,1)} %gate_w.1), custom_call_target="tpu_custom_call" | custom-call | flops 134217728 | bytes 4194304 | tf_op jit(solution)/shard_map/pair_project/pallas_call | solution.py:434
  32.6 4.2 %all-to-all-start = ((bf16[16,192,128]{2,1,0:T(8,128)(2,1)}), bf16[16,192,128]{2,1,0:T(8,128)(2,1)}, u32[]{:S(2)}, u32[]{:S(2)}) async-start(bf16[16,192,128]{2,1,0:T(8,128)(2,1)} %pair_project.1), calls=%async_computation | async-start | bytes 1572864 | tf_op jit(solution)/shard_map/all_to_all | solution.py:599
  36.8 0.1 bitcast_reduce_fusion
  36.9 0.3 collective-permute-start
  37.2 1.6 collective-permute-start.1
  38.7 0.4 collective-permute-start.2
  39.1 1.7 constant_dynamic-slice_fusion.own
  40.8 15.4 %collective-permute-done.1 = f32[2,3,128]{2,1,0:T(4,128)S(1)} collective-permute-done((f32[2,3,128]{2,1,0:T(4,128)S(1)}, f32[2,3,128]{2,1,0:T(4,128)S(1)}, u32[]{:S(2)}, u32[]{:S(2)}) %collective-permute-start.1) | collective-permute-done | bytes 3104 | tf_op jit(solution)/shard_map/ppermute | solution.py:31
  56.2 0.8 collective-permute-done.2
  57.0 0.8 fusion
  57.8 11.6 %all-gather = bf16[12,192,128]{2,1,0:T(8,128)(2,1)} all-gather(bf16[3,192,128]{2,1,0:T(8,128)(2,1)S(1)} %get-tuple-element.35), channel_id=2, replica_groups=mesh['samp'=16,'row'=4,'col'=4] {'col'}, dimensions={0}, use_global_device_ids=true | all-gather | bytes 737280 | tf_op jit(solution)/shard_map/all_gather | solution.py:591
  69.4 2.2 triangle_sums.1
  71.6 13.9 %all-to-all-start.2 = ((bf16[256,4,128]{2,1,0:T(4,128)(2,1)}), bf16[256,4,128]{2,1,0:T(4,128)(2,1)S(1)}, u32[]{:S(2)}, u32[]{:S(2)}) async-start(bf16[256,4,128]{2,1,0:T(4,128)(2,1)} %bitcast.102), calls=%async_computation.2 | async-start | bytes 524288 | tf_op jit(solution)/shard_map/all_to_all | solution.py:603
  85.5 0.6 convert_bitcast_fusion.refs_4_.refs_5_
  86.1 3.0 %project.2 = (bf16[3,192,128]{2,1,0:T(8,128)(2,1)}, bf16[3,192,128]{2,1,0:T(8,128)(2,1)}, bf16[1168,128]{1,0:T(8,128)(2,1)}) custom-call(bf16[4,3,192,128]{3,2,1,0:T(8,128)(2,1)} %bitcast.90, bf16[2,192,768]{2,1,0:T(8,128)(2,1)} %bitcast.96, bf16[2,192,768]{2,1,0:T(8,128)(2,1)} %bitcast.98, bf16[2,2,192,768]{3,2,1,0:T(8,128)(2,1)} %bitcast.91, ...), custom_call_target="tpu_custom_call" | custom-call | flops 452984832 | bytes 2949376 | tf_op jit(solution)/shard_map/project/pallas_call | solution.py:40
  89.1 9.1 %all-gather.1 = bf16[12,192,128]{2,1,0:T(8,128)(2,1)} all-gather(bf16[3,192,128]{2,1,0:T(8,128)(2,1)S(1)} %copy-done.7), channel_id=3, replica_groups=mesh['samp'=16,'row'=4,'col'=4] {'col'}, dimensions={0}, use_global_device_ids=true | all-gather | bytes 737280 | tf_op jit(solution)/shard_map/all_gather | solution.py:594
  98.2 3.8 %transition.2 = (f32[3,192,128]{2,1,0:T(8,128)}, bf16[3,3,192,128]{3,2,1,0:T(8,128)(2,1)}) custom-call(s32[1]{0:T(128)} %bitcast.20.refs_0_, bf16[4,3,192,128]{3,2,1,0:T(8,128)(2,1)} %bitcast.93, bf16[2,2,768,384]{3,2,1,0:T(8,128)(2,1)} %refs_3_.3, bf16[2,384,768]{2,1,0:T(8,128)(2,1)} %refs_4_.1), custom_call_target="tpu_custom_call" | custom-call | flops 679477248 | bytes 4128772 | tf_op jit(solution)/shard_map/transition/pallas_call | solution.py:40
  102.0 0.7 copy-done.5
  102.7 3.0 %pair_update.1 = (bf16[128,8,128]{2,1,0:T(8,128)(2,1)}, bf16[16,4,4,8,128]{4,3,2,1,0:T(8,128)(2,1)}, bf16[16,4,4,8,128]{4,3,2,1,0:T(8,128)(2,1)}) custom-call(bf16[128,8,128]{2,1,0:T(8,128)(2,1)} %bitcast.101, bf16[128,8,128]{2,1,0:T(8,128)(2,1)} %constant_dynamic-slice_fusion.own, bf16[5,128,128]{2,1,0:T(8,128)(2,1)} %gate_w.1, bf16[128,128]{1,0:T(8,128)(2,1)} %out_w.1, ...), custom_call_target="tpu_custom_call" | custom-call | flops 100663296 | bytes 1323008 | tf_op jit(solution)/shard_map/pair_update/pallas_call | solution.py:40
  105.8 9.9 %all-to-all-start.3 = ((bf16[64,4,8,128]{3,2,1,0:T(8,128)(2,1)}), bf16[64,4,8,128]{3,2,1,0:T(8,128)(2,1)S(1)}, u32[]{:S(2)}, u32[]{:S(2)}) async-start(bf16[64,4,8,128]{3,2,1,0:T(8,128)(2,1)} %bitcast.105), calls=%async_computation.3 | async-start | bytes 1048576 | tf_op jit(solution)/shard_map/all_to_all | solution.py:615
  115.7 1.3 collective-permute-start.3
  117.0 2.5 %collective-permute-start.4 = (bf16[1168,128]{1,0:T(8,128)(2,1)S(1)}, bf16[1168,128]{1,0:T(8,128)(2,1)S(1)}, u32[]{:S(2)}, u32[]{:S(2)}) collective-permute-start(bf16[1168,128]{1,0:T(8,128)(2,1)S(1)} %copy-done.10), channel_id=1, source_target_pairs={{0,8},{4,12},{8,0},{12,4},{1,9},{5,13},{9,1},{13,5},{2,10},{6,14},... | collective-permute-start | bytes 897032 | tf_op jit(solution)/shard_map/ppermute | solution.py:31
  119.6 0.1 collective-permute-start.5
  119.7 1.4 collective-permute-start.6
  121.1 1.3 collective-permute-start.7
  122.4 1.6 collective-permute-done.3.kv1
  124.0 3.4 %collective-permute-start.8 = (bf16[3,192,128]{2,1,0:T(8,128)(2,1)S(1)}, bf16[3,192,128]{2,1,0:T(8,128)(2,1)S(1)}, u32[]{:S(2)}, u32[]{:S(2)}) collective-permute-start(bf16[3,192,128]{2,1,0:T(8,128)(2,1)S(1)} %get-tuple-element.39), channel_id=1, source_target_pairs={{0,3},{1,2},{2,1},{3,0},{4,7},{5,6},{6,5},{7,4},{8,11},{9,10},{10,... | collective-permute-start | bytes 442376 | tf_op jit(solution)/shard_map/ppermute | solution.py:31
  127.4 5.4 %collective-permute-done.4.kv2 = bf16[1168,128]{1,0:T(8,128)(2,1)S(1)} collective-permute-done((bf16[1168,128]{1,0:T(8,128)(2,1)S(1)}, bf16[1168,128]{1,0:T(8,128)(2,1)S(1)}, u32[]{:S(2)}, u32[]{:S(2)}) %collective-permute-start.4) | collective-permute-done | bytes 299040 | tf_op jit(solution)/shard_map/ppermute | solution.py:31
  132.8 2.0 collective-permute-done.5.kv3
  134.8 0.7 copy-done.22
  135.5 0.2 copy-done.8
  135.7 4.8 %attention.2 = bf16[3,192,128]{2,1,0:T(8,128)(2,1)} custom-call(s32[1]{0:T(128)} %bitcast.24.me_ref, bf16[3,192,128]{2,1,0:T(8,128)(2,1)} %get-tuple-element.21.queries, bf16[3,192,128]{2,1,0:T(8,128)(2,1)} %get-tuple-element.22.gates, bf16[1168,128]{1,0:T(8,128)(2,1)} %get-tuple-element.18.refs_0_.kv0, bf16[1168,128]{1,0:T(8,128)(2,1)} %copy-done.20, ...), custom_call_target="tpu_custom_call" | custom-call | flops 603979776 | bytes 2015236 | tf_op jit(solution)/shard_map/attention/pallas_call | solution.py:40
  140.4 10.9 %all-gather.2 = bf16[12,192,128]{2,1,0:T(8,128)(2,1)} all-gather(bf16[3,192,128]{2,1,0:T(8,128)(2,1)} %attention.2), channel_id=4, replica_groups=mesh['samp'=16,'row'=4,'col'=4] {'col'}, dimensions={0}, use_global_device_ids=true | all-gather | bytes 737280 | tf_op jit(solution)/shard_map/all_gather | solution.py:638
  151.4 0.6 copy-done.16
  152.1 2.7 %finish.2 = bf16[3,192,128]{2,1,0:T(8,128)(2,1)} custom-call(bf16[4,3,192,128]{3,2,1,0:T(8,128)(2,1)} %bitcast.95, bf16[4,2,192,192]{3,2,1,0:T(8,128)(2,1)} %copy-done.2, f32[3,192,128]{2,1,0:T(8,128)} %get-tuple-element.19.refs_1_.own, bf16[3,192,128]{2,1,0:T(8,128)(2,1)} %copy-done.16, bf16[3,192,128]{2,1,0:T(8,128)(2,1)} %copy-done.17, ...), custom_call_target="tpu_custom_call" | custom-call | flops 113246208 | bytes 6635520 | tf_op jit(solution)/shard_map/finish/pallas_call | solution.py:40
  154.8 9.1 %all-gather.3 = bf16[12,192,128]{2,1,0:T(8,128)(2,1)} all-gather(bf16[3,192,128]{2,1,0:T(8,128)(2,1)} %finish.2), channel_id=5, replica_groups=mesh['samp'=16,'row'=4,'col'=4] {'col'}, dimensions={0}, use_global_device_ids=true | all-gather | bytes 737280 | tf_op jit(solution)/shard_map/all_gather | solution.py:643
  163.8 4.1 %project.3 = (bf16[3,192,128]{2,1,0:T(8,128)(2,1)}, bf16[3,192,128]{2,1,0:T(8,128)(2,1)}, bf16[1168,128]{1,0:T(8,128)(2,1)}) custom-call(bf16[4,3,192,128]{3,2,1,0:T(8,128)(2,1)} %bitcast.87, bf16[4,4,3,192,128]{4,3,2,1,0:T(8,128)(2,1)} %bitcast.85, bf16[2,192,768]{2,1,0:T(8,128)(2,1)} %bitcast.97, bf16[2,192,768]{2,1,0:T(8,128)(2,1)} %bitcast.99, ...), custom_call_target="tpu_custom_call" | custom-call | flops 452984832 | bytes 5308672 | tf_op jit(solution)/shard_map/project/pallas_call | solution.py:40
  167.9 1.7 after.1
  169.7 20.1 %all_to_all.30.came = bf16[16,8,8,128]{3,2,1,0:T(8,128)(2,1)} all-to-all(bf16[16,8,8,128]{3,2,1,0:T(8,128)(2,1)} %bitcast.103), channel_id=1, replica_groups=mesh['samp'=16,'row'=4,'col'=4] {'samp'}, dimensions={0} | all-to-all | bytes 524288 | tf_op jit(solution)/shard_map/all_to_all | solution.py:627
  189.8 7.4 %all-to-all-start.5 = ((bf16[64,4,8,128]{3,2,1,0:T(8,128)(2,1)}), bf16[64,4,8,128]{3,2,1,0:T(8,128)(2,1)S(1)}, u32[]{:S(2)}, u32[]{:S(2)}) async-start(bf16[64,4,8,128]{3,2,1,0:T(8,128)(2,1)} %bitcast.34), calls=%async_computation.5 | async-start | bytes 1048576 | tf_op jit(solution)/shard_map/all_to_all | solution.py:615
  197.2 0.1 collective-permute-start.10
  197.3 1.1 collective-permute-start.11
  198.3 1.6 collective-permute-start.9
  199.9 5.0 %transition.3 = (f32[3,192,128]{2,1,0:T(8,128)}, bf16[3,3,192,128]{3,2,1,0:T(8,128)(2,1)}) custom-call(s32[1]{0:T(128)} %bitcast.20.refs_0_, bf16[4,3,192,128]{3,2,1,0:T(8,128)(2,1)} %bitcast.88, bf16[4,4,3,192,128]{4,3,2,1,0:T(8,128)(2,1)} %bitcast.86, bf16[2,2,768,384]{3,2,1,0:T(8,128)(2,1)} %refs_3_.3, bf16[2,384,768]{2,1,0:T(8,128)(2,1)} %refs_4_.1), custom_call_target="tpu_custom_call" | custom-call | flops 679477248 | bytes 6488068 | tf_op jit(solution)/shard_map/transition/pallas_call | solution.py:40
  204.8 1.1 slice_bitcast_fusion
  205.9 1.4 collective-permute-start.12
  207.3 1.3 collective-permute-start.13
  208.6 1.7 pair_rows.1.refs_0_
  210.3 0.4 collective-permute-start.14
  210.8 3.4 %all-to-all-done.5 = bf16[64,4,8,128]{3,2,1,0:T(8,128)(2,1)S(1)} async-done(((bf16[64,4,8,128]{3,2,1,0:T(8,128)(2,1)}), bf16[64,4,8,128]{3,2,1,0:T(8,128)(2,1)S(1)}, u32[]{:S(2)}, u32[]{:S(2)}) %all-to-all-start.5) | async-done | bytes 524320 | tf_op jit(solution)/shard_map/all_to_all | solution.py:615
  214.2 0.8 copy-done.3
  214.9 0.1 copy-done.12
  215.1 0.1 copy-done.13
  215.1 4.7 %attention.3 = bf16[3,192,128]{2,1,0:T(8,128)(2,1)} custom-call(s32[1]{0:T(128)} %bitcast.24.me_ref, bf16[3,192,128]{2,1,0:T(8,128)(2,1)} %get-tuple-element.27.queries, bf16[3,192,128]{2,1,0:T(8,128)(2,1)} %get-tuple-element.28.gates, bf16[1168,128]{1,0:T(8,128)(2,1)} %get-tuple-element.26.refs_1_.kv0, bf16[1168,128]{1,0:T(8,128)(2,1)} %copy-done.13, ...), custom_call_target="tpu_custom_call" | custom-call | flops 603979776 | bytes 2277380 | tf_op jit(solution)/shard_map/attention/pallas_call | solution.py:40
  219.9 10.3 %all-gather.5 = bf16[12,192,128]{2,1,0:T(8,128)(2,1)} all-gather(bf16[3,192,128]{2,1,0:T(8,128)(2,1)} %attention.3), channel_id=7, replica_groups=mesh['samp'=16,'row'=4,'col'=4] {'col'}, dimensions={0}, use_global_device_ids=true | all-gather | bytes 737280 | tf_op jit(solution)/shard_map/all_gather | solution.py:638
  230.2 0.6 copy-done.14
  230.9 0.1 copy-done.15
  231.0 2.6 %finish.3 = bf16[3,192,128]{2,1,0:T(8,128)(2,1)} custom-call(bf16[4,3,192,128]{3,2,1,0:T(8,128)(2,1)} %bitcast.94, bf16[4,2,192,192]{3,2,1,0:T(8,128)(2,1)} %copy-done.2, f32[3,192,128]{2,1,0:T(8,128)} %get-tuple-element.30.own, bf16[3,192,128]{2,1,0:T(8,128)(2,1)} %copy-done.14, bf16[3,192,128]{2,1,0:T(8,128)(2,1)} %copy-done.15, ...), custom_call_target="tpu_custom_call" | custom-call | flops 113246208 | bytes 6635520 | tf_op jit(solution)/shard_map/finish/pallas_call | solution.py:40
  (65 shorter events, 0.3 us)
Async XLA Ops:
  7.2 10.2 %copy-start = (bf16[256,384]{1,0:T(8,128)(2,1)S(1)}, bf16[256,384]{1,0:T(8,128)(2,1)}, u32[]{:S(2)}) copy-start(bf16[256,384]{1,0:T(8,128)(2,1)} %param.24) | copy-start | bytes 589828
  7.2 10.0 %copy-start.23 = (f32[3]{0:T(128)S(1)}, f32[3]{0:T(128)}, u32[]{:S(2)}) copy-start(f32[3]{0:T(128)} %param.19) | copy-start | bytes 40
  10.5 22.1 %all-to-all-start.1 = ((bf16[4,2,192,192]{3,2,1,0:T(8,128)(2,1)}), bf16[4,2,192,192]{3,2,1,0:T(8,128)(2,1)S(1)}, u32[]{:S(2)}, u32[]{:S(2)}) async-start(bf16[4,2,192,192]{3,2,1,0:T(8,128)(2,1)} %bitcast.84), calls=%async_computation.1 | async-start | bytes 1572864 | tf_op jit(solution)/shard_map/all_to_all | solution.py:574
  17.2 146.6 %all-gather.8.cloned.1.call-start = ((), (), s32[]{:S(2)}) async-start(), calls=%async_computation.6 | async-start | bytes 2949120 | tf_op jit(solution)/shard_map/all_gather | solution.py:581
  22.8 14.1 %copy-start.6 = (bf16[3,128,192]{1,2,0:T(8,128)(2,1)S(1)}, bf16[3,128,192]{1,2,0:T(8,128)(2,1)}, u32[]{:S(2)}) copy-start(bf16[3,128,192]{1,2,0:T(8,128)(2,1)} %param.17) | copy-start | bytes 442372
  22.8 34.2 %copy-start.1 = (f32[8,3,192,128]{3,2,1,0:T(8,128)S(1)}, f32[8,3,192,128]{3,2,1,0:T(8,128)}, u32[]{:S(2)}) copy-start(f32[8,3,192,128]{3,2,1,0:T(8,128)} %get-tuple-element.17.gate_a.gate_t) | copy-start | bytes 7077892
  32.6 36.8 %copy-start.2 = (bf16[4,2,192,192]{3,2,1,0:T(8,128)(2,1)}, bf16[4,2,192,192]{3,2,1,0:T(8,128)(2,1)S(1)}, u32[]{:S(2)}) copy-start(bf16[4,2,192,192]{3,2,1,0:T(8,128)(2,1)S(1)} %all-to-all-done.1.refs_1_.out_w) | copy-start | bytes 1769476
  32.6 36.8 %all-to-all-start = ((bf16[16,192,128]{2,1,0:T(8,128)(2,1)}), bf16[16,192,128]{2,1,0:T(8,128)(2,1)}, u32[]{:S(2)}, u32[]{:S(2)}) async-start(bf16[16,192,128]{2,1,0:T(8,128)(2,1)} %pair_project.1), calls=%async_computation | async-start | bytes 1572864 | tf_op jit(solution)/shard_map/all_to_all | solution.py:599
  36.9 3.9 %collective-permute-start = (f32[2,3,128]{2,1,0:T(4,128)S(1)}, f32[2,3,128]{2,1,0:T(4,128)S(1)}, u32[]{:S(2)}, u32[]{:S(2)}) collective-permute-start(f32[2,3,128]{2,1,0:T(4,128)S(1)} %pad_maximum_fusion), channel_id=1, source_target_pairs={{0,1},{1,0},{2,3},{3,2},{4,5},{5,4},{6,7},{7,6},{8,9},{9,8},{10,11... | collective-permute-start | bytes 9224 | tf_op jit(solution)/shard_map/ppermute | solution.py:31
  37.2 19.0 %collective-permute-start.1 = (f32[2,3,128]{2,1,0:T(4,128)S(1)}, f32[2,3,128]{2,1,0:T(4,128)S(1)}, u32[]{:S(2)}, u32[]{:S(2)}) collective-permute-start(f32[2,3,128]{2,1,0:T(4,128)S(1)} %pad_maximum_fusion), channel_id=1, source_target_pairs={{0,2},{1,3},{2,0},{3,1},{4,6},{5,7},{6,4},{7,5},{8,10},{9,11},{10,... | collective-permute-start | bytes 9224 | tf_op jit(solution)/shard_map/ppermute | solution.py:31
  38.7 18.2 %collective-permute-start.2 = (f32[2,3,128]{2,1,0:T(4,128)S(1)}, f32[2,3,128]{2,1,0:T(4,128)S(1)}, u32[]{:S(2)}, u32[]{:S(2)}) collective-permute-start(f32[2,3,128]{2,1,0:T(4,128)S(1)} %pad_maximum_fusion), channel_id=1, source_target_pairs={{0,3},{1,2},{2,1},{3,0},{4,7},{5,6},{6,5},{7,4},{8,11},{9,10},{10,... | collective-permute-start | bytes 9224 | tf_op jit(solution)/shard_map/ppermute | solution.py:31
  57.0 28.5 %copy-start.24 = (s32[128]{0:T(128)S(1)}, s32[128]{0:T(128)}, u32[]{:S(2)}) copy-start(s32[128]{0:T(128)} %param.20) | copy-start | bytes 1540
  69.4 19.7 %copy-start.7 = (bf16[3,192,128]{2,1,0:T(8,128)(2,1)S(1)}, bf16[3,192,128]{2,1,0:T(8,128)(2,1)}, u32[]{:S(2)}) copy-start(bf16[3,192,128]{2,1,0:T(8,128)(2,1)} %get-tuple-element.34) | copy-start | bytes 442372
  71.6 30.4 %all-to-all-start.2 = ((bf16[256,4,128]{2,1,0:T(4,128)(2,1)}), bf16[256,4,128]{2,1,0:T(4,128)(2,1)S(1)}, u32[]{:S(2)}, u32[]{:S(2)}) async-start(bf16[256,4,128]{2,1,0:T(4,128)(2,1)} %bitcast.102), calls=%async_computation.2 | async-start | bytes 524288 | tf_op jit(solution)/shard_map/all_to_all | solution.py:603
  98.2 17.5 %copy-start.10 = (bf16[1168,128]{1,0:T(8,128)(2,1)S(1)}, bf16[1168,128]{1,0:T(8,128)(2,1)}, u32[]{:S(2)}) copy-start(bf16[1168,128]{1,0:T(8,128)(2,1)} %get-tuple-element.18.refs_0_.kv0) | copy-start | bytes 897028
  102.0 17.6 %copy-start.9 = (bf16[3,3,192,128]{3,2,1,0:T(8,128)(2,1)S(1)}, bf16[3,3,192,128]{3,2,1,0:T(8,128)(2,1)}, u32[]{:S(2)}) copy-start(bf16[3,3,192,128]{3,2,1,0:T(8,128)(2,1)} %get-tuple-element.24) | copy-start | bytes 1327108
  102.0 0.7 copy-start.5
  105.8 29.0 %all-to-all-start.3 = ((bf16[64,4,8,128]{3,2,1,0:T(8,128)(2,1)}), bf16[64,4,8,128]{3,2,1,0:T(8,128)(2,1)S(1)}, u32[]{:S(2)}, u32[]{:S(2)}) async-start(bf16[64,4,8,128]{3,2,1,0:T(8,128)(2,1)} %bitcast.105), calls=%async_computation.3 | async-start | bytes 1048576 | tf_op jit(solution)/shard_map/all_to_all | solution.py:615
  115.7 8.3 %collective-permute-start.3 = (bf16[1168,128]{1,0:T(8,128)(2,1)S(1)}, bf16[1168,128]{1,0:T(8,128)(2,1)S(1)}, u32[]{:S(2)}, u32[]{:S(2)}) collective-permute-start(bf16[1168,128]{1,0:T(8,128)(2,1)S(1)} %copy-done.10), channel_id=1, source_target_pairs={{0,4},{4,0},{8,12},{12,8},{1,5},{5,1},{9,13},{13,9},{2,6},{6,2},{1... | collective-permute-start | bytes 897032 | tf_op jit(solution)/shard_map/ppermute | solution.py:31
  117.0 15.7 %collective-permute-start.4 = (bf16[1168,128]{1,0:T(8,128)(2,1)S(1)}, bf16[1168,128]{1,0:T(8,128)(2,1)S(1)}, u32[]{:S(2)}, u32[]{:S(2)}) collective-permute-start(bf16[1168,128]{1,0:T(8,128)(2,1)S(1)} %copy-done.10), channel_id=1, source_target_pairs={{0,8},{4,12},{8,0},{12,4},{1,9},{5,13},{9,1},{13,5},{2,10},{6,14},... | collective-permute-start | bytes 897032 | tf_op jit(solution)/shard_map/ppermute | solution.py:31
  119.6 15.2 %collective-permute-start.5 = (bf16[1168,128]{1,0:T(8,128)(2,1)S(1)}, bf16[1168,128]{1,0:T(8,128)(2,1)S(1)}, u32[]{:S(2)}, u32[]{:S(2)}) collective-permute-start(bf16[1168,128]{1,0:T(8,128)(2,1)S(1)} %copy-done.10), channel_id=1, source_target_pairs={{0,12},{4,8},{8,4},{12,0},{1,13},{5,9},{9,5},{13,1},{2,14},{6,10},... | collective-permute-start | bytes 897032 | tf_op jit(solution)/shard_map/ppermute | solution.py:31
  119.7 31.7 %collective-permute-start.6 = (bf16[3,192,128]{2,1,0:T(8,128)(2,1)S(1)}, bf16[3,192,128]{2,1,0:T(8,128)(2,1)S(1)}, u32[]{:S(2)}, u32[]{:S(2)}) collective-permute-start(bf16[3,192,128]{2,1,0:T(8,128)(2,1)S(1)} %get-tuple-element.41), channel_id=1, source_target_pairs={{0,1},{1,0},{2,3},{3,2},{4,5},{5,4},{6,7},{7,6},{8,9},{9,8},{10,11... | collective-permute-start | bytes 442376 | tf_op jit(solution)/shard_map/ppermute | solution.py:31
  121.1 30.3 %collective-permute-start.7 = (bf16[3,192,128]{2,1,0:T(8,128)(2,1)S(1)}, bf16[3,192,128]{2,1,0:T(8,128)(2,1)S(1)}, u32[]{:S(2)}, u32[]{:S(2)}) collective-permute-start(bf16[3,192,128]{2,1,0:T(8,128)(2,1)S(1)} %get-tuple-element.40), channel_id=1, source_target_pairs={{0,2},{1,3},{2,0},{3,1},{4,6},{5,7},{6,4},{7,5},{8,10},{9,11},{10,... | collective-permute-start | bytes 442376 | tf_op jit(solution)/shard_map/ppermute | solution.py:31
  124.0 10.8 %copy-start.20 = (bf16[1168,128]{1,0:T(8,128)(2,1)}, bf16[1168,128]{1,0:T(8,128)(2,1)S(1)}, u32[]{:S(2)}) copy-start(bf16[1168,128]{1,0:T(8,128)(2,1)S(1)} %collective-permute-done.3.kv1) | copy-start | bytes 897028
  124.0 27.4 %collective-permute-start.8 = (bf16[3,192,128]{2,1,0:T(8,128)(2,1)S(1)}, bf16[3,192,128]{2,1,0:T(8,128)(2,1)S(1)}, u32[]{:S(2)}, u32[]{:S(2)}) collective-permute-start(bf16[3,192,128]{2,1,0:T(8,128)(2,1)S(1)} %get-tuple-element.39), channel_id=1, source_target_pairs={{0,3},{1,2},{2,1},{3,0},{4,7},{5,6},{6,5},{7,4},{8,11},{9,10},{10,... | collective-permute-start | bytes 442376 | tf_op jit(solution)/shard_map/ppermute | solution.py:31
  132.8 2.0 copy-start.21
  134.8 0.7 copy-start.22
  134.8 0.9 copy-start.8
  151.3 0.7 copy-start.16
  151.4 0.7 copy-start.17
  151.4 0.7 copy-start.19
  167.9 29.2 %copy-start.4 = (bf16[1168,128]{1,0:T(8,128)(2,1)S(1)}, bf16[1168,128]{1,0:T(8,128)(2,1)}, u32[]{:S(2)}) copy-start(bf16[1168,128]{1,0:T(8,128)(2,1)} %get-tuple-element.26.refs_1_.kv0) | copy-start | bytes 897028
  189.8 24.4 %all-to-all-start.5 = ((bf16[64,4,8,128]{3,2,1,0:T(8,128)(2,1)}), bf16[64,4,8,128]{3,2,1,0:T(8,128)(2,1)S(1)}, u32[]{:S(2)}, u32[]{:S(2)}) async-start(bf16[64,4,8,128]{3,2,1,0:T(8,128)(2,1)} %bitcast.34), calls=%async_computation.5 | async-start | bytes 1048576 | tf_op jit(solution)/shard_map/all_to_all | solution.py:615
  197.2 13.2 %collective-permute-start.10 = (bf16[1168,128]{1,0:T(8,128)(2,1)S(1)}, bf16[1168,128]{1,0:T(8,128)(2,1)S(1)}, u32[]{:S(2)}, u32[]{:S(2)}) collective-permute-start(bf16[1168,128]{1,0:T(8,128)(2,1)S(1)} %copy-done.4), channel_id=1, source_target_pairs={{0,8},{4,12},{8,0},{12,4},{1,9},{5,13},{9,1},{13,5},{2,10},{6,14},... | collective-permute-start | bytes 897032 | tf_op jit(solution)/shard_map/ppermute | solution.py:31
  197.3 16.9 %collective-permute-start.11 = (bf16[1168,128]{1,0:T(8,128)(2,1)S(1)}, bf16[1168,128]{1,0:T(8,128)(2,1)S(1)}, u32[]{:S(2)}, u32[]{:S(2)}) collective-permute-start(bf16[1168,128]{1,0:T(8,128)(2,1)S(1)} %copy-done.4), channel_id=1, source_target_pairs={{0,12},{4,8},{8,4},{12,0},{1,13},{5,9},{9,5},{13,1},{2,14},{6,10},... | collective-permute-start | bytes 897032 | tf_op jit(solution)/shard_map/ppermute | solution.py:31
  198.3 15.8 %collective-permute-start.9 = (bf16[1168,128]{1,0:T(8,128)(2,1)S(1)}, bf16[1168,128]{1,0:T(8,128)(2,1)S(1)}, u32[]{:S(2)}, u32[]{:S(2)}) collective-permute-start(bf16[1168,128]{1,0:T(8,128)(2,1)S(1)} %copy-done.4), channel_id=1, source_target_pairs={{0,4},{4,0},{8,12},{12,8},{1,5},{5,1},{9,13},{13,9},{2,6},{6,2},{1... | collective-permute-start | bytes 897032 | tf_op jit(solution)/shard_map/ppermute | solution.py:31
  205.9 24.3 %collective-permute-start.12 = (bf16[3,192,128]{2,1,0:T(8,128)(2,1)S(1)}, bf16[3,192,128]{2,1,0:T(8,128)(2,1)S(1)}, u32[]{:S(2)}, u32[]{:S(2)}) collective-permute-start(bf16[3,192,128]{2,1,0:T(8,128)(2,1)S(1)} %get-tuple-element.38), channel_id=1, source_target_pairs={{0,1},{1,0},{2,3},{3,2},{4,5},{5,4},{6,7},{7,6},{8,9},{9,8},{10,11... | collective-permute-start | bytes 442376 | tf_op jit(solution)/shard_map/ppermute | solution.py:31
  207.3 22.9 %collective-permute-start.13 = (bf16[3,192,128]{2,1,0:T(8,128)(2,1)S(1)}, bf16[3,192,128]{2,1,0:T(8,128)(2,1)S(1)}, u32[]{:S(2)}, u32[]{:S(2)}) collective-permute-start(bf16[3,192,128]{2,1,0:T(8,128)(2,1)S(1)} %get-tuple-element.37), channel_id=1, source_target_pairs={{0,2},{1,3},{2,0},{3,1},{4,6},{5,7},{6,4},{7,5},{8,10},{9,11},{10,... | collective-permute-start | bytes 442376 | tf_op jit(solution)/shard_map/ppermute | solution.py:31
  210.3 3.8 %copy-start.11 = (bf16[1168,128]{1,0:T(8,128)(2,1)}, bf16[1168,128]{1,0:T(8,128)(2,1)S(1)}, u32[]{:S(2)}) copy-start(bf16[1168,128]{1,0:T(8,128)(2,1)S(1)} %collective-permute-done.10.kv2) | copy-start | bytes 897028
  210.3 19.9 %collective-permute-start.14 = (bf16[3,192,128]{2,1,0:T(8,128)(2,1)S(1)}, bf16[3,192,128]{2,1,0:T(8,128)(2,1)S(1)}, u32[]{:S(2)}, u32[]{:S(2)}) collective-permute-start(bf16[3,192,128]{2,1,0:T(8,128)(2,1)S(1)} %get-tuple-element.36), channel_id=1, source_target_pairs={{0,3},{1,2},{2,1},{3,0},{4,7},{5,6},{6,5},{7,4},{8,11},{9,10},{10,... | collective-permute-start | bytes 442376 | tf_op jit(solution)/shard_map/ppermute | solution.py:31
  214.1 0.8 copy-start.3
  214.1 0.9 copy-start.12
  214.1 1.0 copy-start.13
  230.2 0.7 copy-start.14
  230.2 0.7 copy-start.15
  230.2 0.7 copy-start.18
Sparse Core Ops, SparseCore 0:
  22.9 47.2 all-gather.7
where the time goes:
time: 242 us; the launch traced here: 240 us
  blocking collectives  71.1 us (29%)
  starting transfers between devices  60.1 us (25%)
  Pallas kernels  53.8 us (22%)
  waiting for transfers between devices  28.6 us (12%)
  between operations  14.3 us (6%)
  local copies, waits for them, and re-layouts  10.2 us (4%)
    pallas_call x13, Pallas kernels, local_call(): pl.pallas_call(kernel, grid=(1,), out_shape=out_shape, in_specs=in_specs,...  44 us
    ppermute x15, waiting for transfers between devices, swap(): return lax.ppermute(value, axis, [(k, k ^ flip) for k in range(size)])  25.2 us
    all_gather x2, blocking collectives, body(): attended = lax.all_gather(attended, 'col', axis=0)  21.2 us
    all_to_all x1, blocking collectives, body(): lax.all_to_all(after(pair_out, [both]).reshape(samp_size, share, own_rows...  20.1 us
    ppermute x15, starting transfers between devices, swap(): return lax.ppermute(value, axis, [(k, k ^ flip) for k in range(size)])  18.1 us
    all_to_all x2, starting transfers between devices, spread_bias(): lax.all_to_all(part, ('samp', 'col'), 0, 0, tiled=True).reshape(shape)  17.3 us
    all_to_all x1, starting transfers between devices, body(): lax.all_to_all(triangle, ('samp', 'row', 'col'), 0, 0, tiled=True)  13.9 us
    all_gather x1, blocking collectives, body(): attn_full = lax.all_gather(attn_local, 'col', axis=0)  11.6 us
  transfers between devices with their start and end apart: 21, of which 6 were waited for; matrix products, arithmetic and copies ran while one was open for 2% of the time, Pallas kernels for 19%

commit v1 on v0

v1 whole, which is shorter than its diff:
```python
import math

import jax
import jax.numpy as jnp
from jax import lax
from jax.experimental import pallas as pl
from jax.experimental.pallas import tpu as pltpu
from jax.sharding import PartitionSpec as P

DA = 768
HEAD_DIM = 48
TEMB = 256


EPS = 1e-05
MASK_FILL = 1000000000.0
MIB = 1024 * 1024
CLAIM = 63
MASK_ROWS = 16
NEAR = 4


def channel_norm(values, axis):
    mean_value = jnp.mean(values, axis=axis, keepdims=True)
    centred = values - mean_value
    spread = jnp.mean(centred * centred, axis=axis, keepdims=True)
    return centred * lax.rsqrt(spread + EPS)


def swap(value, axis, flip):
    size = lax.axis_size(axis)
    return lax.ppermute(value, axis, [(k, k ^ flip) for k in range(size)])


def swap_all(value, axis):
    return [value] + [swap(value, axis, flip) for flip in range(1, lax.axis_size(axis))]


def expected(micros):
    return pl.CostEstimate(flops=0, bytes_accessed=int(micros * 3.69e6), transcendentals=0)


def local_call(kernel, out_shape, in_specs, args, scratch, micros, name):
    return pl.pallas_call(
        kernel,
        grid=(1,),
        out_shape=out_shape,
        in_specs=in_specs,
        out_specs=jax.tree.map(lambda o: whole(o.shape), out_shape),
        scratch_shapes=scratch,
        compiler_params=pltpu.CompilerParams(vmem_limit_bytes=CLAIM * MIB),
        cost_estimate=expected(micros),
        name=name,
    )(*args)


def whole(shape):
    return pl.BlockSpec(tuple(shape), lambda i: (0,) * len(shape))


def layer_block(shape, at, layer):
    block = tuple(1 if d == at else n for d, n in enumerate(shape))
    return pl.BlockSpec(block, lambda i: tuple(layer if d == at else 0 for d in range(len(shape))))


SCALAR = pl.BlockSpec(memory_space=pltpu.SMEM)
UNREAD = pl.BlockSpec(memory_space=pl.ANY)


def after(value, others):
    return pl.pallas_call(
        lambda *refs: None,
        out_shape=jax.ShapeDtypeStruct(value.shape, value.dtype),
        in_specs=[UNREAD] * (1 + len(others)),
        out_specs=UNREAD,
        input_output_aliases={0: 0},
        name="after",
    )(value, *others)


def stack_gathered(gathered, full):
    parts, samples, width, tokens = gathered.shape
    for k in range(parts):
        for s in range(samples):
            full[k * width : (k + 1) * width, s * tokens : (s + 1) * tokens] = gathered[k, s]


def stack_normed(gathered, shared, full, normed):
    parts, samples, width, tokens = gathered.shape
    for s in range(samples):
        at = slice(s * tokens, (s + 1) * tokens)
        value = jnp.concatenate([gathered[k, s] for k in range(parts)], 0).astype(jnp.float32)
        value = channel_norm(value, 0)
        normed[:, at] = value
        for k in range(parts):
            gain, shift = shared[k, 0, s], shared[k, 1, s]
            full[k * width : (k + 1) * width, at] = (
                gain.astype(jnp.float32) * value[k * width : (k + 1) * width]
                + shift.astype(jnp.float32)
            ).astype(jnp.bfloat16)


def project_full(full, query_w, key_w, value_gate_w, mask, queries, gates, both):
    samples, width, tokens = queries.shape

    def times(weight):
        return jnp.dot(weight, full[...], preferred_element_type=jnp.float32).astype(jnp.bfloat16)

    key, value = times(key_w[0]), times(value_gate_w[0, 0])
    query, gate = times(query_w[0]), times(value_gate_w[0, 1])
    for s in range(samples):
        at = slice(s * tokens, (s + 1) * tokens)
        queries[s] = query[:, at]
        gates[s] = gate[:, at]
        both[2 * s * width : (2 * s + 1) * width] = key[:, at]
        both[(2 * s + 1) * width : (2 * s + 2) * width] = value[:, at]
    both[2 * samples * width :] = jnp.broadcast_to(mask[...], (MASK_ROWS, tokens))


def project_kernel(gathered, *refs):
    stack_gathered(gathered, refs[-1])
    project_full(refs[-1], *refs[:-1])


def normed_project_kernel(me_ref, gathered, shared, gain, shift, *refs):
    query_w, key_w, value_gate_w, mask, queries, gates, both, trans, full, normed = refs
    stack_normed(gathered, shared, full, normed)
    samples, width, tokens = trans.shape
    start = pl.multiple_of(me_ref[0] * width, width)
    for s in range(samples):
        piece = normed[pl.ds(start, width), s * tokens : (s + 1) * tokens]
        trans[s] = (gain[0, s] * piece + shift[0, s]).astype(jnp.bfloat16)
    project_full(full, query_w, key_w, value_gate_w, mask, queries, gates, both)


def mod_block(mods, m):
    return pl.BlockSpec((1,) + mods.shape[1:], lambda i: (m, 0, 0, 0))


def project(blocks, query_w, key_w, value_gate_w, mask, layer, me=None, shared=None, mods=None):
    samples, width, tokens = blocks[0].shape[-3:]
    small = jax.ShapeDtypeStruct((samples, width, tokens), jnp.bfloat16)
    joint = jax.ShapeDtypeStruct((2 * samples * width + MASK_ROWS, tokens), jnp.bfloat16)
    depth = query_w.shape[2]
    specs = [
        layer_block(query_w.shape, 0, layer),
        layer_block(key_w.shape, 0, layer),
        layer_block(value_gate_w.shape, 0, layer),
        whole(mask.shape),
    ]
    args = [query_w, key_w, value_gate_w, mask]
    full = pltpu.VMEM((depth, samples * tokens), jnp.bfloat16)
    if shared is None:
        return local_call(
            project_kernel,
            (small, small, joint),
            [whole(blocks[0].shape)] + specs,
            [*blocks, *args],
            [full],
            3.0,
            "project",
        )
    specs = [whole(blocks[0].shape), whole(shared.shape), mod_block(mods, 6), mod_block(mods, 7)] + specs
    return local_call(
        normed_project_kernel,
        (small, small, joint, small),
        [SCALAR] + specs,
        [me, *blocks, shared, mods, mods, *args],
        [full, pltpu.VMEM((depth, samples * tokens), jnp.float32)],
        4.0,
        "normed_project",
    )


def hand_out(total, me, keep, give):
    samples, width, tokens = keep.shape[1:]
    for e in range(keep.shape[0]):
        for target, flip in ((keep, 2 * e), (give, 2 * e + 1)):
            start = pl.multiple_of((me ^ flip) * width, width)
            for s in range(samples):
                piece = total[pl.ds(start, width), s * tokens : (s + 1) * tokens]
                target[e, s] = piece.astype(target.dtype)


def join_kernel(keep, came, out):
    out[...] = (keep[0] + came[0].astype(jnp.float32)).astype(out.dtype)


def sum_parts(keep, give):
    came = swap(give, "col", 1)
    far = local_call(
        join_kernel,
        jax.ShapeDtypeStruct(keep.shape[1:], jnp.bfloat16),
        [pl.BlockSpec((1,) + keep.shape[1:], lambda i: (1, 0, 0, 0))] * 2,
        [keep, came],
        [],
        1.0,
        "join",
    )
    return [keep, came, swap(far, "col", 2)]


def transition_kernel(me_ref, gathered, up, down, keep, give, full, total):
    stack_gathered(gathered, full)
    over_rows = (((0,), (0,)), ((), ()))
    swish = lax.dot_general(up[0, 0], full[...], over_rows, preferred_element_type=jnp.float32)
    linear = lax.dot_general(up[0, 1], full[...], over_rows, preferred_element_type=jnp.float32)
    hidden = (swish / (1.0 + jnp.exp(-swish)) * linear).astype(jnp.bfloat16)
    total[...] = lax.dot_general(down[0], hidden, over_rows, preferred_element_type=jnp.float32)
    hand_out(total, me_ref[0], keep, give)


def transition(gathered, me, up, down, layer, col_size):
    samples, width, tokens = gathered.shape[1:]
    depth, hidden = up.shape[2:]
    return local_call(
        transition_kernel,
        tuple(
            jax.ShapeDtypeStruct((col_size // 2, samples, width, tokens), dtype)
            for dtype in (jnp.float32, jnp.bfloat16)
        ),
        [SCALAR, whole(gathered.shape)]
        + [layer_block(up.shape, 0, layer), layer_block(down.shape, 0, layer)],
        [me, gathered, up, down],
        [
            pltpu.VMEM((depth, samples * tokens), jnp.bfloat16),
            pltpu.VMEM((depth, samples * tokens), jnp.float32),
        ],
        3.8,
        "transition",
    )


def attention_kernel(me_ref, queries, gates, kv0, kv1, kv2, kv3, bias0, bias1, bias2, bias3, *refs):
    out_w, keep, give, full, total, added = refs[0], *refs[-5:]
    pieces, biases = (kv0, kv1, kv2, kv3), (bias0, bias1, bias2, bias3)
    row_at, near_at, col_at = me_ref[0], me_ref[1], me_ref[2]
    samples, width, tokens = queries.shape
    far, cols, _, heads, count, keys = bias0.shape
    for k, bias in enumerate(biases):
        for z in range(far):
            start = pl.multiple_of((z * len(biases) + (near_at ^ k)) * count, count)
            for j in range(cols):
                added[:, pl.ds(start, count), j * keys : (j + 1) * keys] = bias[
                    z, row_at ^ j, 0
                ].astype(jnp.float32)
    scale = 1.0 / math.sqrt(HEAD_DIM)
    lane = lax.broadcasted_iota(jnp.int32, (tokens, width), 1) // HEAD_DIM
    masks = jnp.concatenate(
        [kv[2 * samples * width : 2 * samples * width + 1].astype(jnp.float32) for kv in pieces], 1
    )
    mask_add = (masks - 1.0) * MASK_FILL
    for s in range(samples):
        query = jnp.transpose(queries[s].astype(jnp.float32))
        key = jnp.concatenate([kv[2 * s * width : (2 * s + 1) * width] for kv in pieces], 1)
        value = jnp.concatenate([kv[(2 * s + 1) * width : (2 * s + 2) * width] for kv in pieces], 1)
        kept = jnp.zeros((tokens, width), jnp.float32)
        for h in range(heads):
            mine = lane == h
            scores = jnp.dot(
                jnp.where(mine, query, 0.0).astype(jnp.bfloat16),
                key,
                preferred_element_type=jnp.float32,
            )
            scores = scores * scale + added[h] + mask_add
            exps = jnp.exp(scores - jnp.max(scores, axis=1, keepdims=True))
            norm = jnp.sum(exps, axis=1, keepdims=True)
            product = lax.dot_general(
                exps.astype(jnp.bfloat16),
                value,
                (((1,), (1,)), ((), ())),
                preferred_element_type=jnp.float32,
            )
            kept = jnp.where(mine, product / norm, kept)
        gate = jax.nn.sigmoid(gates[s].astype(jnp.float32))
        full[:, s * tokens : (s + 1) * tokens] = (gate * jnp.transpose(kept)).astype(jnp.bfloat16)
    total[...] = lax.dot_general(
        out_w[0], full[...], (((0,), (0,)), ((), ())), preferred_element_type=jnp.float32
    )
    hand_out(total, col_at, keep, give)


def attention(me, queries, gates, pieces, biases, out_w, layer, others):
    samples, width, tokens = queries.shape
    heads = biases[0].shape[3]
    parts = out_w.shape[2] // width
    args = [me, queries, gates, *pieces]
    return local_call(
        attention_kernel,
        tuple(
            jax.ShapeDtypeStruct((parts // 2,) + queries.shape, dtype)
            for dtype in (jnp.float32, jnp.bfloat16)
        ),
        [SCALAR]
        + [whole(a.shape) for a in args[1:]]
        + [layer_block(b.shape, 2, layer) for b in biases]
        + [layer_block(out_w.shape, 0, layer)]
        + [UNREAD] * len(others),
        [*args, *biases, out_w, *others],
        [
            pltpu.VMEM((width, samples * tokens), jnp.bfloat16),
            pltpu.VMEM((parts * width, samples * tokens), jnp.float32),
            pltpu.VMEM((heads, tokens, len(pieces) * tokens), jnp.float32),
        ],
        5.4,
        "attention",
    )


def finish_kernel(keep_a, came_a, far_a, keep_t, came_t, far_t, gate_a, gate_t, *refs):
    state = refs[-1]
    for s in range(state.shape[0]):
        branch, trans = (
            keep[0, s] + came[0, s].astype(jnp.float32) + far[s].astype(jnp.float32)
            for keep, came, far in ((keep_a, came_a, far_a), (keep_t, came_t, far_t))
        )
        state[s] = (gate_a[0, s] * branch + gate_t[0, s] * trans).astype(state.dtype)


def finish(attended, trans, mods, gate_at, others):
    block = mods.shape[1:]
    first = pl.BlockSpec((1,) + block, lambda i: (0, 0, 0, 0))
    return local_call(
        finish_kernel,
        jax.ShapeDtypeStruct(block, jnp.bfloat16),
        [first, first, whole(block)] * 2
        + [mod_block(mods, gate_at), mod_block(mods, gate_at + 1)]
        + [UNREAD] * len(others),
        [*attended, *trans, mods, mods, *others],
        [],
        2.0,
        "finish",
    )


def modulate_kernel(single, shift, mod_w, *refs):
    own, shared, normed = refs[-3:]
    samples, width, tokens = own.shape[1:]
    layers, count = mod_w.shape[:2]
    for s in range(samples):
        condition = single[...].astype(jnp.float32) + shift[s : s + 1, :]
        normed[s * tokens : (s + 1) * tokens] = channel_norm(condition, 1).astype(jnp.bfloat16)
    kept = 0
    for layer in range(layers):
        for m in range(count):
            made = lax.dot_general(
                mod_w[layer, m],
                normed[...],
                (((1,), (1,)), ((), ())),
                preferred_element_type=jnp.float32,
            )
            if m not in (1, 3):
                made = jax.nn.sigmoid(made)
            for s in range(samples):
                piece = made[:, s * tokens : (s + 1) * tokens]
                if layer > 0 and m < 2:
                    shared[m, s] = piece.astype(jnp.bfloat16)
                else:
                    own[kept, s] = piece
            kept += layer == 0 or m >= 2


def modulate(single, shift, mod_w, others):
    layers, count, width, depth = mod_w.shape
    tokens, samples = single.shape[0], shift.shape[0]
    return local_call(
        modulate_kernel,
        (
            jax.ShapeDtypeStruct((count + 4, samples, width, tokens), jnp.float32),
            jax.ShapeDtypeStruct((2, samples, width, tokens), jnp.bfloat16),
        ),
        [whole(single.shape), whole(shift.shape), whole(mod_w.shape)] + [UNREAD] * len(others),
        [single, shift, mod_w, *others],
        [pltpu.VMEM((samples * tokens, depth), jnp.bfloat16)],
        4.8,
        "modulate",
    )


def first_inputs_kernel(state, sums, mods, attn, trans):
    mean_value = sums[0] / DA
    scale = lax.rsqrt(sums[1] / DA - mean_value * mean_value + EPS)
    for s in range(state.shape[0]):
        normed = (state[s].astype(jnp.float32) - mean_value[s : s + 1]) * scale[s : s + 1]
        attn[s] = (mods[0, s] * normed + mods[1, s]).astype(jnp.bfloat16)
        trans[s] = (mods[2, s] * normed + mods[3, s]).astype(jnp.bfloat16)


def first_inputs(state, sums, mods):
    out = jax.ShapeDtypeStruct(state.shape, jnp.bfloat16)
    return local_call(
        first_inputs_kernel,
        (out, out),
        [
            whole(state.shape),
            whole(sums.shape),
            pl.BlockSpec((4,) + state.shape, lambda i: (0, 0, 0, 0)),
        ],
        [state, sums, mods],
        [],
        2.0,
        "first_inputs",
    )


def triangle_kernel(came, *refs):
    out = refs[-1]
    rows, cols, _, keys = came.shape
    half = 8 * out.shape[0]

    def joined(at):
        return jnp.concatenate(
            [jnp.concatenate([came[r, c, at] for c in range(cols)], 1) for r in range(rows)], 0
        )

    sums = lax.dot_general(
        joined(slice(0, half)),
        joined(slice(half, half + keys)),
        (((1,), (1,)), ((), ())),
        preferred_element_type=jnp.float32,
    )
    groups = half // 8
    upper = lax.broadcasted_iota(jnp.int32, (groups, 8, keys), 1) < 4
    for r in range(rows):
        for c in range(0, cols, 2):
            one, two = (
                sums[r * half : (r + 1) * half, k * keys : (k + 1) * keys].reshape(groups, 8, keys)
                for k in (c, c + 1)
            )
            even = jnp.where(upper, one, pltpu.roll(two, 4, 1))
            odd = jnp.where(upper, pltpu.roll(one, 4, 1), two)
            out[:, 0, r, c // 2] = even.astype(jnp.bfloat16)
            out[:, 1, r, c // 2] = odd.astype(jnp.bfloat16)


def triangle_sums(came, others):
    rows, cols, height, keys = came.shape
    half = height - keys
    left = rows * half
    return local_call(
        triangle_kernel,
        jax.ShapeDtypeStruct((half // 8, 2, rows, cols // 2, 8, keys), jnp.bfloat16),
        [whole(came.shape)] + [UNREAD] * len(others),
        [came, *others],
        [],
        2.2,
        "triangle_sums",
    )


def pair_project_kernel(me_ref, pair, tri, *refs):
    out, weight, normed, left, right = refs[-5:]
    step = pl.program_id(0)
    channels, rows, keys = pair.shape
    height = rows * pl.num_programs(0)
    share = weight.shape[0] // 4
    halves = out.shape[0] // share
    part = out.shape[1] - keys
    group = 8 // halves

    @pl.when(step == 0)
    def _():
        mine = lax.broadcasted_iota(jnp.int32, (share, channels), 0) + me_ref[0] * share
        pick = mine == lax.broadcasted_iota(jnp.int32, (share, channels), 1)
        for p in range(4):
            weight[p * share : (p + 1) * share] = lax.dot_general(
                pick.astype(jnp.bfloat16),
                tri[p],
                (((1,), (1,)), ((), ())),
                preferred_element_type=jnp.float32,
            )

    value = pair[...].astype(jnp.float32)
    normed[...] = channel_norm(value, 0).reshape(channels * rows, keys)
    weights = weight[...].astype(jnp.bfloat16)
    for i in range(0, rows, 2):
        two = [normed[pl.ds(i + e, channels, stride=rows), :] for e in (0, 1)]
        made = jnp.dot(
            weights, jnp.concatenate(two, 1).astype(jnp.bfloat16), preferred_element_type=jnp.float32
        )
        made_left = jax.nn.sigmoid(made[:share]) * made[share : 2 * share]
        made_right = jax.nn.sigmoid(made[2 * share : 3 * share]) * made[3 * share :]
        for e in (0, 1):
            row, at = i + e, slice(e * keys, (e + 1) * keys)
            right[pl.ds(step * rows + row, share, stride=keys), :] = made_right[:, at]
            place = (row % 8) // group * part + row // 8 * group + row % group
            place = step * (rows // 8 * group) + place
            left[pl.ds(place, share, stride=keys), :] = made_left[:, at]

    @pl.when(step == pl.num_programs(0) - 1)
    def _():
        for c in range(share):
            whole_right = right[c * keys : (c + 1) * keys].astype(jnp.bfloat16)
            for h in range(halves):
                start = c * keys + h * part
                out[c * halves + h, :part] = left[start : start + part].astype(jnp.bfloat16)
                out[c * halves + h, part:] = whole_right


def pair_project(pair_in, tri_weight, me, group, samp_size, others):
    channels, height, keys = pair_in.shape
    share = channels // samp_size
    part = height // (group // share)
    rows = 16
    out = jax.ShapeDtypeStruct((group, part + height, keys), jnp.bfloat16)
    return pl.pallas_call(
        pair_project_kernel,
        grid=(height // rows,),
        out_shape=out,
        in_specs=[
            SCALAR,
            pl.BlockSpec((channels, rows, keys), lambda i: (0, i, 0)),
            whole(tri_weight.shape),
        ]
        + [UNREAD] * len(others),
        out_specs=whole(out.shape),
        scratch_shapes=[
            pltpu.VMEM((4 * share, channels), jnp.float32),
            pltpu.VMEM((channels * rows, keys), jnp.float32),
            pltpu.VMEM((share * height, keys), jnp.float32),
            pltpu.VMEM((share * height, keys), jnp.float32),
        ],
        compiler_params=pltpu.CompilerParams(vmem_limit_bytes=CLAIM * MIB),
        cost_estimate=expected(9.7),
        name="pair_project",
    )(me, pair_in, tri_weight, *others)


def pair_update_kernel(came, own, gate_w, out_w, bias_w, *refs):
    back, message, rows_a, rows_b, rows_c = refs[-5:]
    channels, count, keys = came.shape
    over_rows = (((0,), (0,)), ((), ()))

    def by_channel(value, rows):
        rows[...] = value.astype(jnp.float32).reshape(channels * count, keys)
        return jnp.concatenate([rows[pl.ds(u, channels, stride=count), :] for u in range(count)], 1)

    def normed(value):
        return channel_norm(value, 0).astype(jnp.bfloat16)

    pair = by_channel(own[...], rows_a)
    sums = by_channel(came[...], rows_b)
    gate = lax.dot_general(gate_w[0], normed(pair), over_rows, preferred_element_type=jnp.float32)
    update = lax.dot_general(out_w[...], normed(sums), over_rows, preferred_element_type=jnp.float32)
    new = (pair + jax.nn.sigmoid(gate) * update).astype(jnp.bfloat16).astype(jnp.float32)
    bias = jnp.dot(bias_w[...], normed(new), preferred_element_type=jnp.float32)
    for u in range(count):
        at = slice(u * keys, (u + 1) * keys)
        rows_b[pl.ds(u, channels, stride=count), :] = new[:, at]
        rows_c[pl.ds(u, bias.shape[0], stride=count), :] = bias[:, at]
    back[...] = rows_b[...].reshape(channels, count, keys).astype(jnp.bfloat16)
    _, cols, layers, heads = message.shape[:4]
    made = rows_c[...].reshape(layers, cols, heads, count, keys).astype(jnp.bfloat16)
    for k in range(message.shape[0]):
        for layer in range(layers):
            message[k, :, layer] = made[layer]


def pair_update(came, own, tri_weight, out_weight, bias_w, layers, samp_size, col_size, others):
    channels, count, keys = came.shape
    heads = bias_w.shape[0] // (layers * col_size)
    message = jax.ShapeDtypeStruct(
        (samp_size, col_size, layers, heads, count, keys), jnp.bfloat16
    )
    return local_call(
        pair_update_kernel,
        (jax.ShapeDtypeStruct(came.shape, jnp.bfloat16), message),
        [
            whole(came.shape),
            whole(own.shape),
            layer_block(tri_weight.shape, 0, 4),
            whole(out_weight.shape),
            whole(bias_w.shape),
        ]
        + [UNREAD] * len(others),
        [came, own, tri_weight, out_weight, bias_w, *others],
        [
            pltpu.VMEM((channels * count, keys), jnp.float32),
            pltpu.VMEM((channels * count, keys), jnp.float32),
            pltpu.VMEM((bias_w.shape[0] * count, keys), jnp.float32),
        ],
        2.8,
        "pair_update",
    )


def pair_rows_kernel(came, out):
    for c in range(came.shape[1]):
        rows = [came[k, c].astype(jnp.float32) for k in range(came.shape[0])]
        out[c] = jnp.concatenate(rows, 0).astype(jnp.bfloat16)


def pair_rows_joined(came):
    parts, share, count, keys = came.shape
    return local_call(
        pair_rows_kernel,
        jax.ShapeDtypeStruct((share, parts * count, keys), jnp.bfloat16),
        [whole(came.shape)],
        [came],
        [],
        1.7,
        "pair_rows",
    )


def body(
    pair_in,
    token_act,
    single,
    noise_sigma,
    token_mask,
    tri_weight,
    out_weight,
    bias_weight,
    time_weight,
    mod_weight,
    query_weight,
    key_weight,
    value_gate_weight,
    attn_out_weight,
    up_weight,
    down_weight,
):
    channels, pair_rows, pair_cols = pair_in.shape
    samp_size, row_size, col_size = (lax.axis_size(name) for name in ("samp", "row", "col"))
    group = row_size * col_size
    share = channels // samp_size
    halves = group // share
    half_rows = pair_rows // halves
    cell_rows = half_rows // samp_size
    own_rows = halves * cell_rows
    samp_at = jnp.reshape(lax.axis_index("samp"), (1,))
    row_at = jnp.reshape(lax.axis_index("row"), (1,))
    col_at = jnp.reshape(lax.axis_index("col"), (1,))
    blocks, _, head_count = bias_weight.shape

    state = jnp.swapaxes(token_act, 1, 2)
    samples, width, row_count = state.shape
    wide = state.astype(jnp.float32)
    sums = jnp.stack([jnp.sum(wide, 1), jnp.sum(wide * wide, 1)])
    sums = sum(swap_all(sums, "col"))
    query_w = jnp.swapaxes(query_weight, 1, 2)
    key_w = jnp.swapaxes(key_weight, 1, 2)
    value_gate_w = jnp.swapaxes(value_gate_weight, 2, 3)
    mod_w = jnp.swapaxes(mod_weight, 2, 3)
    half_count = TEMB // 2
    frequency = jnp.exp(jnp.arange(half_count, dtype=jnp.float32) * (math.log(100.0) / half_count))
    angles = (jnp.log(noise_sigma) * 0.25)[:, None] * frequency[None, :]
    time_embed = jnp.concatenate([jnp.cos(angles), jnp.sin(angles)], 1).astype(jnp.bfloat16)
    time_shift = jnp.dot(time_embed, time_weight, preferred_element_type=jnp.float32)

    to_send = pair_project(pair_in, tri_weight, samp_at, group, samp_size, [sums])
    came = lax.all_to_all(to_send, ("row", "col"), 0, 0, tiled=True)
    came = came.reshape(row_size, col_size, half_rows + pair_rows, pair_cols)

    mods, shared = modulate(single, time_shift, mod_w, [to_send])
    attn_local, trans_local = first_inputs(state, sums, mods)
    attn_full = lax.all_gather(attn_local, "col", axis=0)

    triangle = triangle_sums(came, [attn_full])
    shared = lax.all_gather(shared, "col", axis=0)
    triangle = triangle.reshape(samp_size * group, cell_rows, pair_cols)
    triangle = lax.all_to_all(triangle, ("samp", "row", "col"), 0, 0, tiled=True)
    triangle = triangle.reshape(channels, own_rows, pair_cols)
    mask_row = token_mask.astype(jnp.bfloat16)[None]
    queries, gates, both = project([attn_full], query_w, key_w, value_gate_w, mask_row, 0)
    pieces = swap_all(both, "row")

    own_pair = lax.dynamic_slice_in_dim(pair_in, samp_at[0] * own_rows, own_rows, 1)
    bias_w = jnp.swapaxes(bias_weight, 1, 2).reshape(blocks * head_count, channels)
    pair_out, bias = pair_update(
        triangle,
        own_pair,
        tri_weight,
        out_weight,
        bias_w,
        blocks,
        samp_size // NEAR,
        col_size,
        [both, shared],
    )
    far = samp_size // NEAR
    message = bias.shape
    bias = lax.all_to_all(
        bias.reshape((far * col_size,) + message[2:]),
        ("samp", "col"),
        0,
        0,
        axis_index_groups=[
            [(z * NEAR + x) * col_size + c for z in range(far) for c in range(col_size)]
            for x in range(NEAR)
        ],
        tiled=True,
    ).reshape(message)
    biases = [bias] + [
        lax.ppermute(bias, "samp", [(k, k ^ flip) for k in range(samp_size)])
        for flip in range(1, NEAR)
    ]
    pair_back = after(pair_out, [biases[1]]).reshape(samp_size, share, own_rows, pair_cols)
    pair_back = lax.all_to_all(pair_back, "samp", 0, 0, tiled=True)
    trans_full = lax.all_gather(trans_local, "col", axis=0)
    trans = transition(trans_full, col_at, up_weight, down_weight, 0, col_size)
    trans_sum = sum_parts(*trans)
    seat = jnp.concatenate([row_at, samp_at % NEAR, col_at])

    for layer in range(blocks):
        if layer > 0:
            queries, gates, both, trans_local = project(
                [state], query_w, key_w, value_gate_w, mask_row, layer, col_at, shared, mods
            )
            pieces = swap_all(both, "row")
            trans_full = lax.all_gather(trans_local, "col", axis=0)
            trans = transition(trans_full, col_at, up_weight, down_weight, layer, col_size)
            trans_sum = sum_parts(*trans)
        attended = attention(
            seat, queries, gates, pieces, biases, attn_out_weight, layer, [trans[0] if layer else trans_sum[2]]
        )
        state = finish(
            sum_parts(*attended), trans_sum, mods, 4 * (1 + layer), [] if layer else [pair_back]
        )
        if layer == 0:
            state = lax.all_gather(state, "col", axis=0)
    pair_back = pair_rows_joined(pair_back)
    return (pair_back, jnp.swapaxes(state, 1, 2))


def solution(mesh):
    placed = (
        P(None, "row", "col"),
        P("samp", "row", "col"),
        P("row", None),
        P("samp"),
        P("row"),
        P(),
        P(),
        P(),
        P(),
        P(None, None, None, "col"),
        P(None, None, "col"),
        P(None, None, "col"),
        P(None, None, None, "col"),
        P(None, "col", None),
        P(None, None, None, "col"),
        P(None, "col", None),
    )
    return jax.shard_map(
        body,
        mesh=mesh,
        in_specs=placed,
        out_specs=(P("samp", "row", "col"), P("samp", "row", "col")),
        check_vma=False,
    )
```

time: 242 us -> 205 us (0.85)
  blocking collectives: 71.1 us -> 42.6 us
  starting transfers between devices: 60.1 us -> 47.9 us
  Pallas kernels: 53.8 us -> 60.4 us
  waiting for transfers between devices: 28.6 us -> 23.3 us
  other arithmetic: 1.54 us -> 4.78 us
    all_gather x2 -> x0, blocking collectives: 21.2 us -> none  [body(): attended = lax.all_gather(attended, 'col', axis=0)]
    all_to_all x1 -> x0, blocking collectives: 20.1 us -> none  [body(): lax.all_to_all(after(pair_out, [both]).reshape(samp_size, share, own_rows...]
    all_gather x1 -> x2, blocking collectives: 9.11 us -> 23.2 us  [body(): trans_full = lax.all_gather(trans_local, 'col', axis=0)]
    all_to_all x3 -> x2, starting transfers between devices: 24 us -> 10 us  [the longest x1 6.16 us: body(): pair_back = lax.all_to_all(pair_back, 'samp', 0, 0, tiled=True)]
    ppermute x15 -> x17, waiting for transfers between devices: 25.2 us -> 12.2 us  [swap(): return lax.ppermute(value, axis, [(k, k ^ flip) for k in range(size)])]
    all_to_all x1, waiting for transfers between devices: 0.01 us -> 9.99 us  [body(): lax.all_to_all(triangle, ('samp', 'row', 'col'), 0, 0, tiled=True)]
    pallas_call x13 -> x17, Pallas kernels: 44 us -> 50.7 us  [local_call(): pl.pallas_call(kernel, grid=(1,), out_shape=out_shape, in_specs=in_specs,...]
    ppermute x0 -> x3, starting transfers between devices: none -> 3.85 us  [body(): lax.ppermute(bias, 'samp', [(k, k ^ flip) for k in range(samp_size)])]
  transfers between devices with their start and end apart: 21 -> 25, of which waited for: 6 -> 8; matrix products, arithmetic and copies ran while one was open for 2% -> 3% of each run, Pallas kernels for 19% -> 19%
where the time goes in v1:
time: 205 us; the launch traced here: 203 us
  Pallas kernels  60.4 us (29%)
  starting transfers between devices  47.9 us (23%)
  blocking collectives  42.6 us (21%)
  waiting for transfers between devices  23.3 us (11%)
  between operations  14.1 us (7%)
  local copies, waits for them, and re-layouts  8.78 us (4%)
  other arithmetic  4.78 us (2%)
    pallas_call x17, Pallas kernels, local_call(): pl.pallas_call(kernel, grid=(1,), out_shape=out_shape, in_specs=in_specs,...  50.7 us
    all_gather x2, blocking collectives, body(): trans_full = lax.all_gather(trans_local, 'col', axis=0)  23.2 us
    ppermute x17, starting transfers between devices, swap(): return lax.ppermute(value, axis, [(k, k ^ flip) for k in range(size)])  15.8 us
    all_to_all x1, starting transfers between devices, body(): lax.all_to_all(triangle, ('samp', 'row', 'col'), 0, 0, tiled=True)  13.6 us
    ppermute x17, waiting for transfers between devices, swap(): return lax.ppermute(value, axis, [(k, k ^ flip) for k in range(size)])  12.2 us
    all_gather x1, blocking collectives, body(): attn_full = lax.all_gather(attn_local, 'col', axis=0)  10.4 us
    all_to_all x1, waiting for transfers between devices, body(): lax.all_to_all(triangle, ('samp', 'row', 'col'), 0, 0, tiled=True)  9.99 us
    pallas_call x1, Pallas kernels, pair_project(): pl.pallas_call(pair_project_kernel, grid=(height // rows,), out_shape=out...  9.64 us
  transfers between devices with their start and end apart: 25, of which 8 were waited for; matrix products, arithmetic and copies ran while one was open for 3% of the time, Pallas kernels for 19%

profile of v1, /device:TPU:1, one launch (start us, length us, event | category | flops | bytes accessed | tf_op | source)
XLA Modules:
  0.0 203.2 jit_solution(4396098291658935446)
XLA Ops:
  7.2 1.0 convert_reduce_fusion
  8.2 3.3 %collective-permute-start = (f32[2,3,128]{2,1,0:T(4,128)S(1)}, f32[2,3,128]{2,1,0:T(4,128)S(1)}, u32[]{:S(2)}, u32[]{:S(2)}) collective-permute-start(f32[2,3,128]{2,1,0:T(4,128)S(1)} %pad_maximum_fusion), channel_id=1, source_target_pairs={{0,1},{1,0},{2,3},{3,2},{4,5},{5,4},{6,7},{7,6},{8,9},{9,8},{10,11... | collective-permute-start | bytes 9224 | tf_op jit(solution)/shard_map/ppermute | solution.py:32
  11.5 1.7 collective-permute-start.2
  13.3 0.7 log_multiply_fusion
  13.9 0.7 fusion.1
  14.6 0.2 collective-permute-done.2
  14.8 0.6 add_add_fusion.refs_0_.sums
  15.4 9.6 %pair_project.1.refs_0_ = bf16[16,192,128]{2,1,0:T(8,128)(2,1)} custom-call(s32[1]{0:T(128)} %bitcast.me_ref, bf16[128,128,128]{2,1,0:T(8,128)(2,1)} %pair.1, bf16[5,128,128]{2,1,0:T(8,128)(2,1)} %gate_w.1, f32[2,3,128]{2,1,0:T(4,128)} %add_add_fusion.refs_0_.sums), custom_call_target="tpu_custom_call" | custom-call | bytes 35793000 | tf_op jit(solution)/shard_map/pair_project/pallas_call | solution.py:506
  25.1 4.5 %all-to-all-start = ((bf16[16,192,128]{2,1,0:T(8,128)(2,1)}), bf16[16,192,128]{2,1,0:T(8,128)(2,1)S(1)}, u32[]{:S(2)}, u32[]{:S(2)}) async-start(bf16[16,192,128]{2,1,0:T(8,128)(2,1)} %pair_project.1.refs_0_), calls=%async_computation | async-start | bytes 1572864 | tf_op jit(solution)/shard_map/all_to_all | solution.py:653
  29.6 1.4 fusion.3.shift
  31.0 4.8 %modulate.1 = (f32[10,3,192,128]{3,2,1,0:T(8,128)}, bf16[2,3,192,128]{3,2,1,0:T(8,128)(2,1)}) custom-call(bf16[128,384]{1,0:T(8,128)(2,1)} %single.1, f32[3,384]{1,0:T(4,128)} %fusion.3.shift, bf16[2,6,192,384]{3,2,1,0:T(8,128)(2,1)} %bitcast.49, bf16[16,192,128]{2,1,0:T(8,128)(2,1)} %pair_project.1.refs_0_), custom_call_target="tpu_custom_call" | custom-call | bytes 17712000 | tf_op jit(solution)/shard_map/modulate/pallas_call | solution.py:44
  35.9 2.2 %first_inputs.1 = (bf16[3,192,128]{2,1,0:T(8,128)(2,1)}, bf16[3,192,128]{2,1,0:T(8,128)(2,1)}) custom-call(bf16[3,192,128]{2,1,0:T(8,128)(2,1)} %bitcast.53, f32[2,3,128]{2,1,0:T(4,128)} %add_add_fusion.refs_0_.sums, f32[10,3,192,128]{3,2,1,0:T(8,128)} %get-tuple-element.23.mods.gate_a.gate_t.gain.shift), custom_call_target="tpu_custom_call" | custom-call | bytes 7380000 | tf_op jit(solution)/shard_map/first_inputs/pallas_call | solution.py:44
  38.1 10.4 %all-gather = bf16[12,192,128]{2,1,0:T(8,128)(2,1)} all-gather(bf16[3,192,128]{2,1,0:T(8,128)(2,1)} %get-tuple-element.24), channel_id=2, replica_groups=mesh['samp'=16,'row'=4,'col'=4] {'col'}, dimensions={0}, use_global_device_ids=true | all-gather | bytes 737280 | tf_op jit(solution)/shard_map/all_gather | solution.py:658
  48.4 0.9 copy-done.1
  49.3 2.2 %triangle_sums.1 = bf16[8,2,4,2,8,128]{5,4,3,2,1,0:T(8,128)(2,1)} custom-call(bf16[4,4,192,128]{3,2,1,0:T(8,128)(2,1)} %bitcast.36, bf16[4,3,192,128]{3,2,1,0:T(8,128)(2,1)} %bitcast.30), custom_call_target="tpu_custom_call" | custom-call | bytes 8118000 | tf_op jit(solution)/shard_map/triangle_sums/pallas_call | solution.py:44
  51.5 13.6 %all-to-all-start.1 = ((bf16[256,4,128]{2,1,0:T(4,128)(2,1)}), bf16[256,4,128]{2,1,0:T(4,128)(2,1)S(1)}, u32[]{:S(2)}, u32[]{:S(2)}) async-start(bf16[256,4,128]{2,1,0:T(4,128)(2,1)} %bitcast.52), calls=%async_computation.1 | async-start | bytes 524288 | tf_op jit(solution)/shard_map/all_to_all | solution.py:663
  65.2 1.7 constant_dynamic-slice_fusion.own
  66.8 1.2 convert_bitcast_fusion.refs_3_
  68.1 3.0 %project.1 = (bf16[3,192,128]{2,1,0:T(8,128)(2,1)}, bf16[3,192,128]{2,1,0:T(8,128)(2,1)}, bf16[1168,128]{1,0:T(8,128)(2,1)}) custom-call(bf16[4,3,192,128]{3,2,1,0:T(8,128)(2,1)} %bitcast.31, bf16[2,192,768]{2,1,0:T(8,128)(2,1)} %bitcast.45, bf16[2,192,768]{2,1,0:T(8,128)(2,1)} %bitcast.47, bf16[2,2,192,768]{3,2,1,0:T(8,128)(2,1)} %bitcast.32, ...), custom_call_target="tpu_custom_call" | custom-call | bytes 11070000 | tf_op jit(solution)/shard_map/project/pallas_call | solution.py:44
  71.1 10.0 %all-to-all-done.1 = bf16[256,4,128]{2,1,0:T(4,128)(2,1)S(1)} async-done(((bf16[256,4,128]{2,1,0:T(4,128)(2,1)}), bf16[256,4,128]{2,1,0:T(4,128)(2,1)S(1)}, u32[]{:S(2)}, u32[]{:S(2)}) %all-to-all-start.1) | async-done | bytes 262176 | tf_op jit(solution)/shard_map/all_to_all | solution.py:663
  81.1 0.7 copy-done.9
  81.8 2.7 %pair_update.1 = (bf16[128,8,128]{2,1,0:T(8,128)(2,1)}, bf16[4,4,2,4,8,128]{5,4,3,2,1,0:T(8,128)(2,1)}) custom-call(bf16[128,8,128]{2,1,0:T(8,128)(2,1)} %bitcast.51, bf16[128,8,128]{2,1,0:T(8,128)(2,1)} %constant_dynamic-slice_fusion.own, bf16[5,128,128]{2,1,0:T(8,128)(2,1)} %gate_w.1, bf16[128,128]{1,0:T(8,128)(2,1)} %out_w.1, bf16[32,128]{1,0:T(8,128)(2,1)} %bitcast.60, ...), custom_call_target="tpu_custom_call" | custom-call | bytes 10332000 | tf_op jit(solution)/shard_map/pair_update/pallas_call | solution.py:44
  84.5 3.8 %all-to-all-start.2 = ((bf16[16,2,4,8,128]{4,3,2,1,0:T(8,128)(2,1)}), bf16[16,2,4,8,128]{4,3,2,1,0:T(8,128)(2,1)S(1)}, u32[]{:S(2)}, u32[]{:S(2)}) async-start(bf16[16,2,4,8,128]{4,3,2,1,0:T(8,128)(2,1)} %bitcast.54), calls=%async_computation.2 | async-start | bytes 524288 | tf_op jit(solution)/shard_map/all_to_all | solution.py:684
  88.3 0.3 collective-permute-start.4
  88.7 12.8 %all-gather.2 = bf16[12,192,128]{2,1,0:T(8,128)(2,1)} all-gather(bf16[3,192,128]{2,1,0:T(8,128)(2,1)S(1)} %copy-done.12), channel_id=4, replica_groups=mesh['samp'=16,'row'=4,'col'=4] {'col'}, dimensions={0}, use_global_device_ids=true | all-gather | bytes 737280 | tf_op jit(solution)/shard_map/all_gather | solution.py:701
  101.5 3.9 %transition.2 = (f32[2,3,192,128]{3,2,1,0:T(8,128)}, bf16[2,3,192,128]{3,2,1,0:T(8,128)(2,1)}) custom-call(s32[1]{0:T(128)} %bitcast.20.me_ref, bf16[4,3,192,128]{3,2,1,0:T(8,128)(2,1)} %bitcast.38, bf16[2,2,768,384]{3,2,1,0:T(8,128)(2,1)} %up.3, bf16[2,384,768]{2,1,0:T(8,128)(2,1)} %down.3), custom_call_target="tpu_custom_call" | custom-call | bytes 14022000 | tf_op jit(solution)/shard_map/transition/pallas_call | solution.py:44
  105.5 0.3 collective-permute-start.3
  105.8 0.8 collective-permute-start.5
  106.6 2.0 collective-permute-start.6
  108.5 1.3 collective-permute-start.7
  109.8 2.3 %collective-permute-start.8 = (bf16[4,4,2,4,8,128]{5,4,3,2,1,0:T(8,128)(2,1)S(1)}, bf16[4,4,2,4,8,128]{5,4,3,2,1,0:T(8,128)(2,1)}, u32[]{:S(2)}, u32[]{:S(2)}) collective-permute-start(bf16[4,4,2,4,8,128]{5,4,3,2,1,0:T(8,128)(2,1)S(1)} %bitcast.41), channel_id=1, source_target_pairs={{0,48},{16,32},{32,16},{48,0},{64,112},{80,96},{96,80},{112,64},{1... | collective-permute-start | bytes 786440 | tf_op jit(solution)/shard_map/ppermute | solution.py:696
  112.1 1.7 join.4
  113.9 0.6 copy-done.3
  114.5 6.2 %all-to-all-start.3 = ((bf16[16,8,8,128]{3,2,1,0:T(8,128)(2,1)}), bf16[16,8,8,128]{3,2,1,0:T(8,128)(2,1)S(1)}, u32[]{:S(2)}, u32[]{:S(2)}) async-start(bf16[16,8,8,128]{3,2,1,0:T(8,128)(2,1)} %bitcast.50), calls=%async_computation.3 | async-start | bytes 524288 | tf_op jit(solution)/shard_map/all_to_all | solution.py:700
  120.7 0.6 pad_add_fusion.me_ref
  121.3 1.7 collective-permute-done.6.kv3
  123.0 1.1 collective-permute-done.8.bias3
  124.1 5.6 %attention.2 = (f32[2,3,192,128]{3,2,1,0:T(8,128)}, bf16[2,3,192,128]{3,2,1,0:T(8,128)(2,1)}) custom-call(s32[3]{0:T(128)} %pad_add_fusion.me_ref, bf16[3,192,128]{2,1,0:T(8,128)(2,1)} %get-tuple-element.29.queries, bf16[3,192,128]{2,1,0:T(8,128)(2,1)} %get-tuple-element.30.gates, bf16[1168,128]{1,0:T(8,128)(2,1)} %get-tuple-element.25.refs_0_.kv0, ...), custom_call_target="tpu_custom_call" | custom-call | bytes 19926000 | tf_op jit(solution)/shard_map/attention/pallas_call | solution.py:44
  129.7 1.0 collective-permute-start.11
  130.7 1.4 collective-permute-done.11.came.came_a
  132.1 0.7 copy-done.8
  132.8 1.7 join.5
  134.6 5.2 %collective-permute-done.12.far_a = bf16[3,192,128]{2,1,0:T(8,128)(2,1)S(1)} collective-permute-done((bf16[3,192,128]{2,1,0:T(8,128)(2,1)}, bf16[3,192,128]{2,1,0:T(8,128)(2,1)S(1)}, u32[]{:S(2)}, u32[]{:S(2)}) %collective-permute-start.12) | collective-permute-done | bytes 147488 | tf_op jit(solution)/shard_map/ppermute | solution.py:32
  139.8 0.7 copy-done.15
  140.4 0.7 copy-done.2
  141.1 2.3 %finish.2 = bf16[3,192,128]{2,1,0:T(8,128)(2,1)} custom-call(f32[2,3,192,128]{3,2,1,0:T(8,128)} %get-tuple-element.34.keep.keep_a, bf16[2,3,192,128]{3,2,1,0:T(8,128)(2,1)} %copy-done.8, bf16[3,192,128]{2,1,0:T(8,128)(2,1)} %copy-done.15, f32[2,3,192,128]{3,2,1,0:T(8,128)} %get-tuple-element.32.keep.keep_t, bf16[2,3,192,128]{3,2,1,0:T(8,128)(2,1)} %copy-done.5, ...), custom_call_target="tpu_custom_call" | custom-call | bytes 7380000 | tf_op jit(solution)/shard_map/finish/pallas_call | solution.py:44
  143.4 9.1 %all-gather.3 = bf16[12,192,128]{2,1,0:T(8,128)(2,1)} all-gather(bf16[3,192,128]{2,1,0:T(8,128)(2,1)} %finish.2), channel_id=5, replica_groups=mesh['samp'=16,'row'=4,'col'=4] {'col'}, dimensions={0}, use_global_device_ids=true | all-gather | bytes 737280 | tf_op jit(solution)/shard_map/all_gather | solution.py:722
  152.5 4.0 %normed_project.1 = (bf16[3,192,128]{2,1,0:T(8,128)(2,1)}, bf16[3,192,128]{2,1,0:T(8,128)(2,1)}, bf16[1168,128]{1,0:T(8,128)(2,1)}, bf16[3,192,128]{2,1,0:T(8,128)(2,1)}) custom-call(s32[1]{0:T(128)} %bitcast.20.me_ref, bf16[4,3,192,128]{3,2,1,0:T(8,128)(2,1)} %bitcast.44, bf16[4,2,3,192,128]{4,3,2,1,0:T(8,128)(2,1)} %bitcast.35, ...), custom_call_target="tpu_custom_call" | custom-call | bytes 14760000 | tf_op jit(solution)/shard_map/normed_project/pallas_call | solution.py:44
  156.6 2.3 %collective-permute-start.14 = (bf16[1168,128]{1,0:T(8,128)(2,1)}, bf16[1168,128]{1,0:T(8,128)(2,1)}, u32[]{:S(2)}, u32[]{:S(2)}) collective-permute-start(bf16[1168,128]{1,0:T(8,128)(2,1)} %get-tuple-element.38.kv0), channel_id=1, source_target_pairs={{0,8},{4,12},{8,0},{12,4},{1,9},{5,13},{9,1},{13,5},{2,10},{6,14},... | collective-permute-start | bytes 897032 | tf_op jit(solution)/shard_map/ppermute | solution.py:32
  158.9 1.4 collective-permute-start.15
  160.4 10.4 %all-gather.4 = bf16[12,192,128]{2,1,0:T(8,128)(2,1)} all-gather(bf16[3,192,128]{2,1,0:T(8,128)(2,1)} %get-tuple-element.39), channel_id=6, replica_groups=mesh['samp'=16,'row'=4,'col'=4] {'col'}, dimensions={0}, use_global_device_ids=true | all-gather | bytes 737280 | tf_op jit(solution)/shard_map/all_gather | solution.py:712
  170.7 3.9 %transition.3 = (f32[2,3,192,128]{3,2,1,0:T(8,128)}, bf16[2,3,192,128]{3,2,1,0:T(8,128)(2,1)}) custom-call(s32[1]{0:T(128)} %bitcast.20.me_ref, bf16[4,3,192,128]{3,2,1,0:T(8,128)(2,1)} %bitcast.37, bf16[2,2,768,384]{3,2,1,0:T(8,128)(2,1)} %up.3, bf16[2,384,768]{2,1,0:T(8,128)(2,1)} %down.3), custom_call_target="tpu_custom_call" | custom-call | bytes 14022000 | tf_op jit(solution)/shard_map/transition/pallas_call | solution.py:44
  174.8 0.7 copy-done.11
  175.5 5.5 %attention.3 = (f32[2,3,192,128]{3,2,1,0:T(8,128)}, bf16[2,3,192,128]{3,2,1,0:T(8,128)(2,1)}) custom-call(s32[3]{0:T(128)} %pad_add_fusion.me_ref, bf16[3,192,128]{2,1,0:T(8,128)(2,1)} %get-tuple-element.36.queries, bf16[3,192,128]{2,1,0:T(8,128)(2,1)} %get-tuple-element.37.gates, bf16[1168,128]{1,0:T(8,128)(2,1)} %get-tuple-element.38.kv0, ...), custom_call_target="tpu_custom_call" | custom-call | bytes 19926000 | tf_op jit(solution)/shard_map/attention/pallas_call | solution.py:44
  181.0 0.9 collective-permute-start.16
  181.9 0.7 copy-done.6
  182.6 1.7 join.7
  184.3 1.4 collective-permute-start.19
  185.7 0.7 copy-done.7
  186.4 1.7 join.6
  188.2 1.7 pair_rows.1
  190.0 3.4 %collective-permute-done.17.far_a = bf16[3,192,128]{2,1,0:T(8,128)(2,1)S(1)} collective-permute-done((bf16[3,192,128]{2,1,0:T(8,128)(2,1)}, bf16[3,192,128]{2,1,0:T(8,128)(2,1)S(1)}, u32[]{:S(2)}, u32[]{:S(2)}) %collective-permute-start.17) | collective-permute-done | bytes 147488 | tf_op jit(solution)/shard_map/ppermute | solution.py:32
  193.5 0.7 copy-done.14
  194.1 2.2 %finish.3 = bf16[3,192,128]{2,1,0:T(8,128)(2,1)} custom-call(f32[2,3,192,128]{3,2,1,0:T(8,128)} %get-tuple-element.41.keep.keep_a, bf16[2,3,192,128]{3,2,1,0:T(8,128)(2,1)} %copy-done.7, bf16[3,192,128]{2,1,0:T(8,128)(2,1)} %copy-done.14, f32[2,3,192,128]{3,2,1,0:T(8,128)} %get-tuple-element.40.refs_1_.keep.keep_t, bf16[2,3,192,128]{3,2,1,0:T(8,128)(2,1)} %copy-done.6, ...), custom_call_target="tpu_custom_call" | custom-call | bytes 7380000 | tf_op jit(solution)/shard_map/finish/pallas_call | solution.py:44
  (52 shorter events, 1.0 us)
Async XLA Ops:
  7.2 22.5 %copy-start = (bf16[256,384]{1,0:T(8,128)(2,1)S(1)}, bf16[256,384]{1,0:T(8,128)(2,1)}, u32[]{:S(2)}) copy-start(bf16[256,384]{1,0:T(8,128)(2,1)} %param.24) | copy-start | bytes 589828
  8.2 6.4 %collective-permute-start = (f32[2,3,128]{2,1,0:T(4,128)S(1)}, f32[2,3,128]{2,1,0:T(4,128)S(1)}, u32[]{:S(2)}, u32[]{:S(2)}) collective-permute-start(f32[2,3,128]{2,1,0:T(4,128)S(1)} %pad_maximum_fusion), channel_id=1, source_target_pairs={{0,1},{1,0},{2,3},{3,2},{4,5},{5,4},{6,7},{7,6},{8,9},{9,8},{10,11... | collective-permute-start | bytes 9224 | tf_op jit(solution)/shard_map/ppermute | solution.py:32
  11.5 3.1 %collective-permute-start.1 = (f32[2,3,128]{2,1,0:T(4,128)S(1)}, f32[2,3,128]{2,1,0:T(4,128)S(1)}, u32[]{:S(2)}, u32[]{:S(2)}) collective-permute-start(f32[2,3,128]{2,1,0:T(4,128)S(1)} %pad_maximum_fusion), channel_id=1, source_target_pairs={{0,2},{1,3},{2,0},{3,1},{4,6},{5,7},{6,4},{7,5},{8,10},{9,11},{10,... | collective-permute-start | bytes 9224 | tf_op jit(solution)/shard_map/ppermute | solution.py:32
  11.5 3.3 %collective-permute-start.2 = (f32[2,3,128]{2,1,0:T(4,128)S(1)}, f32[2,3,128]{2,1,0:T(4,128)S(1)}, u32[]{:S(2)}, u32[]{:S(2)}) collective-permute-start(f32[2,3,128]{2,1,0:T(4,128)S(1)} %pad_maximum_fusion), channel_id=1, source_target_pairs={{0,3},{1,2},{2,1},{3,0},{4,7},{5,6},{6,5},{7,4},{8,11},{9,10},{10,... | collective-permute-start | bytes 9224 | tf_op jit(solution)/shard_map/ppermute | solution.py:32
  25.1 23.3 %all-to-all-start = ((bf16[16,192,128]{2,1,0:T(8,128)(2,1)}), bf16[16,192,128]{2,1,0:T(8,128)(2,1)S(1)}, u32[]{:S(2)}, u32[]{:S(2)}) async-start(bf16[16,192,128]{2,1,0:T(8,128)(2,1)} %pair_project.1.refs_0_), calls=%async_computation | async-start | bytes 1572864 | tf_op jit(solution)/shard_map/all_to_all | solution.py:653
  29.6 41.5 %all-gather.7.cloned.1.call-start = ((), (), s32[]{:S(2)}) async-start(), calls=%async_computation.4 | async-start | bytes 1474560 | tf_op jit(solution)/shard_map/all_gather | solution.py:661
  48.4 0.9 copy-start.1
  51.5 29.5 %all-to-all-start.1 = ((bf16[256,4,128]{2,1,0:T(4,128)(2,1)}), bf16[256,4,128]{2,1,0:T(4,128)(2,1)S(1)}, u32[]{:S(2)}, u32[]{:S(2)}) async-start(bf16[256,4,128]{2,1,0:T(4,128)(2,1)} %bitcast.52), calls=%async_computation.1 | async-start | bytes 524288 | tf_op jit(solution)/shard_map/all_to_all | solution.py:663
  68.1 20.6 %copy-start.12 = (bf16[3,192,128]{2,1,0:T(8,128)(2,1)S(1)}, bf16[3,192,128]{2,1,0:T(8,128)(2,1)}, u32[]{:S(2)}) copy-start(bf16[3,192,128]{2,1,0:T(8,128)(2,1)} %get-tuple-element.31) | copy-start | bytes 442372
  81.1 0.7 copy-start.9
  84.5 21.0 %all-to-all-start.2 = ((bf16[16,2,4,8,128]{4,3,2,1,0:T(8,128)(2,1)}), bf16[16,2,4,8,128]{4,3,2,1,0:T(8,128)(2,1)S(1)}, u32[]{:S(2)}, u32[]{:S(2)}) async-start(bf16[16,2,4,8,128]{4,3,2,1,0:T(8,128)(2,1)} %bitcast.54), calls=%async_computation.2 | async-start | bytes 524288 | tf_op jit(solution)/shard_map/all_to_all | solution.py:684
  88.3 21.5 %collective-permute-start.4 = (bf16[1168,128]{1,0:T(8,128)(2,1)}, bf16[1168,128]{1,0:T(8,128)(2,1)}, u32[]{:S(2)}, u32[]{:S(2)}) collective-permute-start(bf16[1168,128]{1,0:T(8,128)(2,1)} %get-tuple-element.25.refs_0_.kv0), channel_id=1, source_target_pairs={{0,4},{4,0},{8,12},{12,8},{1,5},{5,1},{9,13},{13,9},{2,6},{6,2},{1... | collective-permute-start | bytes 897032 | tf_op jit(solution)/shard_map/ppermute | solution.py:32
  105.3 3.2 %collective-permute-start.9 = (bf16[2,3,192,128]{3,2,1,0:T(8,128)(2,1)}, bf16[2,3,192,128]{3,2,1,0:T(8,128)(2,1)S(1)}, u32[]{:S(2)}, u32[]{:S(2)}) collective-permute-start(bf16[2,3,192,128]{3,2,1,0:T(8,128)(2,1)} %get-tuple-element.33), channel_id=1, source_target_pairs={{0,1},{1,0},{2,3},{3,2},{4,5},{5,4},{6,7},{7,6},{8,9},{9,8},{10,11... | collective-permute-start | bytes 884744 | tf_op jit(solution)/shard_map/ppermute | solution.py:32
  105.5 18.6 %copy-start.4 = (bf16[16,2,4,8,128]{4,3,2,1,0:T(8,128)(2,1)}, bf16[16,2,4,8,128]{4,3,2,1,0:T(8,128)(2,1)S(1)}, u32[]{:S(2)}) copy-start(bf16[16,2,4,8,128]{4,3,2,1,0:T(8,128)(2,1)S(1)} %all-to-all-done.2) | copy-start | bytes 786436
  105.5 8.3 %collective-permute-start.3 = (bf16[4,4,2,4,8,128]{5,4,3,2,1,0:T(8,128)(2,1)S(1)}, bf16[4,4,2,4,8,128]{5,4,3,2,1,0:T(8,128)(2,1)S(1)}, u32[]{:S(2)}, u32[]{:S(2)}) collective-permute-start(bf16[4,4,2,4,8,128]{5,4,3,2,1,0:T(8,128)(2,1)S(1)} %bitcast.39), channel_id=1, source_target_pairs={{0,16},{16,0},{32,48},{48,32},{64,80},{80,64},{96,112},{112,96},{1... | collective-permute-start | bytes 786440 | tf_op jit(solution)/shard_map/ppermute | solution.py:696
  105.8 15.5 %collective-permute-start.5 = (bf16[1168,128]{1,0:T(8,128)(2,1)}, bf16[1168,128]{1,0:T(8,128)(2,1)}, u32[]{:S(2)}, u32[]{:S(2)}) collective-permute-start(bf16[1168,128]{1,0:T(8,128)(2,1)} %get-tuple-element.25.refs_0_.kv0), channel_id=1, source_target_pairs={{0,8},{4,12},{8,0},{12,4},{1,9},{5,13},{9,1},{13,5},{2,10},{6,14},... | collective-permute-start | bytes 897032 | tf_op jit(solution)/shard_map/ppermute | solution.py:32
  106.6 16.5 %collective-permute-start.6 = (bf16[1168,128]{1,0:T(8,128)(2,1)}, bf16[1168,128]{1,0:T(8,128)(2,1)}, u32[]{:S(2)}, u32[]{:S(2)}) collective-permute-start(bf16[1168,128]{1,0:T(8,128)(2,1)} %get-tuple-element.25.refs_0_.kv0), channel_id=1, source_target_pairs={{0,12},{4,8},{8,4},{12,0},{1,13},{5,9},{9,5},{13,1},{2,14},{6,10},... | collective-permute-start | bytes 897032 | tf_op jit(solution)/shard_map/ppermute | solution.py:32
  108.5 1.3 copy-start.5
  108.5 14.5 %collective-permute-start.7 = (bf16[4,4,2,4,8,128]{5,4,3,2,1,0:T(8,128)(2,1)S(1)}, bf16[4,4,2,4,8,128]{5,4,3,2,1,0:T(8,128)(2,1)}, u32[]{:S(2)}, u32[]{:S(2)}) collective-permute-start(bf16[4,4,2,4,8,128]{5,4,3,2,1,0:T(8,128)(2,1)S(1)} %bitcast.40), channel_id=1, source_target_pairs={{0,32},{16,48},{32,0},{48,16},{64,96},{80,112},{96,64},{112,80},{1... | collective-permute-start | bytes 786440 | tf_op jit(solution)/shard_map/ppermute | solution.py:696
  109.8 14.3 %collective-permute-start.8 = (bf16[4,4,2,4,8,128]{5,4,3,2,1,0:T(8,128)(2,1)S(1)}, bf16[4,4,2,4,8,128]{5,4,3,2,1,0:T(8,128)(2,1)}, u32[]{:S(2)}, u32[]{:S(2)}) collective-permute-start(bf16[4,4,2,4,8,128]{5,4,3,2,1,0:T(8,128)(2,1)S(1)} %bitcast.41), channel_id=1, source_target_pairs={{0,48},{16,32},{32,16},{48,0},{64,112},{80,96},{96,80},{112,64},{1... | collective-permute-start | bytes 786440 | tf_op jit(solution)/shard_map/ppermute | solution.py:696
  113.8 0.7 copy-start.3
  113.8 9.2 %collective-permute-start.10 = (bf16[3,192,128]{2,1,0:T(8,128)(2,1)}, bf16[3,192,128]{2,1,0:T(8,128)(2,1)S(1)}, u32[]{:S(2)}, u32[]{:S(2)}) collective-permute-start(bf16[3,192,128]{2,1,0:T(8,128)(2,1)} %join.4), channel_id=1, source_target_pairs={{0,2},{1,3},{2,0},{3,1},{4,6},{5,7},{6,4},{7,5},{8,10},{9,11},{10,... | collective-permute-start | bytes 442376 | tf_op jit(solution)/shard_map/ppermute | solution.py:32
  114.5 25.3 %all-to-all-start.3 = ((bf16[16,8,8,128]{3,2,1,0:T(8,128)(2,1)}), bf16[16,8,8,128]{3,2,1,0:T(8,128)(2,1)S(1)}, u32[]{:S(2)}, u32[]{:S(2)}) async-start(bf16[16,8,8,128]{3,2,1,0:T(8,128)(2,1)} %bitcast.50), calls=%async_computation.3 | async-start | bytes 524288 | tf_op jit(solution)/shard_map/all_to_all | solution.py:700
  123.0 1.1 copy-start.10
  129.7 2.4 %collective-permute-start.11 = (bf16[2,3,192,128]{3,2,1,0:T(8,128)(2,1)}, bf16[2,3,192,128]{3,2,1,0:T(8,128)(2,1)S(1)}, u32[]{:S(2)}, u32[]{:S(2)}) collective-permute-start(bf16[2,3,192,128]{3,2,1,0:T(8,128)(2,1)} %get-tuple-element.35), channel_id=1, source_target_pairs={{0,1},{1,0},{2,3},{3,2},{4,5},{5,4},{6,7},{7,6},{8,9},{9,8},{10,11... | collective-permute-start | bytes 884744 | tf_op jit(solution)/shard_map/ppermute | solution.py:32
  132.1 0.7 copy-start.8
  134.5 5.3 %collective-permute-start.12 = (bf16[3,192,128]{2,1,0:T(8,128)(2,1)}, bf16[3,192,128]{2,1,0:T(8,128)(2,1)S(1)}, u32[]{:S(2)}, u32[]{:S(2)}) collective-permute-start(bf16[3,192,128]{2,1,0:T(8,128)(2,1)} %join.5), channel_id=1, source_target_pairs={{0,2},{1,3},{2,0},{3,1},{4,6},{5,7},{6,4},{7,5},{8,10},{9,11},{10,... | collective-permute-start | bytes 442376 | tf_op jit(solution)/shard_map/ppermute | solution.py:32
  139.8 0.7 copy-start.15
  140.4 0.7 copy-start.2
  156.5 18.2 %collective-permute-start.13 = (bf16[1168,128]{1,0:T(8,128)(2,1)}, bf16[1168,128]{1,0:T(8,128)(2,1)S(1)}, u32[]{:S(2)}, u32[]{:S(2)}) collective-permute-start(bf16[1168,128]{1,0:T(8,128)(2,1)} %get-tuple-element.38.kv0), channel_id=1, source_target_pairs={{0,4},{4,0},{8,12},{12,8},{1,5},{5,1},{9,13},{13,9},{2,6},{6,2},{1... | collective-permute-start | bytes 897032 | tf_op jit(solution)/shard_map/ppermute | solution.py:32
  156.6 18.1 %collective-permute-start.14 = (bf16[1168,128]{1,0:T(8,128)(2,1)}, bf16[1168,128]{1,0:T(8,128)(2,1)}, u32[]{:S(2)}, u32[]{:S(2)}) collective-permute-start(bf16[1168,128]{1,0:T(8,128)(2,1)} %get-tuple-element.38.kv0), channel_id=1, source_target_pairs={{0,8},{4,12},{8,0},{12,4},{1,9},{5,13},{9,1},{13,5},{2,10},{6,14},... | collective-permute-start | bytes 897032 | tf_op jit(solution)/shard_map/ppermute | solution.py:32
  158.9 15.8 %collective-permute-start.15 = (bf16[1168,128]{1,0:T(8,128)(2,1)}, bf16[1168,128]{1,0:T(8,128)(2,1)}, u32[]{:S(2)}, u32[]{:S(2)}) collective-permute-start(bf16[1168,128]{1,0:T(8,128)(2,1)} %get-tuple-element.38.kv0), channel_id=1, source_target_pairs={{0,12},{4,8},{8,4},{12,0},{1,13},{5,9},{9,5},{13,1},{2,14},{6,10},... | collective-permute-start | bytes 897032 | tf_op jit(solution)/shard_map/ppermute | solution.py:32
  174.6 7.3 %collective-permute-start.18 = (bf16[2,3,192,128]{3,2,1,0:T(8,128)(2,1)}, bf16[2,3,192,128]{3,2,1,0:T(8,128)(2,1)S(1)}, u32[]{:S(2)}, u32[]{:S(2)}) collective-permute-start(bf16[2,3,192,128]{3,2,1,0:T(8,128)(2,1)} %get-tuple-element.43), channel_id=1, source_target_pairs={{0,1},{1,0},{2,3},{3,2},{4,5},{5,4},{6,7},{7,6},{8,9},{9,8},{10,11... | collective-permute-start | bytes 884744 | tf_op jit(solution)/shard_map/ppermute | solution.py:32
  174.7 0.7 copy-start.11
  181.0 4.7 %collective-permute-start.16 = (bf16[2,3,192,128]{3,2,1,0:T(8,128)(2,1)}, bf16[2,3,192,128]{3,2,1,0:T(8,128)(2,1)S(1)}, u32[]{:S(2)}, u32[]{:S(2)}) collective-permute-start(bf16[2,3,192,128]{3,2,1,0:T(8,128)(2,1)} %get-tuple-element.42), channel_id=1, source_target_pairs={{0,1},{1,0},{2,3},{3,2},{4,5},{5,4},{6,7},{7,6},{8,9},{9,8},{10,11... | collective-permute-start | bytes 884744 | tf_op jit(solution)/shard_map/ppermute | solution.py:32
  181.9 0.7 copy-start.6
  184.3 5.7 %collective-permute-start.19 = (bf16[3,192,128]{2,1,0:T(8,128)(2,1)}, bf16[3,192,128]{2,1,0:T(8,128)(2,1)S(1)}, u32[]{:S(2)}, u32[]{:S(2)}) collective-permute-start(bf16[3,192,128]{2,1,0:T(8,128)(2,1)} %join.7), channel_id=1, source_target_pairs={{0,2},{1,3},{2,0},{3,1},{4,6},{5,7},{6,4},{7,5},{8,10},{9,11},{10,... | collective-permute-start | bytes 442376 | tf_op jit(solution)/shard_map/ppermute | solution.py:32
  185.7 0.7 copy-start.7
  188.1 5.4 %collective-permute-start.17 = (bf16[3,192,128]{2,1,0:T(8,128)(2,1)}, bf16[3,192,128]{2,1,0:T(8,128)(2,1)S(1)}, u32[]{:S(2)}, u32[]{:S(2)}) collective-permute-start(bf16[3,192,128]{2,1,0:T(8,128)(2,1)} %join.6), channel_id=1, source_target_pairs={{0,2},{1,3},{2,0},{3,1},{4,6},{5,7},{6,4},{7,5},{8,10},{9,11},{10,... | collective-permute-start | bytes 442376 | tf_op jit(solution)/shard_map/ppermute | solution.py:32
  190.0 3.4 %copy-start.13 = (bf16[3,192,128]{2,1,0:T(8,128)(2,1)}, bf16[3,192,128]{2,1,0:T(8,128)(2,1)S(1)}, u32[]{:S(2)}) copy-start(bf16[3,192,128]{2,1,0:T(8,128)(2,1)S(1)} %collective-permute-done.19.far_t) | copy-start | bytes 442372
  193.4 0.7 copy-start.14
Sparse Core Ops, SparseCore 0:
  36.0 26.7 all-gather.6

commit v2 on v1

--- a/solution.py
+++ b/solution.py
@@ -85,22 +85,35 @@
             full[k * width : (k + 1) * width, s * tokens : (s + 1) * tokens] = gathered[k, s]
 
 
-def stack_normed(gathered, shared, full, normed):
+def stack_normed(me, gathered, shared, own, full, normed, trans):
     parts, samples, width, tokens = gathered.shape
     for s in range(samples):
         at = slice(s * tokens, (s + 1) * tokens)
         value = jnp.concatenate([gathered[k, s] for k in range(parts)], 0).astype(jnp.float32)
-        value = channel_norm(value, 0)
-        normed[:, at] = value
-        for k in range(parts):
-            gain, shift = shared[k, 0, s], shared[k, 1, s]
-            full[k * width : (k + 1) * width, at] = (
-                gain.astype(jnp.float32) * value[k * width : (k + 1) * width]
-                + shift.astype(jnp.float32)
-            ).astype(jnp.bfloat16)
-
-
-def project_full(full, query_w, key_w, value_gate_w, mask, queries, gates, both):
+        normed[...] = channel_norm(value, 0)
+        for k, pair in enumerate(shared):
+            rows = pl.ds(pl.multiple_of((me ^ k) * width, width), width)
+            value = normed[rows, :]
+            gain, shift = pair[0, s].astype(jnp.float32), pair[1, s].astype(jnp.float32)
+            full[rows, at] = (gain * value + shift).astype(jnp.bfloat16)
+            if k == 0:
+                gain, shift = own[0, s].astype(jnp.float32), own[1, s].astype(jnp.float32)
+                trans[s] = (gain * value + shift).astype(jnp.bfloat16)
+
+
+def first_project_kernel(me_ref, block0, block1, block2, block3, *refs):
+    stack_features((block0, block1, block2, block3), refs[-1], me_ref[0])
+    project_full(*refs)
+
+
+def later_project_kernel(me_ref, gathered, pair0, pair1, pair2, pair3, own, *refs):
+    *rest, trans, full, normed = refs
+    shared = (pair0, pair1, pair2, pair3)
+    stack_normed(me_ref[0], gathered, shared, own, full, normed, trans)
+    project_full(*rest, full)
+
+
+def project_full(query_w, key_w, value_gate_w, mask, queries, gates, both, full):
     samples, width, tokens = queries.shape
 
     def times(weight):
@@ -114,34 +127,15 @@
         gates[s] = gate[:, at]
         both[2 * s * width : (2 * s + 1) * width] = key[:, at]
         both[(2 * s + 1) * width : (2 * s + 2) * width] = value[:, at]
-    both[2 * samples * width :] = jnp.broadcast_to(mask[...], (MASK_ROWS, tokens))
-
-
-def project_kernel(gathered, *refs):
-    stack_gathered(gathered, refs[-1])
-    project_full(refs[-1], *refs[:-1])
-
-
-def normed_project_kernel(me_ref, gathered, shared, gain, shift, *refs):
-    query_w, key_w, value_gate_w, mask, queries, gates, both, trans, full, normed = refs
-    stack_normed(gathered, shared, full, normed)
-    samples, width, tokens = trans.shape
-    start = pl.multiple_of(me_ref[0] * width, width)
-    for s in range(samples):
-        piece = normed[pl.ds(start, width), s * tokens : (s + 1) * tokens]
-        trans[s] = (gain[0, s] * piece + shift[0, s]).astype(jnp.bfloat16)
-    project_full(full, query_w, key_w, value_gate_w, mask, queries, gates, both)
-
-
-def mod_block(mods, m):
-    return pl.BlockSpec((1,) + mods.shape[1:], lambda i: (m, 0, 0, 0))
-
-
-def project(blocks, query_w, key_w, value_gate_w, mask, layer, me=None, shared=None, mods=None):
+    both[2 * samples * width :] = jnp.broadcast_to(
+        mask[...].astype(jnp.float32), (MASK_ROWS, tokens)
+    ).astype(jnp.bfloat16)
+
+
+def project(blocks, me, query_w, key_w, value_gate_w, mask, layer, shared=None, own=None):
     samples, width, tokens = blocks[0].shape[-3:]
     small = jax.ShapeDtypeStruct((samples, width, tokens), jnp.bfloat16)
     joint = jax.ShapeDtypeStruct((2 * samples * width + MASK_ROWS, tokens), jnp.bfloat16)
-    depth = query_w.shape[2]
     specs = [
         layer_block(query_w.shape, 0, layer),
         layer_block(key_w.shape, 0, layer),
@@ -149,27 +143,31 @@
         whole(mask.shape),
     ]
     args = [query_w, key_w, value_gate_w, mask]
+    depth = query_w.shape[2]
     full = pltpu.VMEM((depth, samples * tokens), jnp.bfloat16)
     if shared is None:
         return local_call(
-            project_kernel,
+            first_project_kernel,
             (small, small, joint),
-            [whole(blocks[0].shape)] + specs,
-            [*blocks, *args],
+            [SCALAR] + [whole(b.shape) for b in blocks] + specs,
+            [me, *blocks, *args],
             [full],
             3.0,
-            "project",
+            "first_project",
         )
-    specs = [whole(blocks[0].shape), whole(shared.shape), mod_block(mods, 6), mod_block(mods, 7)] + specs
     return local_call(
-        normed_project_kernel,
+        later_project_kernel,
         (small, small, joint, small),
-        [SCALAR] + specs,
-        [me, *blocks, shared, mods, mods, *args],
-        [full, pltpu.VMEM((depth, samples * tokens), jnp.float32)],
+        [SCALAR] + [whole(a.shape) for a in (*blocks, *shared, own)] + specs,
+        [me, *blocks, *shared, own, *args],
+        [full, pltpu.VMEM((depth, tokens), jnp.float32)],
         4.0,
-        "normed_project",
-    )
+        "later_project",
+    )
+
+
+def mod_block(mods, m):
+    return pl.BlockSpec((1,) + mods.shape[1:], lambda i: (m, 0, 0, 0))
 
 
 def hand_out(total, me, keep, give):
@@ -197,11 +195,23 @@
         1.0,
         "join",
     )
-    return [keep, came, swap(far, "col", 2)]
-
-
-def transition_kernel(me_ref, gathered, up, down, keep, give, full, total):
-    stack_gathered(gathered, full)
+    return [keep, came, swap(far, "col", 2)], far
+
+
+def stack_features(blocks, full, me):
+    for k, block in enumerate(blocks):
+        samples, width, tokens = block.shape
+        start = pl.multiple_of((me ^ k) * width, width)
+        for s in range(samples):
+            full[pl.ds(start, width), s * tokens : (s + 1) * tokens] = block[s]
+
+
+def transition_kernel(count, me_ref, *refs):
+    up, down, keep, give, full, total = refs[count:]
+    if count > 1:
+        stack_features(refs[:count], full, me_ref[0])
+    else:
+        stack_gathered(refs[0], full)
     over_rows = (((0,), (0,)), ((), ()))
     swish = lax.dot_general(up[0, 0], full[...], over_rows, preferred_element_type=jnp.float32)
     linear = lax.dot_general(up[0, 1], full[...], over_rows, preferred_element_type=jnp.float32)
@@ -210,18 +220,19 @@
     hand_out(total, me_ref[0], keep, give)
 
 
-def transition(gathered, me, up, down, layer, col_size):
-    samples, width, tokens = gathered.shape[1:]
+def transition(blocks, me, up, down, layer, col_size):
+    samples, width, tokens = blocks[0].shape[-3:]
     depth, hidden = up.shape[2:]
     return local_call(
-        transition_kernel,
+        lambda *refs: transition_kernel(len(blocks), *refs),
         tuple(
             jax.ShapeDtypeStruct((col_size // 2, samples, width, tokens), dtype)
             for dtype in (jnp.float32, jnp.bfloat16)
         ),
-        [SCALAR, whole(gathered.shape)]
+        [SCALAR]
+        + [whole(b.shape) for b in blocks]
         + [layer_block(up.shape, 0, layer), layer_block(down.shape, 0, layer)],
-        [me, gathered, up, down],
+        [me, *blocks, up, down],
         [
             pltpu.VMEM((depth, samples * tokens), jnp.bfloat16),
             pltpu.VMEM((depth, samples * tokens), jnp.float32),
@@ -314,7 +325,8 @@
             keep[0, s] + came[0, s].astype(jnp.float32) + far[s].astype(jnp.float32)
             for keep, came, far in ((keep_a, came_a, far_a), (keep_t, came_t, far_t))
         )
-        state[s] = (gate_a[0, s] * branch + gate_t[0, s] * trans).astype(state.dtype)
+        value = gate_a[0, s].astype(jnp.float32) * branch + gate_t[0, s].astype(jnp.float32) * trans
+        state[s] = value.astype(state.dtype)
 
 
 def finish(attended, trans, mods, gate_at, others):
@@ -333,73 +345,57 @@
     )
 
 
-def modulate_kernel(single, shift, mod_w, *refs):
-    own, shared, normed = refs[-3:]
-    samples, width, tokens = own.shape[1:]
+def modulate_kernel(single, time_embed, time_w, mod_w, state, sums, *refs):
+    attn, trans, gates, later, shared, normed = refs[-6:]
+    samples, width, tokens = state.shape
     layers, count = mod_w.shape[:2]
+    shift = jnp.dot(time_embed[...], time_w[...], preferred_element_type=jnp.float32)
     for s in range(samples):
         condition = single[...].astype(jnp.float32) + shift[s : s + 1, :]
         normed[s * tokens : (s + 1) * tokens] = channel_norm(condition, 1).astype(jnp.bfloat16)
-    kept = 0
+
+    def made(layer, m):
+        value = lax.dot_general(
+            mod_w[layer, m],
+            normed[...],
+            (((1,), (1,)), ((), ())),
+            preferred_element_type=jnp.float32,
+        )
+        value = value if m in (1, 3) else jax.nn.sigmoid(value)
+        return [value[:, s * tokens : (s + 1) * tokens] for s in range(samples)]
+
+    mean_value = sums[0] / DA
+    scale = lax.rsqrt(sums[1] / DA - mean_value * mean_value + EPS)
+    for target, m in ((attn, 0), (trans, 2)):
+        gain, shift = made(0, m), made(0, m + 1)
+        for s in range(samples):
+            value = (state[s].astype(jnp.float32) - mean_value[s : s + 1]) * scale[s : s + 1]
+            target[s] = (gain[s] * value + shift[s]).astype(jnp.bfloat16)
     for layer in range(layers):
-        for m in range(count):
-            made = lax.dot_general(
-                mod_w[layer, m],
-                normed[...],
-                (((1,), (1,)), ((), ())),
-                preferred_element_type=jnp.float32,
-            )
-            if m not in (1, 3):
-                made = jax.nn.sigmoid(made)
-            for s in range(samples):
-                piece = made[:, s * tokens : (s + 1) * tokens]
-                if layer > 0 and m < 2:
-                    shared[m, s] = piece.astype(jnp.bfloat16)
-                else:
-                    own[kept, s] = piece
-            kept += layer == 0 or m >= 2
-
-
-def modulate(single, shift, mod_w, others):
-    layers, count, width, depth = mod_w.shape
-    tokens, samples = single.shape[0], shift.shape[0]
+        for m in range(4, count):
+            for s, value in enumerate(made(layer, m)):
+                gates[layer * (count - 4) + m - 4, s] = value.astype(jnp.bfloat16)
+    for m in range(4):
+        for s, value in enumerate(made(layers - 1, m)):
+            target = shared if m < 2 else later
+            target[m % 2, s] = value.astype(jnp.bfloat16)
+
+
+def modulate(single, time_embed, time_w, mod_w, state, sums, others):
+    layers, count, _, depth = mod_w.shape
+    samples, _, tokens = state.shape
+    args = [single, time_embed, time_w, mod_w, state, sums]
     return local_call(
         modulate_kernel,
-        (
-            jax.ShapeDtypeStruct((count + 4, samples, width, tokens), jnp.float32),
-            jax.ShapeDtypeStruct((2, samples, width, tokens), jnp.bfloat16),
+        tuple(
+            jax.ShapeDtypeStruct(lead + state.shape, jnp.bfloat16)
+            for lead in ((), (), (2 * layers,), (2,), (2,))
         ),
-        [whole(single.shape), whole(shift.shape), whole(mod_w.shape)] + [UNREAD] * len(others),
-        [single, shift, mod_w, *others],
+        [whole(a.shape) for a in args] + [UNREAD] * len(others),
+        args + others,
         [pltpu.VMEM((samples * tokens, depth), jnp.bfloat16)],
-        4.8,
+        4.5,
         "modulate",
-    )
-
-
-def first_inputs_kernel(state, sums, mods, attn, trans):
-    mean_value = sums[0] / DA
-    scale = lax.rsqrt(sums[1] / DA - mean_value * mean_value + EPS)
-    for s in range(state.shape[0]):
-        normed = (state[s].astype(jnp.float32) - mean_value[s : s + 1]) * scale[s : s + 1]
-        attn[s] = (mods[0, s] * normed + mods[1, s]).astype(jnp.bfloat16)
-        trans[s] = (mods[2, s] * normed + mods[3, s]).astype(jnp.bfloat16)
-
-
-def first_inputs(state, sums, mods):
-    out = jax.ShapeDtypeStruct(state.shape, jnp.bfloat16)
-    return local_call(
-        first_inputs_kernel,
-        (out, out),
-        [
-            whole(state.shape),
-            whole(sums.shape),
-            pl.BlockSpec((4,) + state.shape, lambda i: (0, 0, 0, 0)),
-        ],
-        [state, sums, mods],
-        [],
-        2.0,
-        "first_inputs",
     )
 
 
@@ -526,20 +522,23 @@
     )(me, pair_in, tri_weight, *others)
 
 
-def pair_update_kernel(came, own, gate_w, out_w, bias_w, *refs):
+def pair_update_kernel(me_ref, came, own, gate_w, out_w, bias_w, *refs):
     back, message, rows_a, rows_b, rows_c = refs[-5:]
     channels, count, keys = came.shape
     over_rows = (((0,), (0,)), ((), ()))
 
-    def by_channel(value, rows):
-        rows[...] = value.astype(jnp.float32).reshape(channels * count, keys)
-        return jnp.concatenate([rows[pl.ds(u, channels, stride=count), :] for u in range(count)], 1)
+    def by_channel(value, rows, first):
+        height = value.shape[1]
+        rows[...] = value.astype(jnp.float32).reshape(channels * height, keys)
+        return jnp.concatenate(
+            [rows[pl.ds(first + u, channels, stride=height), :] for u in range(count)], 1
+        )
 
     def normed(value):
         return channel_norm(value, 0).astype(jnp.bfloat16)
 
-    pair = by_channel(own[...], rows_a)
-    sums = by_channel(came[...], rows_b)
+    pair = by_channel(own[...], rows_a, lax.rem(me_ref[0], own.shape[1] // count) * count)
+    sums = by_channel(came[...], rows_b, 0)
     gate = lax.dot_general(gate_w[0], normed(pair), over_rows, preferred_element_type=jnp.float32)
     update = lax.dot_general(out_w[...], normed(sums), over_rows, preferred_element_type=jnp.float32)
     new = (pair + jax.nn.sigmoid(gate) * update).astype(jnp.bfloat16).astype(jnp.float32)
@@ -556,32 +555,44 @@
             message[k, :, layer] = made[layer]
 
 
-def pair_update(came, own, tri_weight, out_weight, bias_w, layers, samp_size, col_size, others):
+def pair_update(
+    me, came, pair_in, tri_weight, out_weight, bias_w, layers, samp_size, col_size, others
+):
     channels, count, keys = came.shape
     heads = bias_w.shape[0] // (layers * col_size)
-    message = jax.ShapeDtypeStruct(
-        (samp_size, col_size, layers, heads, count, keys), jnp.bfloat16
-    )
-    return local_call(
+    out_shape = (
+        jax.ShapeDtypeStruct(came.shape, jnp.bfloat16),
+        jax.ShapeDtypeStruct((samp_size, col_size, layers, heads, count, keys), jnp.bfloat16),
+    )
+
+    def fixed(shape, *at):
+        return pl.BlockSpec(tuple(shape), lambda i, me: (at or (0,) * len(shape)))
+
+    return pl.pallas_call(
         pair_update_kernel,
-        (jax.ShapeDtypeStruct(came.shape, jnp.bfloat16), message),
-        [
-            whole(came.shape),
-            whole(own.shape),
-            layer_block(tri_weight.shape, 0, 4),
-            whole(out_weight.shape),
-            whole(bias_w.shape),
-        ]
-        + [UNREAD] * len(others),
-        [came, own, tri_weight, out_weight, bias_w, *others],
-        [
-            pltpu.VMEM((channels * count, keys), jnp.float32),
-            pltpu.VMEM((channels * count, keys), jnp.float32),
-            pltpu.VMEM((bias_w.shape[0] * count, keys), jnp.float32),
-        ],
-        2.8,
-        "pair_update",
-    )
+        grid_spec=pltpu.PrefetchScalarGridSpec(
+            num_scalar_prefetch=1,
+            grid=(1,),
+            in_specs=[
+                fixed(came.shape),
+                pl.BlockSpec((channels, 2 * count, keys), lambda i, me: (0, me[0] // 2, 0)),
+                fixed((1,) + tri_weight.shape[1:], 4, 0, 0),
+                fixed(out_weight.shape),
+                fixed(bias_w.shape),
+            ]
+            + [UNREAD] * len(others),
+            out_specs=tuple(fixed(o.shape) for o in out_shape),
+            scratch_shapes=[
+                pltpu.VMEM((2 * channels * count, keys), jnp.float32),
+                pltpu.VMEM((channels * count, keys), jnp.float32),
+                pltpu.VMEM((bias_w.shape[0] * count, keys), jnp.float32),
+            ],
+        ),
+        out_shape=out_shape,
+        compiler_params=pltpu.CompilerParams(vmem_limit_bytes=CLAIM * MIB),
+        cost_estimate=expected(2.8),
+        name="pair_update",
+    )(me, came, pair_in, tri_weight, out_weight, bias_w, *others)
 
 
 def pair_rows_kernel(came, out):
@@ -647,37 +658,41 @@
     frequency = jnp.exp(jnp.arange(half_count, dtype=jnp.float32) * (math.log(100.0) / half_count))
     angles = (jnp.log(noise_sigma) * 0.25)[:, None] * frequency[None, :]
     time_embed = jnp.concatenate([jnp.cos(angles), jnp.sin(angles)], 1).astype(jnp.bfloat16)
-    time_shift = jnp.dot(time_embed, time_weight, preferred_element_type=jnp.float32)
-
-    to_send = pair_project(pair_in, tri_weight, samp_at, group, samp_size, [sums])
+
+    to_send = pair_project(pair_in, tri_weight, samp_at, group, samp_size, [sums, time_embed])
     came = lax.all_to_all(to_send, ("row", "col"), 0, 0, tiled=True)
     came = came.reshape(row_size, col_size, half_rows + pair_rows, pair_cols)
 
-    mods, shared = modulate(single, time_shift, mod_w, [to_send])
-    attn_local, trans_local = first_inputs(state, sums, mods)
-    attn_full = lax.all_gather(attn_local, "col", axis=0)
-
-    triangle = triangle_sums(came, [attn_full])
-    shared = lax.all_gather(shared, "col", axis=0)
+    attn_local, trans_local, mods, later, shared = modulate(
+        single, time_embed, time_weight, mod_w, state, sums, [to_send]
+    )
+
+    attn_full = swap_all(attn_local, "col")
+    triangle = triangle_sums(came, attn_full[1:])
+    shared = swap_all(shared, "col")
     triangle = triangle.reshape(samp_size * group, cell_rows, pair_cols)
     triangle = lax.all_to_all(triangle, ("samp", "row", "col"), 0, 0, tiled=True)
     triangle = triangle.reshape(channels, own_rows, pair_cols)
-    mask_row = token_mask.astype(jnp.bfloat16)[None]
-    queries, gates, both = project([attn_full], query_w, key_w, value_gate_w, mask_row, 0)
+    mask_row = token_mask[None]
+    queries, gates, both = project(
+        attn_full, col_at, query_w, key_w, value_gate_w, mask_row, 0
+    )
     pieces = swap_all(both, "row")
 
-    own_pair = lax.dynamic_slice_in_dim(pair_in, samp_at[0] * own_rows, own_rows, 1)
+    trans_full = swap_all(trans_local, "col")
+
     bias_w = jnp.swapaxes(bias_weight, 1, 2).reshape(blocks * head_count, channels)
     pair_out, bias = pair_update(
+        samp_at,
         triangle,
-        own_pair,
+        pair_in,
         tri_weight,
         out_weight,
         bias_w,
         blocks,
         samp_size // NEAR,
         col_size,
-        [both, shared],
+        [both, *trans_full[1:]],
     )
     far = samp_size // NEAR
     message = bias.shape
@@ -698,25 +713,25 @@
     ]
     pair_back = after(pair_out, [biases[1]]).reshape(samp_size, share, own_rows, pair_cols)
     pair_back = lax.all_to_all(pair_back, "samp", 0, 0, tiled=True)
-    trans_full = lax.all_gather(trans_local, "col", axis=0)
     trans = transition(trans_full, col_at, up_weight, down_weight, 0, col_size)
-    trans_sum = sum_parts(*trans)
+    trans_sum, sent = sum_parts(*trans)
     seat = jnp.concatenate([row_at, samp_at % NEAR, col_at])
 
     for layer in range(blocks):
         if layer > 0:
             queries, gates, both, trans_local = project(
-                [state], query_w, key_w, value_gate_w, mask_row, layer, col_at, shared, mods
+                [state], col_at, query_w, key_w, value_gate_w, mask_row, layer, shared, later
             )
             pieces = swap_all(both, "row")
-            trans_full = lax.all_gather(trans_local, "col", axis=0)
+            trans_full = swap_all(trans_local, "col")
             trans = transition(trans_full, col_at, up_weight, down_weight, layer, col_size)
-            trans_sum = sum_parts(*trans)
+            trans_sum, sent = sum_parts(*trans)
+        others = [sent] if layer else [trans_sum[2], *shared[1:]]
         attended = attention(
-            seat, queries, gates, pieces, biases, attn_out_weight, layer, [trans[0] if layer else trans_sum[2]]
+            seat, queries, gates, pieces, biases, attn_out_weight, layer, others
         )
         state = finish(
-            sum_parts(*attended), trans_sum, mods, 4 * (1 + layer), [] if layer else [pair_back]
+            sum_parts(*attended)[0], trans_sum, mods, 2 * layer, [] if layer else [pair_back]
         )
         if layer == 0:
             state = lax.all_gather(state, "col", axis=0)

time: 205 us -> 192 us (0.937)
  blocking collectives: 42.6 us -> 9.63 us
  waiting for transfers between devices: 23.3 us -> 46.3 us
  starting transfers between devices: 47.9 us -> 65.7 us
  between operations: 14.1 us -> 0.78 us
  local copies, waits for them, and re-layouts: 8.78 us -> 6.54 us
  Pallas kernels: 60.4 us -> 58.3 us
    all_gather x3 -> x0, blocking collectives: 33.6 us -> none  [the longest x2 23.2 us: body(): trans_full = lax.all_gather(trans_local, 'col', axis=0)]
    ppermute x17 -> x29, waiting for transfers between devices: 12.2 us -> 38 us  [swap(): return lax.ppermute(value, axis, [(k, k ^ flip) for k in range(size)])]
    ppermute x17 -> x29, starting transfers between devices: 15.8 us -> 31.3 us  [swap(): return lax.ppermute(value, axis, [(k, k ^ flip) for k in range(size)])]
    all_to_all x1, waiting for transfers between devices: 9.99 us -> 3 us  [body(): lax.all_to_all(triangle, ('samp', 'row', 'col'), 0, 0, tiled=True)]
    pallas_call x17 -> x15, Pallas kernels: 50.7 us -> 45.7 us  [local_call(): pl.pallas_call(kernel, grid=(1,), out_shape=out_shape, in_specs=in_specs,...]
    all_to_all x1, waiting for transfers between devices: 0.01 us -> 4.13 us  [body(): lax.all_to_all(bias.reshape((far * col_size,) + message[2:]), ('samp', 'c...]
    pallas_call x0 -> x1, Pallas kernels: none -> 2.94 us  [pair_update(): pl.pallas_call(pair_update_kernel, grid_spec=pltpu.PrefetchScalarGridSpec...]
    unnamed x32 -> x50, local copies, waits for them, and re-layouts: 7.12 us -> 6.54 us
  transfers between devices with their start and end apart: 25 -> 36, of which waited for: 8 -> 17; matrix products, arithmetic and copies ran while one was open for 3% -> 1% of each run, Pallas kernels for 19% -> 15%
where the time goes in v2:
time: 192 us; the launch traced here: 191 us
  starting transfers between devices  65.7 us (34%)
  Pallas kernels  58.3 us (30%)
  waiting for transfers between devices  46.3 us (24%)
  blocking collectives  9.63 us (5%)
  local copies, waits for them, and re-layouts  6.54 us (3%)
  other arithmetic  3.6 us (2%)
    pallas_call x15, Pallas kernels, local_call(): pl.pallas_call(kernel, grid=(1,), out_shape=out_shape, in_specs=in_specs,...  45.7 us
    ppermute x29, waiting for transfers between devices, swap(): return lax.ppermute(value, axis, [(k, k ^ flip) for k in range(size)])  38 us
    ppermute x29, starting transfers between devices, swap(): return lax.ppermute(value, axis, [(k, k ^ flip) for k in range(size)])  31.3 us
    all_to_all x1, starting transfers between devices, body(): lax.all_to_all(triangle, ('samp', 'row', 'col'), 0, 0, tiled=True)  13.7 us
    pallas_call x1, Pallas kernels, pair_project(): pl.pallas_call(pair_project_kernel, grid=(height // rows,), out_shape=out...  9.66 us
    all_gather x1, blocking collectives, body(): state = lax.all_gather(state, 'col', axis=0)  9.63 us
    all_to_all x1, starting transfers between devices, body(): pair_back = lax.all_to_all(pair_back, 'samp', 0, 0, tiled=True)  7.59 us
    unnamed x50, local copies, waits for them, and re-layouts  6.54 us
  transfers between devices with their start and end apart: 36, of which 17 were waited for; matrix products, arithmetic and copies ran while one was open for 1% of the time, Pallas kernels for 15%

profile of v2, /device:TPU:1, one launch (start us, length us, event | category | flops | bytes accessed | tf_op | source)
XLA Modules:
  0.0 190.9 jit_solution(15100155919006602087)
XLA Ops:
  0.6 1.0 convert_reduce_fusion
  1.6 3.3 %collective-permute-start = (f32[2,3,128]{2,1,0:T(4,128)S(1)}, f32[2,3,128]{2,1,0:T(4,128)S(1)}, u32[]{:S(2)}, u32[]{:S(2)}) collective-permute-start(f32[2,3,128]{2,1,0:T(4,128)S(1)} %pad_maximum_fusion), channel_id=1, source_target_pairs={{0,1},{1,0},{2,3},{3,2},{4,5},{5,4},{6,7},{7,6},{8,9},{9,8},{10,11... | collective-permute-start | bytes 9224 | tf_op jit(solution)/shard_map/ppermute | solution.py:32
  4.9 1.7 collective-permute-start.2
  6.7 0.7 log_multiply_fusion
  8.8 9.7 %pair_project.1.refs_0_ = bf16[16,192,128]{2,1,0:T(8,128)(2,1)} custom-call(s32[1]{0:T(128)} %bitcast.me_ref, bf16[128,128,128]{2,1,0:T(8,128)(2,1)} %own.1, bf16[5,128,128]{2,1,0:T(8,128)(2,1)} %gate_w.1, f32[2,3,128]{2,1,0:T(4,128)} %add_add_fusion.refs_0_.sums, bf16[3,256]{1,0:T(4,128)(2,1)} %pad_maximum_fusion.1.refs_1_.time_embed), custom_call_target="tpu_custom_call" | custom-call | bytes 35793000 | tf_op jit(solution)/shard_map/pair_project/pallas_call | solution.py:502
  18.5 4.5 %all-to-all-start = ((bf16[16,192,128]{2,1,0:T(8,128)(2,1)}), bf16[16,192,128]{2,1,0:T(8,128)(2,1)S(1)}, u32[]{:S(2)}, u32[]{:S(2)}) async-start(bf16[16,192,128]{2,1,0:T(8,128)(2,1)} %pair_project.1.refs_0_), calls=%async_computation | async-start | bytes 1572864 | tf_op jit(solution)/shard_map/all_to_all | solution.py:663
  23.0 4.2 %modulate.1 = (bf16[3,192,128]{2,1,0:T(8,128)(2,1)}, bf16[3,192,128]{2,1,0:T(8,128)(2,1)}, bf16[4,3,192,128]{3,2,1,0:T(8,128)(2,1)}, bf16[2,3,192,128]{3,2,1,0:T(8,128)(2,1)}, bf16[2,3,192,128]{3,2,1,0:T(8,128)(2,1)}) custom-call(bf16[128,384]{1,0:T(8,128)(2,1)} %single.1, bf16[3,256]{1,0:T(4,128)(2,1)} %pad_maximum_fusion.1.refs_1_.time_embed, ...), custom_call_target="tpu_custom_call" | custom-call | bytes 16605000 | tf_op jit(solution)/shard_map/modulate/pallas_call | solution.py:44
  27.3 1.6 collective-permute-start.4
  29.3 7.6 %collective-permute-done.4.refs_1_.block2 = bf16[3,192,128]{2,1,0:T(8,128)(2,1)S(1)} collective-permute-done((bf16[3,192,128]{2,1,0:T(8,128)(2,1)}, bf16[3,192,128]{2,1,0:T(8,128)(2,1)S(1)}, u32[]{:S(2)}, u32[]{:S(2)}) %collective-permute-start.4) | collective-permute-done | bytes 147488 | tf_op jit(solution)/shard_map/ppermute | solution.py:32
  37.6 2.8 %collective-permute-done.5.refs_2_.block3 = bf16[3,192,128]{2,1,0:T(8,128)(2,1)} collective-permute-done((bf16[3,192,128]{2,1,0:T(8,128)(2,1)}, bf16[3,192,128]{2,1,0:T(8,128)(2,1)}, u32[]{:S(2)}, u32[]{:S(2)}) %collective-permute-start.5) | collective-permute-done | bytes 147488 | tf_op jit(solution)/shard_map/ppermute | solution.py:32
  40.4 0.9 copy-done
  41.4 2.2 %triangle_sums.1 = bf16[8,2,4,2,8,128]{5,4,3,2,1,0:T(8,128)(2,1)} custom-call(bf16[4,4,192,128]{3,2,1,0:T(8,128)(2,1)} %bitcast.26, bf16[3,192,128]{2,1,0:T(8,128)(2,1)} %copy-done.16, bf16[3,192,128]{2,1,0:T(8,128)(2,1)} %copy-done.17, bf16[3,192,128]{2,1,0:T(8,128)(2,1)} %collective-permute-done.5.refs_2_.block3), custom_call_target="tpu_custom_call" | custom-call | bytes 8118000 | tf_op jit(solution)/shard_map/triangle_sums/pallas_call | solution.py:44
  43.5 13.7 %all-to-all-start.1 = ((bf16[256,4,128]{2,1,0:T(4,128)(2,1)}), bf16[256,4,128]{2,1,0:T(4,128)(2,1)S(1)}, u32[]{:S(2)}, u32[]{:S(2)}) async-start(bf16[256,4,128]{2,1,0:T(4,128)(2,1)} %bitcast.40), calls=%async_computation.1 | async-start | bytes 524288 | tf_op jit(solution)/shard_map/all_to_all | solution.py:674
  57.2 2.2 %collective-permute-start.6 = (bf16[3,192,128]{2,1,0:T(8,128)(2,1)}, bf16[3,192,128]{2,1,0:T(8,128)(2,1)S(1)}, u32[]{:S(2)}, u32[]{:S(2)}) collective-permute-start(bf16[3,192,128]{2,1,0:T(8,128)(2,1)} %get-tuple-element.26.refs_1_), channel_id=1, source_target_pairs={{0,1},{1,0},{2,3},{3,2},{4,5},{5,4},{6,7},{7,6},{8,9},{9,8},{10,11... | collective-permute-start | bytes 442376 | tf_op jit(solution)/shard_map/ppermute | solution.py:32
  59.5 1.7 collective-permute-start.8
  61.2 3.1 %first_project.1 = (bf16[3,192,128]{2,1,0:T(8,128)(2,1)}, bf16[3,192,128]{2,1,0:T(8,128)(2,1)}, bf16[1168,128]{1,0:T(8,128)(2,1)}) custom-call(s32[1]{0:T(128)} %bitcast.10.me_ref.refs_0_, bf16[3,192,128]{2,1,0:T(8,128)(2,1)} %get-tuple-element.24.block0, bf16[3,192,128]{2,1,0:T(8,128)(2,1)} %copy-done.16, bf16[3,192,128]{2,1,0:T(8,128)(2,1)} %copy-done.17, ...), custom_call_target="tpu_custom_call" | custom-call | bytes 11070000 | tf_op jit(solution)/shard_map/first_project/pallas_call | solution.py:44
  64.3 2.4 %collective-permute-done.7.refs_2_.refs_3_ = bf16[3,192,128]{2,1,0:T(8,128)(2,1)S(1)} collective-permute-done((bf16[3,192,128]{2,1,0:T(8,128)(2,1)}, bf16[3,192,128]{2,1,0:T(8,128)(2,1)S(1)}, u32[]{:S(2)}, u32[]{:S(2)}) %collective-permute-start.7) | collective-permute-done | bytes 147488 | tf_op jit(solution)/shard_map/ppermute | solution.py:32
  66.7 3.6 %collective-permute-done.8.refs_3_.refs_4_ = bf16[3,192,128]{2,1,0:T(8,128)(2,1)S(1)} collective-permute-done((bf16[3,192,128]{2,1,0:T(8,128)(2,1)}, bf16[3,192,128]{2,1,0:T(8,128)(2,1)S(1)}, u32[]{:S(2)}, u32[]{:S(2)}) %collective-permute-start.8) | collective-permute-done | bytes 147488 | tf_op jit(solution)/shard_map/ppermute | solution.py:32
  70.3 3.0 %all-to-all-done.1 = bf16[256,4,128]{2,1,0:T(4,128)(2,1)S(1)} async-done(((bf16[256,4,128]{2,1,0:T(4,128)(2,1)}), bf16[256,4,128]{2,1,0:T(4,128)(2,1)S(1)}, u32[]{:S(2)}, u32[]{:S(2)}) %all-to-all-start.1) | async-done | bytes 262176 | tf_op jit(solution)/shard_map/all_to_all | solution.py:674
  73.3 0.7 copy-done.9
  74.0 2.9 %pair_update.1 = (bf16[128,8,128]{2,1,0:T(8,128)(2,1)}, bf16[4,4,2,4,8,128]{5,4,3,2,1,0:T(8,128)(2,1)}) custom-call(s32[1]{0:T(128)} %bitcast.me_ref, bf16[128,8,128]{2,1,0:T(8,128)(2,1)} %bitcast.39, bf16[128,128,128]{2,1,0:T(8,128)(2,1)} %own.1, bf16[5,128,128]{2,1,0:T(8,128)(2,1)} %gate_w.1, bf16[128,128]{1,0:T(8,128)(2,1)} %out_w.1, ...), custom_call_target="tpu_custom_call" | custom-call | bytes 10332000 | tf_op jit(solution)/shard_map/pair_update/pallas_call | solution.py:571
  77.0 3.8 %all-to-all-start.2 = ((bf16[16,2,4,8,128]{4,3,2,1,0:T(8,128)(2,1)}), bf16[16,2,4,8,128]{4,3,2,1,0:T(8,128)(2,1)S(1)}, u32[]{:S(2)}, u32[]{:S(2)}) async-start(bf16[16,2,4,8,128]{4,3,2,1,0:T(8,128)(2,1)} %bitcast.42), calls=%async_computation.2 | async-start | bytes 524288 | tf_op jit(solution)/shard_map/all_to_all | solution.py:699
  81.2 1.4 collective-permute-start.18
  83.1 1.1 collective-permute-start.10
  84.2 4.1 %transition.2 = (f32[2,3,192,128]{3,2,1,0:T(8,128)}, bf16[2,3,192,128]{3,2,1,0:T(8,128)(2,1)}) custom-call(s32[1]{0:T(128)} %bitcast.10.me_ref.refs_0_, bf16[3,192,128]{2,1,0:T(8,128)(2,1)} %get-tuple-element.26.refs_1_, bf16[3,192,128]{2,1,0:T(8,128)(2,1)} %copy-done.12, bf16[3,192,128]{2,1,0:T(8,128)(2,1)} %copy-done.13, bf16[3,192,128]{2,1,0:T(8,128)(2,1)} %copy-done.14, ...), custom_call_target="tpu_custom_call" | custom-call | bytes 14022000 | tf_op jit(solution)/shard_map/transition/pallas_call | solution.py:44
  88.6 4.1 %all-to-all-done.2 = bf16[16,2,4,8,128]{4,3,2,1,0:T(8,128)(2,1)S(1)} async-done(((bf16[16,2,4,8,128]{4,3,2,1,0:T(8,128)(2,1)}), bf16[16,2,4,8,128]{4,3,2,1,0:T(8,128)(2,1)S(1)}, u32[]{:S(2)}, u32[]{:S(2)}) %all-to-all-start.2) | async-done | bytes 262176 | tf_op jit(solution)/shard_map/all_to_all | solution.py:699
  92.7 1.2 collective-permute-start.9
  94.0 1.2 collective-permute-done.18.refs_3_.pair2
  95.2 2.8 %collective-permute-start.11 = (bf16[1168,128]{1,0:T(8,128)(2,1)}, bf16[1168,128]{1,0:T(8,128)(2,1)}, u32[]{:S(2)}, u32[]{:S(2)}) collective-permute-start(bf16[1168,128]{1,0:T(8,128)(2,1)} %get-tuple-element.25.refs_0_.kv0), channel_id=1, source_target_pairs={{0,8},{4,12},{8,0},{12,4},{1,9},{5,13},{9,1},{13,5},{2,10},{6,14},... | collective-permute-start | bytes 897032 | tf_op jit(solution)/shard_map/ppermute | solution.py:32
  98.0 4.0 %collective-permute-done.19.refs_4_.pair3 = bf16[2,3,192,128]{3,2,1,0:T(8,128)(2,1)} collective-permute-done((bf16[2,3,192,128]{3,2,1,0:T(8,128)(2,1)}, bf16[2,3,192,128]{3,2,1,0:T(8,128)(2,1)}, u32[]{:S(2)}, u32[]{:S(2)}) %collective-permute-start.19) | collective-permute-done | bytes 294944 | tf_op jit(solution)/shard_map/ppermute | solution.py:32
  101.9 2.6 %collective-permute-start.12 = (bf16[1168,128]{1,0:T(8,128)(2,1)}, bf16[1168,128]{1,0:T(8,128)(2,1)}, u32[]{:S(2)}, u32[]{:S(2)}) collective-permute-start(bf16[1168,128]{1,0:T(8,128)(2,1)} %get-tuple-element.25.refs_0_.kv0), channel_id=1, source_target_pairs={{0,12},{4,8},{8,4},{12,0},{1,13},{5,9},{9,5},{13,1},{2,14},{6,10},... | collective-permute-start | bytes 897032 | tf_op jit(solution)/shard_map/ppermute | solution.py:32
  104.5 2.7 %collective-permute-start.13 = (bf16[4,4,2,4,8,128]{5,4,3,2,1,0:T(8,128)(2,1)S(1)}, bf16[4,4,2,4,8,128]{5,4,3,2,1,0:T(8,128)(2,1)S(1)}, u32[]{:S(2)}, u32[]{:S(2)}) collective-permute-start(bf16[4,4,2,4,8,128]{5,4,3,2,1,0:T(8,128)(2,1)S(1)} %bitcast.33), channel_id=1, source_target_pairs={{0,32},{16,48},{32,0},{48,16},{64,96},{80,112},{96,64},{112,80},{1... | collective-permute-start | bytes 786440 | tf_op jit(solution)/shard_map/ppermute | solution.py:711
  107.3 0.9 collective-permute-start.14
  108.2 1.7 join.4
  110.6 7.6 %all-to-all-start.3 = ((bf16[16,8,8,128]{3,2,1,0:T(8,128)(2,1)}), bf16[16,8,8,128]{3,2,1,0:T(8,128)(2,1)S(1)}, u32[]{:S(2)}, u32[]{:S(2)}) async-start(bf16[16,8,8,128]{3,2,1,0:T(8,128)(2,1)} %bitcast.38), calls=%async_computation.3 | async-start | bytes 524288 | tf_op jit(solution)/shard_map/all_to_all | solution.py:715
  118.9 1.1 collective-permute-done.14.bias3
  120.0 5.5 %attention.2 = (f32[2,3,192,128]{3,2,1,0:T(8,128)}, bf16[2,3,192,128]{3,2,1,0:T(8,128)(2,1)}) custom-call(s32[3]{0:T(128)} %pad_add_fusion.me_ref, bf16[3,192,128]{2,1,0:T(8,128)(2,1)} %get-tuple-element.29.queries, bf16[3,192,128]{2,1,0:T(8,128)(2,1)} %get-tuple-element.30.gates, bf16[1168,128]{1,0:T(8,128)(2,1)} %get-tuple-element.25.refs_0_.kv0, ...), custom_call_target="tpu_custom_call" | custom-call | bytes 19926000 | tf_op jit(solution)/shard_map/attention/pallas_call | solution.py:44
  125.5 1.1 collective-permute-start.20
  126.6 1.4 collective-permute-done.20.came.came_a
  128.1 0.7 copy-done.8
  128.8 1.7 join.5
  130.9 4.9 %collective-permute-done.21.far_a = bf16[3,192,128]{2,1,0:T(8,128)(2,1)S(1)} collective-permute-done((bf16[3,192,128]{2,1,0:T(8,128)(2,1)}, bf16[3,192,128]{2,1,0:T(8,128)(2,1)S(1)}, u32[]{:S(2)}, u32[]{:S(2)}) %collective-permute-start.21) | collective-permute-done | bytes 147488 | tf_op jit(solution)/shard_map/ppermute | solution.py:32
  136.5 2.2 %finish.2 = bf16[3,192,128]{2,1,0:T(8,128)(2,1)} custom-call(f32[2,3,192,128]{3,2,1,0:T(8,128)} %get-tuple-element.34.keep.keep_a, bf16[2,3,192,128]{3,2,1,0:T(8,128)(2,1)} %copy-done.8, bf16[3,192,128]{2,1,0:T(8,128)(2,1)} %copy-done.24, f32[2,3,192,128]{3,2,1,0:T(8,128)} %get-tuple-element.31.keep.keep_t, bf16[2,3,192,128]{3,2,1,0:T(8,128)(2,1)} %copy-done.5, ...), custom_call_target="tpu_custom_call" | custom-call | bytes 7380000 | tf_op jit(solution)/shard_map/finish/pallas_call | solution.py:44
  138.7 9.6 %all-gather = bf16[12,192,128]{2,1,0:T(8,128)(2,1)} all-gather(bf16[3,192,128]{2,1,0:T(8,128)(2,1)} %finish.2), channel_id=2, replica_groups=mesh['samp'=16,'row'=4,'col'=4] {'col'}, dimensions={0}, use_global_device_ids=true | all-gather | bytes 737280 | tf_op jit(solution)/shard_map/all_gather | solution.py:737
  148.3 4.2 %later_project.1 = (bf16[3,192,128]{2,1,0:T(8,128)(2,1)}, bf16[3,192,128]{2,1,0:T(8,128)(2,1)}, bf16[1168,128]{1,0:T(8,128)(2,1)}, bf16[3,192,128]{2,1,0:T(8,128)(2,1)}) custom-call(s32[1]{0:T(128)} %bitcast.10.me_ref.refs_0_, bf16[4,3,192,128]{3,2,1,0:T(8,128)(2,1)} %bitcast.27, bf16[2,3,192,128]{3,2,1,0:T(8,128)(2,1)} %get-tuple-element.33.pair0, ...), custom_call_target="tpu_custom_call" | custom-call | bytes 14760000 | tf_op jit(solution)/shard_map/later_project/pallas_call | solution.py:44
  152.7 1.0 collective-permute-start.26
  153.7 0.9 collective-permute-start.27
  154.7 1.2 collective-permute-start.23
  155.9 2.6 %collective-permute-start.24 = (bf16[1168,128]{1,0:T(8,128)(2,1)}, bf16[1168,128]{1,0:T(8,128)(2,1)}, u32[]{:S(2)}, u32[]{:S(2)}) collective-permute-start(bf16[1168,128]{1,0:T(8,128)(2,1)} %get-tuple-element.40.kv0), channel_id=1, source_target_pairs={{0,12},{4,8},{8,4},{12,0},{1,13},{5,9},{9,5},{13,1},{2,14},{6,10},... | collective-permute-start | bytes 897032 | tf_op jit(solution)/shard_map/ppermute | solution.py:32
  158.5 3.5 %collective-permute-done.27.refs_4_ = bf16[3,192,128]{2,1,0:T(8,128)(2,1)} collective-permute-done((bf16[3,192,128]{2,1,0:T(8,128)(2,1)}, bf16[3,192,128]{2,1,0:T(8,128)(2,1)}, u32[]{:S(2)}, u32[]{:S(2)}) %collective-permute-start.27) | collective-permute-done | bytes 147488 | tf_op jit(solution)/shard_map/ppermute | solution.py:32
  162.0 4.1 %transition.3 = (f32[2,3,192,128]{3,2,1,0:T(8,128)}, bf16[2,3,192,128]{3,2,1,0:T(8,128)(2,1)}) custom-call(s32[1]{0:T(128)} %bitcast.10.me_ref.refs_0_, bf16[3,192,128]{2,1,0:T(8,128)(2,1)} %get-tuple-element.41.refs_1_, bf16[3,192,128]{2,1,0:T(8,128)(2,1)} %copy-done.20, bf16[3,192,128]{2,1,0:T(8,128)(2,1)} %copy-done.21, ...), custom_call_target="tpu_custom_call" | custom-call | bytes 14022000 | tf_op jit(solution)/shard_map/transition/pallas_call | solution.py:44
  166.1 1.8 collective-permute-done.28.came.came_t
  167.9 0.7 copy-done.6
  168.6 1.7 join.6.refs_1_
  170.3 1.8 collective-permute-done.24.kv3
  172.1 5.5 %attention.3 = (f32[2,3,192,128]{3,2,1,0:T(8,128)}, bf16[2,3,192,128]{3,2,1,0:T(8,128)(2,1)}) custom-call(s32[3]{0:T(128)} %pad_add_fusion.me_ref, bf16[3,192,128]{2,1,0:T(8,128)(2,1)} %get-tuple-element.38.queries, bf16[3,192,128]{2,1,0:T(8,128)(2,1)} %get-tuple-element.39.gates, bf16[1168,128]{1,0:T(8,128)(2,1)} %get-tuple-element.40.kv0, ...), custom_call_target="tpu_custom_call" | custom-call | bytes 19926000 | tf_op jit(solution)/shard_map/attention/pallas_call | solution.py:44
  177.7 1.3 collective-permute-start.29
  178.9 1.1 collective-permute-start.31
  180.3 0.7 copy-done.7
  181.1 1.7 join.7
  182.8 1.1 collective-permute-start.30
  183.8 1.7 pair_rows.1
  185.5 2.5 %collective-permute-done.30.far_a = bf16[3,192,128]{2,1,0:T(8,128)(2,1)S(1)} collective-permute-done((bf16[3,192,128]{2,1,0:T(8,128)(2,1)}, bf16[3,192,128]{2,1,0:T(8,128)(2,1)S(1)}, u32[]{:S(2)}, u32[]{:S(2)}) %collective-permute-start.30) | collective-permute-done | bytes 147488 | tf_op jit(solution)/shard_map/ppermute | solution.py:32
  188.7 2.2 %finish.3 = bf16[3,192,128]{2,1,0:T(8,128)(2,1)} custom-call(f32[2,3,192,128]{3,2,1,0:T(8,128)} %get-tuple-element.44.keep.keep_a, bf16[2,3,192,128]{3,2,1,0:T(8,128)(2,1)} %copy-done.7, bf16[3,192,128]{2,1,0:T(8,128)(2,1)} %copy-done.23, f32[2,3,192,128]{3,2,1,0:T(8,128)} %get-tuple-element.42.keep.keep_t, bf16[2,3,192,128]{3,2,1,0:T(8,128)(2,1)} %copy-done.6, ...), custom_call_target="tpu_custom_call" | custom-call | bytes 7380000 | tf_op jit(solution)/shard_map/finish/pallas_call | solution.py:44
  (85 shorter events, 7.8 us)
Async XLA Ops:
  1.6 6.4 %collective-permute-start = (f32[2,3,128]{2,1,0:T(4,128)S(1)}, f32[2,3,128]{2,1,0:T(4,128)S(1)}, u32[]{:S(2)}, u32[]{:S(2)}) collective-permute-start(f32[2,3,128]{2,1,0:T(4,128)S(1)} %pad_maximum_fusion), channel_id=1, source_target_pairs={{0,1},{1,0},{2,3},{3,2},{4,5},{5,4},{6,7},{7,6},{8,9},{9,8},{10,11... | collective-permute-start | bytes 9224 | tf_op jit(solution)/shard_map/ppermute | solution.py:32
  4.9 3.1 %collective-permute-start.1 = (f32[2,3,128]{2,1,0:T(4,128)S(1)}, f32[2,3,128]{2,1,0:T(4,128)S(1)}, u32[]{:S(2)}, u32[]{:S(2)}) collective-permute-start(f32[2,3,128]{2,1,0:T(4,128)S(1)} %pad_maximum_fusion), channel_id=1, source_target_pairs={{0,2},{1,3},{2,0},{3,1},{4,6},{5,7},{6,4},{7,5},{8,10},{9,11},{10,... | collective-permute-start | bytes 9224 | tf_op jit(solution)/shard_map/ppermute | solution.py:32
  4.9 3.3 %collective-permute-start.2 = (f32[2,3,128]{2,1,0:T(4,128)S(1)}, f32[2,3,128]{2,1,0:T(4,128)S(1)}, u32[]{:S(2)}, u32[]{:S(2)}) collective-permute-start(f32[2,3,128]{2,1,0:T(4,128)S(1)} %pad_maximum_fusion), channel_id=1, source_target_pairs={{0,3},{1,2},{2,1},{3,0},{4,7},{5,6},{6,5},{7,4},{8,11},{9,10},{10,... | collective-permute-start | bytes 9224 | tf_op jit(solution)/shard_map/ppermute | solution.py:32
  18.5 21.9 %all-to-all-start = ((bf16[16,192,128]{2,1,0:T(8,128)(2,1)}), bf16[16,192,128]{2,1,0:T(8,128)(2,1)S(1)}, u32[]{:S(2)}, u32[]{:S(2)}) async-start(bf16[16,192,128]{2,1,0:T(8,128)(2,1)} %pair_project.1.refs_0_), calls=%async_computation | async-start | bytes 1572864 | tf_op jit(solution)/shard_map/all_to_all | solution.py:663
  27.2 2.1 %collective-permute-start.3 = (bf16[3,192,128]{2,1,0:T(8,128)(2,1)}, bf16[3,192,128]{2,1,0:T(8,128)(2,1)S(1)}, u32[]{:S(2)}, u32[]{:S(2)}) collective-permute-start(bf16[3,192,128]{2,1,0:T(8,128)(2,1)} %get-tuple-element.24.block0), channel_id=1, source_target_pairs={{0,1},{1,0},{2,3},{3,2},{4,5},{5,4},{6,7},{7,6},{8,9},{9,8},{10,11... | collective-permute-start | bytes 442376 | tf_op jit(solution)/shard_map/ppermute | solution.py:32
  27.3 9.7 %collective-permute-start.4 = (bf16[3,192,128]{2,1,0:T(8,128)(2,1)}, bf16[3,192,128]{2,1,0:T(8,128)(2,1)S(1)}, u32[]{:S(2)}, u32[]{:S(2)}) collective-permute-start(bf16[3,192,128]{2,1,0:T(8,128)(2,1)} %get-tuple-element.24.block0), channel_id=1, source_target_pairs={{0,2},{1,3},{2,0},{3,1},{4,6},{5,7},{6,4},{7,5},{8,10},{9,11},{10,... | collective-permute-start | bytes 442376 | tf_op jit(solution)/shard_map/ppermute | solution.py:32
  28.9 11.5 %collective-permute-start.5 = (bf16[3,192,128]{2,1,0:T(8,128)(2,1)}, bf16[3,192,128]{2,1,0:T(8,128)(2,1)}, u32[]{:S(2)}, u32[]{:S(2)}) collective-permute-start(bf16[3,192,128]{2,1,0:T(8,128)(2,1)} %get-tuple-element.24.block0), channel_id=1, source_target_pairs={{0,3},{1,2},{2,1},{3,0},{4,7},{5,6},{6,5},{7,4},{8,11},{9,10},{10,... | collective-permute-start | bytes 442376 | tf_op jit(solution)/shard_map/ppermute | solution.py:32
  29.3 11.1 %copy-start.16 = (bf16[3,192,128]{2,1,0:T(8,128)(2,1)}, bf16[3,192,128]{2,1,0:T(8,128)(2,1)S(1)}, u32[]{:S(2)}) copy-start(bf16[3,192,128]{2,1,0:T(8,128)(2,1)S(1)} %collective-permute-done.3.refs_0_.block1) | copy-start | bytes 442372
  37.0 0.7 copy-start.17
  40.4 0.9 copy-start
  43.5 29.8 %all-to-all-start.1 = ((bf16[256,4,128]{2,1,0:T(4,128)(2,1)}), bf16[256,4,128]{2,1,0:T(4,128)(2,1)S(1)}, u32[]{:S(2)}, u32[]{:S(2)}) async-start(bf16[256,4,128]{2,1,0:T(4,128)(2,1)} %bitcast.40), calls=%async_computation.1 | async-start | bytes 524288 | tf_op jit(solution)/shard_map/all_to_all | solution.py:674
  57.2 7.1 %collective-permute-start.6 = (bf16[3,192,128]{2,1,0:T(8,128)(2,1)}, bf16[3,192,128]{2,1,0:T(8,128)(2,1)S(1)}, u32[]{:S(2)}, u32[]{:S(2)}) collective-permute-start(bf16[3,192,128]{2,1,0:T(8,128)(2,1)} %get-tuple-element.26.refs_1_), channel_id=1, source_target_pairs={{0,1},{1,0},{2,3},{3,2},{4,5},{5,4},{6,7},{7,6},{8,9},{9,8},{10,11... | collective-permute-start | bytes 442376 | tf_op jit(solution)/shard_map/ppermute | solution.py:32
  59.5 7.3 %collective-permute-start.7 = (bf16[3,192,128]{2,1,0:T(8,128)(2,1)}, bf16[3,192,128]{2,1,0:T(8,128)(2,1)S(1)}, u32[]{:S(2)}, u32[]{:S(2)}) collective-permute-start(bf16[3,192,128]{2,1,0:T(8,128)(2,1)} %get-tuple-element.26.refs_1_), channel_id=1, source_target_pairs={{0,2},{1,3},{2,0},{3,1},{4,6},{5,7},{6,4},{7,5},{8,10},{9,11},{10,... | collective-permute-start | bytes 442376 | tf_op jit(solution)/shard_map/ppermute | solution.py:32
  59.5 10.9 %collective-permute-start.8 = (bf16[3,192,128]{2,1,0:T(8,128)(2,1)}, bf16[3,192,128]{2,1,0:T(8,128)(2,1)S(1)}, u32[]{:S(2)}, u32[]{:S(2)}) collective-permute-start(bf16[3,192,128]{2,1,0:T(8,128)(2,1)} %get-tuple-element.26.refs_1_), channel_id=1, source_target_pairs={{0,3},{1,2},{2,1},{3,0},{4,7},{5,6},{6,5},{7,4},{8,11},{9,10},{10,... | collective-permute-start | bytes 442376 | tf_op jit(solution)/shard_map/ppermute | solution.py:32
  64.3 9.0 %copy-start.12 = (bf16[3,192,128]{2,1,0:T(8,128)(2,1)}, bf16[3,192,128]{2,1,0:T(8,128)(2,1)S(1)}, u32[]{:S(2)}) copy-start(bf16[3,192,128]{2,1,0:T(8,128)(2,1)S(1)} %collective-permute-done.6.refs_1_.refs_2_) | copy-start | bytes 442372
  66.7 6.6 %copy-start.13 = (bf16[3,192,128]{2,1,0:T(8,128)(2,1)}, bf16[3,192,128]{2,1,0:T(8,128)(2,1)S(1)}, u32[]{:S(2)}) copy-start(bf16[3,192,128]{2,1,0:T(8,128)(2,1)S(1)} %collective-permute-done.7.refs_2_.refs_3_) | copy-start | bytes 442372
  70.3 3.0 %copy-start.14 = (bf16[3,192,128]{2,1,0:T(8,128)(2,1)}, bf16[3,192,128]{2,1,0:T(8,128)(2,1)S(1)}, u32[]{:S(2)}) copy-start(bf16[3,192,128]{2,1,0:T(8,128)(2,1)S(1)} %collective-permute-done.8.refs_3_.refs_4_) | copy-start | bytes 442372
  73.3 0.7 copy-start.9
  77.0 15.8 %all-to-all-start.2 = ((bf16[16,2,4,8,128]{4,3,2,1,0:T(8,128)(2,1)}), bf16[16,2,4,8,128]{4,3,2,1,0:T(8,128)(2,1)S(1)}, u32[]{:S(2)}, u32[]{:S(2)}) async-start(bf16[16,2,4,8,128]{4,3,2,1,0:T(8,128)(2,1)} %bitcast.42), calls=%async_computation.2 | async-start | bytes 524288 | tf_op jit(solution)/shard_map/all_to_all | solution.py:699
  80.8 7.9 %collective-permute-start.17 = (bf16[2,3,192,128]{3,2,1,0:T(8,128)(2,1)}, bf16[2,3,192,128]{3,2,1,0:T(8,128)(2,1)S(1)}, u32[]{:S(2)}, u32[]{:S(2)}) collective-permute-start(bf16[2,3,192,128]{3,2,1,0:T(8,128)(2,1)} %get-tuple-element.33.pair0), channel_id=1, source_target_pairs={{0,1},{1,0},{2,3},{3,2},{4,5},{5,4},{6,7},{7,6},{8,9},{9,8},{10,11... | collective-permute-start | bytes 884744 | tf_op jit(solution)/shard_map/ppermute | solution.py:32
  81.2 14.0 %collective-permute-start.18 = (bf16[2,3,192,128]{3,2,1,0:T(8,128)(2,1)}, bf16[2,3,192,128]{3,2,1,0:T(8,128)(2,1)}, u32[]{:S(2)}, u32[]{:S(2)}) collective-permute-start(bf16[2,3,192,128]{3,2,1,0:T(8,128)(2,1)} %get-tuple-element.33.pair0), channel_id=1, source_target_pairs={{0,2},{1,3},{2,0},{3,1},{4,6},{5,7},{6,4},{7,5},{8,10},{9,11},{10,... | collective-permute-start | bytes 884744 | tf_op jit(solution)/shard_map/ppermute | solution.py:32
  82.5 19.4 %collective-permute-start.19 = (bf16[2,3,192,128]{3,2,1,0:T(8,128)(2,1)}, bf16[2,3,192,128]{3,2,1,0:T(8,128)(2,1)}, u32[]{:S(2)}, u32[]{:S(2)}) collective-permute-start(bf16[2,3,192,128]{3,2,1,0:T(8,128)(2,1)} %get-tuple-element.33.pair0), channel_id=1, source_target_pairs={{0,3},{1,2},{2,1},{3,0},{4,7},{5,6},{6,5},{7,4},{8,11},{9,10},{10,... | collective-permute-start | bytes 884744 | tf_op jit(solution)/shard_map/ppermute | solution.py:32
  83.1 24.2 %collective-permute-start.10 = (bf16[1168,128]{1,0:T(8,128)(2,1)}, bf16[1168,128]{1,0:T(8,128)(2,1)}, u32[]{:S(2)}, u32[]{:S(2)}) collective-permute-start(bf16[1168,128]{1,0:T(8,128)(2,1)} %get-tuple-element.25.refs_0_.kv0), channel_id=1, source_target_pairs={{0,4},{4,0},{8,12},{12,8},{1,5},{5,1},{9,13},{13,9},{2,6},{6,2},{1... | collective-permute-start | bytes 897032 | tf_op jit(solution)/shard_map/ppermute | solution.py:32
  88.3 16.3 %collective-permute-start.15 = (bf16[2,3,192,128]{3,2,1,0:T(8,128)(2,1)}, bf16[2,3,192,128]{3,2,1,0:T(8,128)(2,1)S(1)}, u32[]{:S(2)}, u32[]{:S(2)}) collective-permute-start(bf16[2,3,192,128]{3,2,1,0:T(8,128)(2,1)} %get-tuple-element.32), channel_id=1, source_target_pairs={{0,1},{1,0},{2,3},{3,2},{4,5},{5,4},{6,7},{7,6},{8,9},{9,8},{10,11... | collective-permute-start | bytes 884744 | tf_op jit(solution)/shard_map/ppermute | solution.py:32
  88.6 4.1 %copy-start.4 = (bf16[2,3,192,128]{3,2,1,0:T(8,128)(2,1)}, bf16[2,3,192,128]{3,2,1,0:T(8,128)(2,1)S(1)}, u32[]{:S(2)}) copy-start(bf16[2,3,192,128]{3,2,1,0:T(8,128)(2,1)S(1)} %collective-permute-done.17.refs_2_.pair1) | copy-start | bytes 884740
  92.7 27.3 %copy-start.3 = (bf16[16,2,4,8,128]{4,3,2,1,0:T(8,128)(2,1)}, bf16[16,2,4,8,128]{4,3,2,1,0:T(8,128)(2,1)S(1)}, u32[]{:S(2)}) copy-start(bf16[16,2,4,8,128]{4,3,2,1,0:T(8,128)(2,1)S(1)} %all-to-all-done.2) | copy-start | bytes 786436
  92.7 17.1 %collective-permute-start.9 = (bf16[4,4,2,4,8,128]{5,4,3,2,1,0:T(8,128)(2,1)S(1)}, bf16[4,4,2,4,8,128]{5,4,3,2,1,0:T(8,128)(2,1)S(1)}, u32[]{:S(2)}, u32[]{:S(2)}) collective-permute-start(bf16[4,4,2,4,8,128]{5,4,3,2,1,0:T(8,128)(2,1)S(1)} %bitcast.32), channel_id=1, source_target_pairs={{0,16},{16,0},{32,48},{48,32},{64,80},{80,64},{96,112},{112,96},{1... | collective-permute-start | bytes 786440 | tf_op jit(solution)/shard_map/ppermute | solution.py:711
  95.2 23.7 %collective-permute-start.11 = (bf16[1168,128]{1,0:T(8,128)(2,1)}, bf16[1168,128]{1,0:T(8,128)(2,1)}, u32[]{:S(2)}, u32[]{:S(2)}) collective-permute-start(bf16[1168,128]{1,0:T(8,128)(2,1)} %get-tuple-element.25.refs_0_.kv0), channel_id=1, source_target_pairs={{0,8},{4,12},{8,0},{12,4},{1,9},{5,13},{9,1},{13,5},{2,10},{6,14},... | collective-permute-start | bytes 897032 | tf_op jit(solution)/shard_map/ppermute | solution.py:32
  101.9 16.9 %collective-permute-start.12 = (bf16[1168,128]{1,0:T(8,128)(2,1)}, bf16[1168,128]{1,0:T(8,128)(2,1)}, u32[]{:S(2)}, u32[]{:S(2)}) collective-permute-start(bf16[1168,128]{1,0:T(8,128)(2,1)} %get-tuple-element.25.refs_0_.kv0), channel_id=1, source_target_pairs={{0,12},{4,8},{8,4},{12,0},{1,13},{5,9},{9,5},{13,1},{2,14},{6,10},... | collective-permute-start | bytes 897032 | tf_op jit(solution)/shard_map/ppermute | solution.py:32
  104.5 2.8 %copy-start.5 = (bf16[2,3,192,128]{3,2,1,0:T(8,128)(2,1)}, bf16[2,3,192,128]{3,2,1,0:T(8,128)(2,1)S(1)}, u32[]{:S(2)}) copy-start(bf16[2,3,192,128]{3,2,1,0:T(8,128)(2,1)S(1)} %collective-permute-done.15.came.came_t) | copy-start | bytes 884740
  104.5 14.3 %collective-permute-start.13 = (bf16[4,4,2,4,8,128]{5,4,3,2,1,0:T(8,128)(2,1)S(1)}, bf16[4,4,2,4,8,128]{5,4,3,2,1,0:T(8,128)(2,1)S(1)}, u32[]{:S(2)}, u32[]{:S(2)}) collective-permute-start(bf16[4,4,2,4,8,128]{5,4,3,2,1,0:T(8,128)(2,1)S(1)} %bitcast.33), channel_id=1, source_target_pairs={{0,32},{16,48},{32,0},{48,16},{64,96},{80,112},{96,64},{112,80},{1... | collective-permute-start | bytes 786440 | tf_op jit(solution)/shard_map/ppermute | solution.py:711
  107.3 12.7 %collective-permute-start.14 = (bf16[4,4,2,4,8,128]{5,4,3,2,1,0:T(8,128)(2,1)S(1)}, bf16[4,4,2,4,8,128]{5,4,3,2,1,0:T(8,128)(2,1)}, u32[]{:S(2)}, u32[]{:S(2)}) collective-permute-start(bf16[4,4,2,4,8,128]{5,4,3,2,1,0:T(8,128)(2,1)S(1)} %bitcast.34), channel_id=1, source_target_pairs={{0,48},{16,32},{32,16},{48,0},{64,112},{80,96},{96,80},{112,64},{1... | collective-permute-start | bytes 786440 | tf_op jit(solution)/shard_map/ppermute | solution.py:711
  109.8 0.7 copy-start.2
  109.9 9.0 %collective-permute-start.16 = (bf16[3,192,128]{2,1,0:T(8,128)(2,1)}, bf16[3,192,128]{2,1,0:T(8,128)(2,1)S(1)}, u32[]{:S(2)}, u32[]{:S(2)}) collective-permute-start(bf16[3,192,128]{2,1,0:T(8,128)(2,1)} %join.4), channel_id=1, source_target_pairs={{0,2},{1,3},{2,0},{3,1},{4,6},{5,7},{6,4},{7,5},{8,10},{9,11},{10,... | collective-permute-start | bytes 442376 | tf_op jit(solution)/shard_map/ppermute | solution.py:32
  110.6 25.2 %all-to-all-start.3 = ((bf16[16,8,8,128]{3,2,1,0:T(8,128)(2,1)}), bf16[16,8,8,128]{3,2,1,0:T(8,128)(2,1)S(1)}, u32[]{:S(2)}, u32[]{:S(2)}) async-start(bf16[16,8,8,128]{3,2,1,0:T(8,128)(2,1)} %bitcast.38), calls=%async_computation.3 | async-start | bytes 524288 | tf_op jit(solution)/shard_map/all_to_all | solution.py:715
  118.8 1.2 copy-start.11
  118.8 1.2 copy-start.10
  125.5 2.5 %collective-permute-start.20 = (bf16[2,3,192,128]{3,2,1,0:T(8,128)(2,1)}, bf16[2,3,192,128]{3,2,1,0:T(8,128)(2,1)S(1)}, u32[]{:S(2)}, u32[]{:S(2)}) collective-permute-start(bf16[2,3,192,128]{3,2,1,0:T(8,128)(2,1)} %get-tuple-element.35), channel_id=1, source_target_pairs={{0,1},{1,0},{2,3},{3,2},{4,5},{5,4},{6,7},{7,6},{8,9},{9,8},{10,11... | collective-permute-start | bytes 884744 | tf_op jit(solution)/shard_map/ppermute | solution.py:32
  128.1 0.7 copy-start.8
  130.5 5.3 %collective-permute-start.21 = (bf16[3,192,128]{2,1,0:T(8,128)(2,1)}, bf16[3,192,128]{2,1,0:T(8,128)(2,1)S(1)}, u32[]{:S(2)}, u32[]{:S(2)}) collective-permute-start(bf16[3,192,128]{2,1,0:T(8,128)(2,1)} %join.5), channel_id=1, source_target_pairs={{0,2},{1,3},{2,0},{3,1},{4,6},{5,7},{6,4},{7,5},{8,10},{9,11},{10,... | collective-permute-start | bytes 442376 | tf_op jit(solution)/shard_map/ppermute | solution.py:32
  135.8 0.7 copy-start.24
  135.8 0.8 copy-start.1
  152.5 3.4 %collective-permute-start.25 = (bf16[3,192,128]{2,1,0:T(8,128)(2,1)}, bf16[3,192,128]{2,1,0:T(8,128)(2,1)S(1)}, u32[]{:S(2)}, u32[]{:S(2)}) collective-permute-start(bf16[3,192,128]{2,1,0:T(8,128)(2,1)} %get-tuple-element.41.refs_1_), channel_id=1, source_target_pairs={{0,1},{1,0},{2,3},{3,2},{4,5},{5,4},{6,7},{7,6},{8,9},{9,8},{10,11... | collective-permute-start | bytes 442376 | tf_op jit(solution)/shard_map/ppermute | solution.py:32
  152.7 5.8 %collective-permute-start.26 = (bf16[3,192,128]{2,1,0:T(8,128)(2,1)}, bf16[3,192,128]{2,1,0:T(8,128)(2,1)S(1)}, u32[]{:S(2)}, u32[]{:S(2)}) collective-permute-start(bf16[3,192,128]{2,1,0:T(8,128)(2,1)} %get-tuple-element.41.refs_1_), channel_id=1, source_target_pairs={{0,2},{1,3},{2,0},{3,1},{4,6},{5,7},{6,4},{7,5},{8,10},{9,11},{10,... | collective-permute-start | bytes 442376 | tf_op jit(solution)/shard_map/ppermute | solution.py:32
  153.7 8.3 %collective-permute-start.27 = (bf16[3,192,128]{2,1,0:T(8,128)(2,1)}, bf16[3,192,128]{2,1,0:T(8,128)(2,1)}, u32[]{:S(2)}, u32[]{:S(2)}) collective-permute-start(bf16[3,192,128]{2,1,0:T(8,128)(2,1)} %get-tuple-element.41.refs_1_), channel_id=1, source_target_pairs={{0,3},{1,2},{2,1},{3,0},{4,7},{5,6},{6,5},{7,4},{8,11},{9,10},{10,... | collective-permute-start | bytes 442376 | tf_op jit(solution)/shard_map/ppermute | solution.py:32
  154.7 15.6 %collective-permute-start.22 = (bf16[1168,128]{1,0:T(8,128)(2,1)}, bf16[1168,128]{1,0:T(8,128)(2,1)S(1)}, u32[]{:S(2)}, u32[]{:S(2)}) collective-permute-start(bf16[1168,128]{1,0:T(8,128)(2,1)} %get-tuple-element.40.kv0), channel_id=1, source_target_pairs={{0,4},{4,0},{8,12},{12,8},{1,5},{5,1},{9,13},{13,9},{2,6},{6,2},{1... | collective-permute-start | bytes 897032 | tf_op jit(solution)/shard_map/ppermute | solution.py:32
  154.7 15.7 %collective-permute-start.23 = (bf16[1168,128]{1,0:T(8,128)(2,1)}, bf16[1168,128]{1,0:T(8,128)(2,1)S(1)}, u32[]{:S(2)}, u32[]{:S(2)}) collective-permute-start(bf16[1168,128]{1,0:T(8,128)(2,1)} %get-tuple-element.40.kv0), channel_id=1, source_target_pairs={{0,8},{4,12},{8,0},{12,4},{1,9},{5,13},{9,1},{13,5},{2,10},{6,14},... | collective-permute-start | bytes 897032 | tf_op jit(solution)/shard_map/ppermute | solution.py:32
  155.9 6.1 %copy-start.20 = (bf16[3,192,128]{2,1,0:T(8,128)(2,1)}, bf16[3,192,128]{2,1,0:T(8,128)(2,1)S(1)}, u32[]{:S(2)}) copy-start(bf16[3,192,128]{2,1,0:T(8,128)(2,1)S(1)} %collective-permute-done.25.refs_2_) | copy-start | bytes 442372
  155.9 16.2 %collective-permute-start.24 = (bf16[1168,128]{1,0:T(8,128)(2,1)}, bf16[1168,128]{1,0:T(8,128)(2,1)}, u32[]{:S(2)}, u32[]{:S(2)}) collective-permute-start(bf16[1168,128]{1,0:T(8,128)(2,1)} %get-tuple-element.40.kv0), channel_id=1, source_target_pairs={{0,12},{4,8},{8,4},{12,0},{1,13},{5,9},{9,5},{13,1},{2,14},{6,10},... | collective-permute-start | bytes 897032 | tf_op jit(solution)/shard_map/ppermute | solution.py:32
  158.5 3.5 %copy-start.21 = (bf16[3,192,128]{2,1,0:T(8,128)(2,1)}, bf16[3,192,128]{2,1,0:T(8,128)(2,1)S(1)}, u32[]{:S(2)}) copy-start(bf16[3,192,128]{2,1,0:T(8,128)(2,1)S(1)} %collective-permute-done.26.refs_3_) | copy-start | bytes 442372
  166.1 1.8 collective-permute-start.28
  167.9 0.7 copy-start.6
  170.3 8.6 %copy-start.15 = (bf16[3,192,128]{2,1,0:T(8,128)(2,1)S(1)}, bf16[3,192,128]{2,1,0:T(8,128)(2,1)}, u32[]{:S(2)}) copy-start(bf16[3,192,128]{2,1,0:T(8,128)(2,1)} %join.6.refs_1_) | copy-start | bytes 442372
  170.3 1.8 copy-start.18
  170.3 1.8 copy-start.19
  177.7 2.7 %collective-permute-start.29 = (bf16[2,3,192,128]{3,2,1,0:T(8,128)(2,1)}, bf16[2,3,192,128]{3,2,1,0:T(8,128)(2,1)S(1)}, u32[]{:S(2)}, u32[]{:S(2)}) collective-permute-start(bf16[2,3,192,128]{3,2,1,0:T(8,128)(2,1)} %get-tuple-element.45), channel_id=1, source_target_pairs={{0,1},{1,0},{2,3},{3,2},{4,5},{5,4},{6,7},{7,6},{8,9},{9,8},{10,11... | collective-permute-start | bytes 884744 | tf_op jit(solution)/shard_map/ppermute | solution.py:32
  178.9 6.6 %collective-permute-start.31 = (bf16[3,192,128]{2,1,0:T(8,128)(2,1)S(1)}, bf16[3,192,128]{2,1,0:T(8,128)(2,1)S(1)}, u32[]{:S(2)}, u32[]{:S(2)}) collective-permute-start(bf16[3,192,128]{2,1,0:T(8,128)(2,1)S(1)} %copy-done.15), channel_id=1, source_target_pairs={{0,2},{1,3},{2,0},{3,1},{4,6},{5,7},{6,4},{7,5},{8,10},{9,11},{10,... | collective-permute-start | bytes 442376 | tf_op jit(solution)/shard_map/ppermute | solution.py:32
  180.3 0.7 copy-start.7
  182.8 5.3 %collective-permute-start.30 = (bf16[3,192,128]{2,1,0:T(8,128)(2,1)}, bf16[3,192,128]{2,1,0:T(8,128)(2,1)S(1)}, u32[]{:S(2)}, u32[]{:S(2)}) collective-permute-start(bf16[3,192,128]{2,1,0:T(8,128)(2,1)} %join.7), channel_id=1, source_target_pairs={{0,2},{1,3},{2,0},{3,1},{4,6},{5,7},{6,4},{7,5},{8,10},{9,11},{10,... | collective-permute-start | bytes 442376 | tf_op jit(solution)/shard_map/ppermute | solution.py:32
  185.5 2.5 %copy-start.22 = (bf16[3,192,128]{2,1,0:T(8,128)(2,1)}, bf16[3,192,128]{2,1,0:T(8,128)(2,1)S(1)}, u32[]{:S(2)}) copy-start(bf16[3,192,128]{2,1,0:T(8,128)(2,1)S(1)} %collective-permute-done.31.far_t) | copy-start | bytes 442372
  188.0 0.7 copy-start.23

commit v3 on v2

--- a/solution.py
+++ b/solution.py
@@ -15,7 +15,7 @@
 EPS = 1e-05
 MASK_FILL = 1000000000.0
 MIB = 1024 * 1024
-CLAIM = 63
+CLAIM = 64 * MIB - 64 * 1024
 MASK_ROWS = 16
 NEAR = 4
 
@@ -48,7 +48,7 @@
         in_specs=in_specs,
         out_specs=jax.tree.map(lambda o: whole(o.shape), out_shape),
         scratch_shapes=scratch,
-        compiler_params=pltpu.CompilerParams(vmem_limit_bytes=CLAIM * MIB),
+        compiler_params=pltpu.CompilerParams(vmem_limit_bytes=CLAIM),
         cost_estimate=expected(micros),
         name=name,
     )(*args)
@@ -101,8 +101,8 @@
                 trans[s] = (gain * value + shift).astype(jnp.bfloat16)
 
 
-def first_project_kernel(me_ref, block0, block1, block2, block3, *refs):
-    stack_features((block0, block1, block2, block3), refs[-1], me_ref[0])
+def first_project_kernel(gathered, *refs):
+    stack_gathered(gathered, refs[-1])
     project_full(*refs)
 
 
@@ -149,8 +149,8 @@
         return local_call(
             first_project_kernel,
             (small, small, joint),
-            [SCALAR] + [whole(b.shape) for b in blocks] + specs,
-            [me, *blocks, *args],
+            [whole(blocks[0].shape)] + specs,
+            [*blocks, *args],
             [full],
             3.0,
             "first_project",
@@ -207,7 +207,8 @@
 
 
 def transition_kernel(count, me_ref, *refs):
-    up, down, keep, give, full, total = refs[count:]
+    up, down = refs[count : count + 2]
+    keep, give, full, total = refs[-4:]
     if count > 1:
         stack_features(refs[:count], full, me_ref[0])
     else:
@@ -220,7 +221,7 @@
     hand_out(total, me_ref[0], keep, give)
 
 
-def transition(blocks, me, up, down, layer, col_size):
+def transition(blocks, me, up, down, layer, col_size, others):
     samples, width, tokens = blocks[0].shape[-3:]
     depth, hidden = up.shape[2:]
     return local_call(
@@ -231,8 +232,9 @@
         ),
         [SCALAR]
         + [whole(b.shape) for b in blocks]
-        + [layer_block(up.shape, 0, layer), layer_block(down.shape, 0, layer)],
-        [me, *blocks, up, down],
+        + [layer_block(up.shape, 0, layer), layer_block(down.shape, 0, layer)]
+        + [UNREAD] * len(others),
+        [me, *blocks, up, down, *others],
         [
             pltpu.VMEM((depth, samples * tokens), jnp.bfloat16),
             pltpu.VMEM((depth, samples * tokens), jnp.float32),
@@ -242,10 +244,10 @@
     )
 
 
-def attention_kernel(me_ref, queries, gates, kv0, kv1, kv2, kv3, bias0, bias1, bias2, bias3, *refs):
+def attention_kernel(row_ref, samp_ref, col_ref, queries, gates, kv0, kv1, kv2, kv3, bias0, bias1, bias2, bias3, *refs):
     out_w, keep, give, full, total, added = refs[0], *refs[-5:]
     pieces, biases = (kv0, kv1, kv2, kv3), (bias0, bias1, bias2, bias3)
-    row_at, near_at, col_at = me_ref[0], me_ref[1], me_ref[2]
+    row_at, near_at, col_at = row_ref[0], lax.rem(samp_ref[0], NEAR), col_ref[0]
     samples, width, tokens = queries.shape
     far, cols, _, heads, count, keys = bias0.shape
     for k, bias in enumerate(biases):
@@ -265,24 +267,21 @@
         query = jnp.transpose(queries[s].astype(jnp.float32))
         key = jnp.concatenate([kv[2 * s * width : (2 * s + 1) * width] for kv in pieces], 1)
         value = jnp.concatenate([kv[(2 * s + 1) * width : (2 * s + 2) * width] for kv in pieces], 1)
-        kept = jnp.zeros((tokens, width), jnp.float32)
-        for h in range(heads):
-            mine = lane == h
-            scores = jnp.dot(
-                jnp.where(mine, query, 0.0).astype(jnp.bfloat16),
-                key,
-                preferred_element_type=jnp.float32,
-            )
-            scores = scores * scale + added[h] + mask_add
-            exps = jnp.exp(scores - jnp.max(scores, axis=1, keepdims=True))
-            norm = jnp.sum(exps, axis=1, keepdims=True)
-            product = lax.dot_general(
-                exps.astype(jnp.bfloat16),
-                value,
-                (((1,), (1,)), ((), ())),
-                preferred_element_type=jnp.float32,
-            )
-            kept = jnp.where(mine, product / norm, kept)
+        stacked = jnp.concatenate([jnp.where(lane == h, query, 0.0) for h in range(heads)], 0)
+        scores = jnp.dot(stacked.astype(jnp.bfloat16), key, preferred_element_type=jnp.float32)
+        scores = scores * scale + added[...].reshape(scores.shape) + mask_add
+        exps = jnp.exp(scores - jnp.max(scores, axis=1, keepdims=True))
+        norm = jnp.sum(exps, axis=1, keepdims=True)
+        product = lax.dot_general(
+            exps.astype(jnp.bfloat16),
+            value,
+            (((1,), (1,)), ((), ())),
+            preferred_element_type=jnp.float32,
+        )
+        product = product / norm
+        kept = product[:tokens]
+        for h in range(1, heads):
+            kept = jnp.where(lane == h, product[h * tokens : (h + 1) * tokens], kept)
         gate = jax.nn.sigmoid(gates[s].astype(jnp.float32))
         full[:, s * tokens : (s + 1) * tokens] = (gate * jnp.transpose(kept)).astype(jnp.bfloat16)
     total[...] = lax.dot_general(
@@ -295,19 +294,19 @@
     samples, width, tokens = queries.shape
     heads = biases[0].shape[3]
     parts = out_w.shape[2] // width
-    args = [me, queries, gates, *pieces]
+    args = [queries, gates, *pieces]
     return local_call(
         attention_kernel,
         tuple(
             jax.ShapeDtypeStruct((parts // 2,) + queries.shape, dtype)
             for dtype in (jnp.float32, jnp.bfloat16)
         ),
-        [SCALAR]
-        + [whole(a.shape) for a in args[1:]]
+        [SCALAR] * len(me)
+        + [whole(a.shape) for a in args]
         + [layer_block(b.shape, 2, layer) for b in biases]
         + [layer_block(out_w.shape, 0, layer)]
         + [UNREAD] * len(others),
-        [*args, *biases, out_w, *others],
+        [*me, *args, *biases, out_w, *others],
         [
             pltpu.VMEM((width, samples * tokens), jnp.bfloat16),
             pltpu.VMEM((parts * width, samples * tokens), jnp.float32),
@@ -466,8 +465,17 @@
                 preferred_element_type=jnp.float32,
             )
 
-    value = pair[...].astype(jnp.float32)
-    normed[...] = channel_norm(value, 0).reshape(channels * rows, keys)
+    def over_channels(term):
+        lanes = [term(c) for c in range(4)]
+        for c in range(4, channels):
+            lanes[c % 4] = lanes[c % 4] + term(c)
+        return (lanes[0] + lanes[1] + (lanes[2] + lanes[3])) / channels
+
+    mean_value = over_channels(lambda c: pair[c].astype(jnp.float32))
+    spread = over_channels(lambda c: jnp.square(pair[c].astype(jnp.float32) - mean_value))
+    scale = lax.rsqrt(spread + EPS)
+    for c in range(channels):
+        normed[c * rows : (c + 1) * rows] = (pair[c].astype(jnp.float32) - mean_value) * scale
     weights = weight[...].astype(jnp.bfloat16)
     for i in range(0, rows, 2):
         two = [normed[pl.ds(i + e, channels, stride=rows), :] for e in (0, 1)]
@@ -516,7 +524,7 @@
             pltpu.VMEM((share * height, keys), jnp.float32),
             pltpu.VMEM((share * height, keys), jnp.float32),
         ],
-        compiler_params=pltpu.CompilerParams(vmem_limit_bytes=CLAIM * MIB),
+        compiler_params=pltpu.CompilerParams(vmem_limit_bytes=CLAIM),
         cost_estimate=expected(9.7),
         name="pair_project",
     )(me, pair_in, tri_weight, *others)
@@ -589,7 +597,7 @@
             ],
         ),
         out_shape=out_shape,
-        compiler_params=pltpu.CompilerParams(vmem_limit_bytes=CLAIM * MIB),
+        compiler_params=pltpu.CompilerParams(vmem_limit_bytes=CLAIM),
         cost_estimate=expected(2.8),
         name="pair_update",
     )(me, came, pair_in, tri_weight, out_weight, bias_w, *others)
@@ -667,15 +675,15 @@
         single, time_embed, time_weight, mod_w, state, sums, [to_send]
     )
 
-    attn_full = swap_all(attn_local, "col")
-    triangle = triangle_sums(came, attn_full[1:])
+    attn_full = lax.all_gather(attn_local, "col", axis=0)
+    triangle = triangle_sums(came, [attn_full])
     shared = swap_all(shared, "col")
     triangle = triangle.reshape(samp_size * group, cell_rows, pair_cols)
     triangle = lax.all_to_all(triangle, ("samp", "row", "col"), 0, 0, tiled=True)
     triangle = triangle.reshape(channels, own_rows, pair_cols)
     mask_row = token_mask[None]
     queries, gates, both = project(
-        attn_full, col_at, query_w, key_w, value_gate_w, mask_row, 0
+        [attn_full], col_at, query_w, key_w, value_gate_w, mask_row, 0
     )
     pieces = swap_all(both, "row")
 
@@ -713,9 +721,9 @@
     ]
     pair_back = after(pair_out, [biases[1]]).reshape(samp_size, share, own_rows, pair_cols)
     pair_back = lax.all_to_all(pair_back, "samp", 0, 0, tiled=True)
-    trans = transition(trans_full, col_at, up_weight, down_weight, 0, col_size)
+    trans = transition(trans_full, col_at, up_weight, down_weight, 0, col_size, [])
     trans_sum, sent = sum_parts(*trans)
-    seat = jnp.concatenate([row_at, samp_at % NEAR, col_at])
+    seat = [row_at, samp_at, col_at]
 
     for layer in range(blocks):
         if layer > 0:
@@ -724,7 +732,9 @@
             )
             pieces = swap_all(both, "row")
             trans_full = swap_all(trans_local, "col")
-            trans = transition(trans_full, col_at, up_weight, down_weight, layer, col_size)
+            trans = transition(
+                trans_full, col_at, up_weight, down_weight, layer, col_size, pieces[1:2]
+            )
             trans_sum, sent = sum_parts(*trans)
         others = [sent] if layer else [trans_sum[2], *shared[1:]]
         attended = attention(

time: 192 us -> 184 us (0.958)
  blocking collectives: 9.63 us -> 20.9 us
  waiting for transfers between devices: 46.3 us -> 37.9 us
  local copies, waits for them, and re-layouts: 6.54 us -> 0 us
  Pallas kernels: 58.3 us -> 55.9 us
    all_gather x0 -> x1, blocking collectives: none -> 11.8 us  [body(): attn_full = lax.all_gather(attn_local, 'col', axis=0)]
    ppermute x29 -> x26, waiting for transfers between devices: 38 us -> 28.3 us  [swap(): return lax.ppermute(value, axis, [(k, k ^ flip) for k in range(size)])]
    unnamed x50 -> x0, local copies, waits for them, and re-layouts: 6.54 us -> none
    ppermute x29 -> x26, starting transfers between devices: 31.3 us -> 28.4 us  [swap(): return lax.ppermute(value, axis, [(k, k ^ flip) for k in range(size)])]
    pallas_call x15, Pallas kernels: 45.7 us -> 43.7 us  [local_call(): pl.pallas_call(kernel, grid=(1,), out_shape=out_shape, in_specs=in_specs,...]
  transfers between devices with their start and end apart: 36 -> 33, of which waited for: 17 -> 15; matrix products, arithmetic and copies ran while one was open for 1% -> 1% of each run, Pallas kernels for 15% -> 16%
where the time goes in v3:
time: 184 us; the launch traced here: 183 us
  starting transfers between devices  64.5 us (35%)
  Pallas kernels  55.9 us (30%)
  waiting for transfers between devices  37.9 us (21%)
  blocking collectives  20.9 us (11%)
  other arithmetic  2.96 us (2%)
    pallas_call x15, Pallas kernels, local_call(): pl.pallas_call(kernel, grid=(1,), out_shape=out_shape, in_specs=in_specs,...  43.7 us
    ppermute x26, starting transfers between devices, swap(): return lax.ppermute(value, axis, [(k, k ^ flip) for k in range(size)])  28.4 us
    ppermute x26, waiting for transfers between devices, swap(): return lax.ppermute(value, axis, [(k, k ^ flip) for k in range(size)])  28.3 us
    all_to_all x1, starting transfers between devices, body(): lax.all_to_all(triangle, ('samp', 'row', 'col'), 0, 0, tiled=True)  14.6 us
    all_gather x1, blocking collectives, body(): attn_full = lax.all_gather(attn_local, 'col', axis=0)  11.8 us
    pallas_call x1, Pallas kernels, pair_project(): pl.pallas_call(pair_project_kernel, grid=(height // rows,), out_shape=out...  9.22 us
    all_gather x1, blocking collectives, body(): state = lax.all_gather(state, 'col', axis=0)  9.06 us
    all_to_all x1, starting transfers between devices, body(): pair_back = lax.all_to_all(pair_back, 'samp', 0, 0, tiled=True)  8.24 us
  transfers between devices with their start and end apart: 33, of which 15 were waited for; matrix products, arithmetic and copies ran while one was open for 1% of the time, Pallas kernels for 16%

profile of v3, /device:TPU:1, one launch (start us, length us, event | category | flops | bytes accessed | tf_op | source)
XLA Modules:
  0.0 182.9 jit_solution(5107729681395715636)
XLA Ops:
  0.6 1.0 convert_reduce_fusion
  1.6 3.3 %collective-permute-start = (f32[2,3,128]{2,1,0:T(4,128)S(1)}, f32[2,3,128]{2,1,0:T(4,128)S(1)}, u32[]{:S(2)}, u32[]{:S(2)}) collective-permute-start(f32[2,3,128]{2,1,0:T(4,128)S(1)} %pad_maximum_fusion), channel_id=1, source_target_pairs={{0,1},{1,0},{2,3},{3,2},{4,5},{5,4},{6,7},{7,6},{8,9},{9,8},{10,11... | collective-permute-start | bytes 9224 | tf_op jit(solution)/shard_map/ppermute | solution.py:32
  4.9 1.7 collective-permute-start.2
  6.7 0.7 log_multiply_fusion
  7.5 0.6 pad_maximum_fusion.1.refs_1_.time_embed
  8.2 0.6 add_add_fusion.refs_0_.sums
  8.8 9.2 %pair_project.1.refs_0_ = bf16[16,192,128]{2,1,0:T(8,128)(2,1)} custom-call(s32[1]{0:T(128)} %bitcast.me_ref.samp_ref, bf16[128,128,128]{2,1,0:T(8,128)(2,1)} %own.1, bf16[5,128,128]{2,1,0:T(8,128)(2,1)} %gate_w.1, f32[2,3,128]{2,1,0:T(4,128)} %add_add_fusion.refs_0_.sums, bf16[3,256]{1,0:T(4,128)(2,1)} %pad_maximum_fusion.1.refs_1_.time_embed), custom_call_target="tpu_custom_call" | custom-call | bytes 35793000 | tf_op jit(solution)/shard_map/pair_project/pallas_call | solution.py:510
  18.1 4.5 %all-to-all-start = ((bf16[16,192,128]{2,1,0:T(8,128)(2,1)}), bf16[16,192,128]{2,1,0:T(8,128)(2,1)}, u32[]{:S(2)}, u32[]{:S(2)}) async-start(bf16[16,192,128]{2,1,0:T(8,128)(2,1)} %pair_project.1.refs_0_), calls=%async_computation | async-start | bytes 1572864 | tf_op jit(solution)/shard_map/all_to_all | solution.py:671
  22.6 4.2 %modulate.1 = (bf16[3,192,128]{2,1,0:T(8,128)(2,1)}, bf16[3,192,128]{2,1,0:T(8,128)(2,1)}, bf16[4,3,192,128]{3,2,1,0:T(8,128)(2,1)}, bf16[2,3,192,128]{3,2,1,0:T(8,128)(2,1)}, bf16[2,3,192,128]{3,2,1,0:T(8,128)(2,1)}) custom-call(bf16[128,384]{1,0:T(8,128)(2,1)} %single.1, bf16[3,256]{1,0:T(4,128)(2,1)} %pad_maximum_fusion.1.refs_1_.time_embed, ...), custom_call_target="tpu_custom_call" | custom-call | bytes 16605000 | tf_op jit(solution)/shard_map/modulate/pallas_call | solution.py:44
  26.8 11.8 %all-gather = bf16[12,192,128]{2,1,0:T(8,128)(2,1)} all-gather(bf16[3,192,128]{2,1,0:T(8,128)(2,1)} %get-tuple-element.24), channel_id=2, replica_groups=mesh['samp'=16,'row'=4,'col'=4] {'col'}, dimensions={0}, use_global_device_ids=true | all-gather | bytes 737280 | tf_op jit(solution)/shard_map/all_gather | solution.py:678
  38.6 2.2 %triangle_sums.1 = bf16[8,2,4,2,8,128]{5,4,3,2,1,0:T(8,128)(2,1)} custom-call(bf16[4,4,192,128]{3,2,1,0:T(8,128)(2,1)} %bitcast.4.came, bf16[4,3,192,128]{3,2,1,0:T(8,128)(2,1)} %bitcast.25), custom_call_target="tpu_custom_call" | custom-call | bytes 8118000 | tf_op jit(solution)/shard_map/triangle_sums/pallas_call | solution.py:44
  40.8 14.6 %all-to-all-start.1 = ((bf16[256,4,128]{2,1,0:T(4,128)(2,1)}), bf16[256,4,128]{2,1,0:T(4,128)(2,1)}, u32[]{:S(2)}, u32[]{:S(2)}) async-start(bf16[256,4,128]{2,1,0:T(4,128)(2,1)} %bitcast.36), calls=%async_computation.1 | async-start | bytes 524288 | tf_op jit(solution)/shard_map/all_to_all | solution.py:682
  55.4 2.3 %collective-permute-start.3 = (bf16[3,192,128]{2,1,0:T(8,128)(2,1)}, bf16[3,192,128]{2,1,0:T(8,128)(2,1)}, u32[]{:S(2)}, u32[]{:S(2)}) collective-permute-start(bf16[3,192,128]{2,1,0:T(8,128)(2,1)} %get-tuple-element.26.refs_1_), channel_id=1, source_target_pairs={{0,1},{1,0},{2,3},{3,2},{4,5},{5,4},{6,7},{7,6},{8,9},{9,8},{10,11... | collective-permute-start | bytes 442376 | tf_op jit(solution)/shard_map/ppermute | solution.py:32
  57.7 1.7 collective-permute-start.5
  59.4 3.0 %first_project.1 = (bf16[3,192,128]{2,1,0:T(8,128)(2,1)}, bf16[3,192,128]{2,1,0:T(8,128)(2,1)}, bf16[1168,128]{1,0:T(8,128)(2,1)}) custom-call(bf16[4,3,192,128]{3,2,1,0:T(8,128)(2,1)} %bitcast.26, bf16[2,192,768]{2,1,0:T(8,128)(2,1)} %bitcast.30, bf16[2,192,768]{2,1,0:T(8,128)(2,1)} %bitcast.32, bf16[2,2,192,768]{3,2,1,0:T(8,128)(2,1)} %bitcast.27, ...), custom_call_target="tpu_custom_call" | custom-call | bytes 11070000 | tf_op jit(solution)/shard_map/first_project/pallas_call | solution.py:44
  62.4 2.0 %collective-permute-done.4.refs_2_.refs_3_ = bf16[3,192,128]{2,1,0:T(8,128)(2,1)} collective-permute-done((bf16[3,192,128]{2,1,0:T(8,128)(2,1)}, bf16[3,192,128]{2,1,0:T(8,128)(2,1)}, u32[]{:S(2)}, u32[]{:S(2)}) %collective-permute-start.4) | collective-permute-done | bytes 147488 | tf_op jit(solution)/shard_map/ppermute | solution.py:32
  64.5 3.3 %collective-permute-done.5.refs_3_.refs_4_ = bf16[3,192,128]{2,1,0:T(8,128)(2,1)} collective-permute-done((bf16[3,192,128]{2,1,0:T(8,128)(2,1)}, bf16[3,192,128]{2,1,0:T(8,128)(2,1)}, u32[]{:S(2)}, u32[]{:S(2)}) %collective-permute-start.5) | collective-permute-done | bytes 147488 | tf_op jit(solution)/shard_map/ppermute | solution.py:32
  67.7 2.9 %all-to-all-done.1 = bf16[256,4,128]{2,1,0:T(4,128)(2,1)} async-done(((bf16[256,4,128]{2,1,0:T(4,128)(2,1)}), bf16[256,4,128]{2,1,0:T(4,128)(2,1)}, u32[]{:S(2)}, u32[]{:S(2)}) %all-to-all-start.1) | async-done | bytes 262176 | tf_op jit(solution)/shard_map/all_to_all | solution.py:682
  70.6 2.9 %pair_update.1 = (bf16[128,8,128]{2,1,0:T(8,128)(2,1)}, bf16[4,4,2,4,8,128]{5,4,3,2,1,0:T(8,128)(2,1)}) custom-call(s32[1]{0:T(128)} %bitcast.me_ref.samp_ref, bf16[128,8,128]{2,1,0:T(8,128)(2,1)} %bitcast.8.came, bf16[128,128,128]{2,1,0:T(8,128)(2,1)} %own.1, bf16[5,128,128]{2,1,0:T(8,128)(2,1)} %gate_w.1, bf16[128,128]{1,0:T(8,128)(2,1)} %out_w.1, ...), custom_call_target="tpu_custom_call" | custom-call | bytes 10332000 | tf_op jit(solution)/shard_map/pair_update/pallas_call | solution.py:579
  73.5 4.3 %all-to-all-start.2 = ((bf16[16,2,4,8,128]{4,3,2,1,0:T(8,128)(2,1)}), bf16[16,2,4,8,128]{4,3,2,1,0:T(8,128)(2,1)}, u32[]{:S(2)}, u32[]{:S(2)}) async-start(bf16[16,2,4,8,128]{4,3,2,1,0:T(8,128)(2,1)} %bitcast.38), calls=%async_computation.2 | async-start | bytes 524288 | tf_op jit(solution)/shard_map/all_to_all | solution.py:707
  77.9 0.4 collective-permute-start.14
  78.2 1.4 collective-permute-start.15
  79.6 0.4 collective-permute-start.16
  80.0 0.9 collective-permute-start.7
  80.9 4.0 %transition.2 = (f32[2,3,192,128]{3,2,1,0:T(8,128)}, bf16[2,3,192,128]{3,2,1,0:T(8,128)(2,1)}) custom-call(s32[1]{0:T(128)} %bitcast.19.refs_0_.col_ref.me_ref, bf16[3,192,128]{2,1,0:T(8,128)(2,1)} %get-tuple-element.26.refs_1_, bf16[3,192,128]{2,1,0:T(8,128)(2,1)} %collective-permute-done.3.refs_1_.refs_2_, ...), custom_call_target="tpu_custom_call" | custom-call | bytes 14022000 | tf_op jit(solution)/shard_map/transition/pallas_call | solution.py:44
  84.9 0.3 collective-permute-start.12
  85.3 4.8 %all-to-all-done.2 = bf16[16,2,4,8,128]{4,3,2,1,0:T(8,128)(2,1)} async-done(((bf16[16,2,4,8,128]{4,3,2,1,0:T(8,128)(2,1)}), bf16[16,2,4,8,128]{4,3,2,1,0:T(8,128)(2,1)}, u32[]{:S(2)}, u32[]{:S(2)}) %all-to-all-start.2) | async-done | bytes 262176 | tf_op jit(solution)/shard_map/all_to_all | solution.py:707
  90.0 0.8 collective-permute-start.6
  90.8 1.4 collective-permute-done.15.refs_3_.pair2
  92.3 2.4 %collective-permute-start.8 = (bf16[1168,128]{1,0:T(8,128)(2,1)}, bf16[1168,128]{1,0:T(8,128)(2,1)}, u32[]{:S(2)}, u32[]{:S(2)}) collective-permute-start(bf16[1168,128]{1,0:T(8,128)(2,1)} %get-tuple-element.25.refs_0_.kv0), channel_id=1, source_target_pairs={{0,8},{4,12},{8,0},{12,4},{1,9},{5,13},{9,1},{13,5},{2,10},{6,14},... | collective-permute-start | bytes 897032 | tf_op jit(solution)/shard_map/ppermute | solution.py:32
  94.7 4.4 %collective-permute-done.16.refs_4_.pair3 = bf16[2,3,192,128]{3,2,1,0:T(8,128)(2,1)} collective-permute-done((bf16[2,3,192,128]{3,2,1,0:T(8,128)(2,1)}, bf16[2,3,192,128]{3,2,1,0:T(8,128)(2,1)}, u32[]{:S(2)}, u32[]{:S(2)}) %collective-permute-start.16) | collective-permute-done | bytes 294944 | tf_op jit(solution)/shard_map/ppermute | solution.py:32
  99.1 2.2 %collective-permute-start.9 = (bf16[1168,128]{1,0:T(8,128)(2,1)}, bf16[1168,128]{1,0:T(8,128)(2,1)}, u32[]{:S(2)}, u32[]{:S(2)}) collective-permute-start(bf16[1168,128]{1,0:T(8,128)(2,1)} %get-tuple-element.25.refs_0_.kv0), channel_id=1, source_target_pairs={{0,12},{4,8},{8,4},{12,0},{1,13},{5,9},{9,5},{13,1},{2,14},{6,10},... | collective-permute-start | bytes 897032 | tf_op jit(solution)/shard_map/ppermute | solution.py:32
  101.3 2.7 %collective-permute-start.10 = (bf16[4,4,2,4,8,128]{5,4,3,2,1,0:T(8,128)(2,1)}, bf16[4,4,2,4,8,128]{5,4,3,2,1,0:T(8,128)(2,1)}, u32[]{:S(2)}, u32[]{:S(2)}) collective-permute-start(bf16[4,4,2,4,8,128]{5,4,3,2,1,0:T(8,128)(2,1)} %bitcast.16.bias0), channel_id=1, source_target_pairs={{0,32},{16,48},{32,0},{48,16},{64,96},{80,112},{96,64},{112,80},{1... | collective-permute-start | bytes 786440 | tf_op jit(solution)/shard_map/ppermute | solution.py:719
  104.0 0.9 collective-permute-start.11
  104.9 1.7 join.4
  106.7 8.2 %all-to-all-start.3 = ((bf16[16,8,8,128]{3,2,1,0:T(8,128)(2,1)}), bf16[16,8,8,128]{3,2,1,0:T(8,128)(2,1)}, u32[]{:S(2)}, u32[]{:S(2)}) async-start(bf16[16,8,8,128]{3,2,1,0:T(8,128)(2,1)} %bitcast.35), calls=%async_computation.3 | async-start | bytes 524288 | tf_op jit(solution)/shard_map/all_to_all | solution.py:723
  115.0 2.0 %collective-permute-done.11.bias3 = bf16[4,4,2,4,8,128]{5,4,3,2,1,0:T(8,128)(2,1)} collective-permute-done((bf16[4,4,2,4,8,128]{5,4,3,2,1,0:T(8,128)(2,1)}, bf16[4,4,2,4,8,128]{5,4,3,2,1,0:T(8,128)(2,1)}, u32[]{:S(2)}, u32[]{:S(2)}) %collective-permute-start.11) | collective-permute-done | bytes 262176 | tf_op jit(solution)/shard_map/ppermute | solution.py:719
  116.9 4.7 %attention.2 = (f32[2,3,192,128]{3,2,1,0:T(8,128)}, bf16[2,3,192,128]{3,2,1,0:T(8,128)(2,1)}) custom-call(s32[1]{0:T(128)} %bitcast.18.row_ref, s32[1]{0:T(128)} %bitcast.me_ref.samp_ref, s32[1]{0:T(128)} %bitcast.19.refs_0_.col_ref.me_ref, bf16[3,192,128]{2,1,0:T(8,128)(2,1)} %get-tuple-element.29.queries, bf16[3,192,128]{2,1,0:T(8,128)(2,1)} %get-tuple-element.30.gates, ...), custom_call_target="tpu_custom_call" | custom-call | bytes 19926000 | tf_op jit(solution)/shard_map/attention/pallas_call | solution.py:44
  121.7 0.5 collective-permute-start.17
  122.2 1.6 collective-permute-done.17.came.came_a
  123.7 1.7 join.5
  125.5 5.3 %collective-permute-done.18.far_a = bf16[3,192,128]{2,1,0:T(8,128)(2,1)} collective-permute-done((bf16[3,192,128]{2,1,0:T(8,128)(2,1)}, bf16[3,192,128]{2,1,0:T(8,128)(2,1)}, u32[]{:S(2)}, u32[]{:S(2)}) %collective-permute-start.18) | collective-permute-done | bytes 147488 | tf_op jit(solution)/shard_map/ppermute | solution.py:32
  130.8 2.2 %finish.2 = bf16[3,192,128]{2,1,0:T(8,128)(2,1)} custom-call(f32[2,3,192,128]{3,2,1,0:T(8,128)} %get-tuple-element.34.keep.keep_a, bf16[2,3,192,128]{3,2,1,0:T(8,128)(2,1)} %collective-permute-done.17.came.came_a, bf16[3,192,128]{2,1,0:T(8,128)(2,1)} %collective-permute-done.18.far_a, f32[2,3,192,128]{3,2,1,0:T(8,128)} %get-tuple-element.31.keep.keep_t, ...), custom_call_target="tpu_custom_call" | custom-call | bytes 7380000 | tf_op jit(solution)/shard_map/finish/pallas_call | solution.py:44
  132.9 9.1 %all-gather.1 = bf16[12,192,128]{2,1,0:T(8,128)(2,1)} all-gather(bf16[3,192,128]{2,1,0:T(8,128)(2,1)} %finish.2), channel_id=3, replica_groups=mesh['samp'=16,'row'=4,'col'=4] {'col'}, dimensions={0}, use_global_device_ids=true | all-gather | bytes 737280 | tf_op jit(solution)/shard_map/all_gather | solution.py:747
  142.0 4.2 %later_project.1 = (bf16[3,192,128]{2,1,0:T(8,128)(2,1)}, bf16[3,192,128]{2,1,0:T(8,128)(2,1)}, bf16[1168,128]{1,0:T(8,128)(2,1)}, bf16[3,192,128]{2,1,0:T(8,128)(2,1)}) custom-call(s32[1]{0:T(128)} %bitcast.19.refs_0_.col_ref.me_ref, bf16[4,3,192,128]{3,2,1,0:T(8,128)(2,1)} %bitcast.29, bf16[2,3,192,128]{3,2,1,0:T(8,128)(2,1)} %get-tuple-element.33.pair0, ...), custom_call_target="tpu_custom_call" | custom-call | bytes 14760000 | tf_op jit(solution)/shard_map/later_project/pallas_call | solution.py:44
  146.2 0.3 collective-permute-start.22
  146.5 1.5 collective-permute-start.23
  148.0 0.4 collective-permute-start.24
  148.4 1.6 collective-permute-start.20
  150.0 2.2 %collective-permute-start.21 = (bf16[1168,128]{1,0:T(8,128)(2,1)}, bf16[1168,128]{1,0:T(8,128)(2,1)}, u32[]{:S(2)}, u32[]{:S(2)}) collective-permute-start(bf16[1168,128]{1,0:T(8,128)(2,1)} %get-tuple-element.40.kv0), channel_id=1, source_target_pairs={{0,12},{4,8},{8,4},{12,0},{1,13},{5,9},{9,5},{13,1},{2,14},{6,10},... | collective-permute-start | bytes 897032 | tf_op jit(solution)/shard_map/ppermute | solution.py:32
  152.2 3.7 %collective-permute-done.24.refs_4_ = bf16[3,192,128]{2,1,0:T(8,128)(2,1)} collective-permute-done((bf16[3,192,128]{2,1,0:T(8,128)(2,1)}, bf16[3,192,128]{2,1,0:T(8,128)(2,1)}, u32[]{:S(2)}, u32[]{:S(2)}) %collective-permute-start.24) | collective-permute-done | bytes 147488 | tf_op jit(solution)/shard_map/ppermute | solution.py:32
  155.9 4.0 %transition.3 = (f32[2,3,192,128]{3,2,1,0:T(8,128)}, bf16[2,3,192,128]{3,2,1,0:T(8,128)(2,1)}) custom-call(s32[1]{0:T(128)} %bitcast.19.refs_0_.col_ref.me_ref, bf16[3,192,128]{2,1,0:T(8,128)(2,1)} %get-tuple-element.41.refs_1_, bf16[3,192,128]{2,1,0:T(8,128)(2,1)} %collective-permute-done.22.refs_2_, bf16[3,192,128]{2,1,0:T(8,128)(2,1)} %collective-permute-done.23.refs_3_, ...), custom_call_target="tpu_custom_call" | custom-call | bytes 14022000 | tf_op jit(solution)/shard_map/transition/pallas_call | solution.py:44
  159.9 0.6 collective-permute-start.25
  160.6 1.6 collective-permute-done.25.came.came_t
  162.1 1.7 join.6.refs_1_
  163.8 2.3 %collective-permute-done.21.kv3 = bf16[1168,128]{1,0:T(8,128)(2,1)} collective-permute-done((bf16[1168,128]{1,0:T(8,128)(2,1)}, bf16[1168,128]{1,0:T(8,128)(2,1)}, u32[]{:S(2)}, u32[]{:S(2)}) %collective-permute-start.21) | collective-permute-done | bytes 299040 | tf_op jit(solution)/shard_map/ppermute | solution.py:32
  166.1 4.7 %attention.3 = (f32[2,3,192,128]{3,2,1,0:T(8,128)}, bf16[2,3,192,128]{3,2,1,0:T(8,128)(2,1)}) custom-call(s32[1]{0:T(128)} %bitcast.18.row_ref, s32[1]{0:T(128)} %bitcast.me_ref.samp_ref, s32[1]{0:T(128)} %bitcast.19.refs_0_.col_ref.me_ref, bf16[3,192,128]{2,1,0:T(8,128)(2,1)} %get-tuple-element.38.queries, bf16[3,192,128]{2,1,0:T(8,128)(2,1)} %get-tuple-element.39.gates, ...), custom_call_target="tpu_custom_call" | custom-call | bytes 19926000 | tf_op jit(solution)/shard_map/attention/pallas_call | solution.py:44
  170.8 1.3 collective-permute-start.26
  172.1 1.4 collective-permute-start.28
  173.7 1.7 join.7
  175.4 1.4 collective-permute-start.27
  176.8 1.7 pair_rows.1
  178.5 2.3 %collective-permute-done.27.far_a = bf16[3,192,128]{2,1,0:T(8,128)(2,1)} collective-permute-done((bf16[3,192,128]{2,1,0:T(8,128)(2,1)}, bf16[3,192,128]{2,1,0:T(8,128)(2,1)}, u32[]{:S(2)}, u32[]{:S(2)}) %collective-permute-start.27) | collective-permute-done | bytes 147488 | tf_op jit(solution)/shard_map/ppermute | solution.py:32
  180.8 2.2 %finish.3 = bf16[3,192,128]{2,1,0:T(8,128)(2,1)} custom-call(f32[2,3,192,128]{3,2,1,0:T(8,128)} %get-tuple-element.44.keep.keep_a, bf16[2,3,192,128]{3,2,1,0:T(8,128)(2,1)} %collective-permute-done.26.came.came_a, bf16[3,192,128]{2,1,0:T(8,128)(2,1)} %collective-permute-done.27.far_a, f32[2,3,192,128]{3,2,1,0:T(8,128)} %get-tuple-element.42.keep.keep_t, ...), custom_call_target="tpu_custom_call" | custom-call | bytes 7380000 | tf_op jit(solution)/shard_map/finish/pallas_call | solution.py:44
  (29 shorter events, 0.7 us)
Async XLA Ops:
  1.6 6.5 %collective-permute-start = (f32[2,3,128]{2,1,0:T(4,128)S(1)}, f32[2,3,128]{2,1,0:T(4,128)S(1)}, u32[]{:S(2)}, u32[]{:S(2)}) collective-permute-start(f32[2,3,128]{2,1,0:T(4,128)S(1)} %pad_maximum_fusion), channel_id=1, source_target_pairs={{0,1},{1,0},{2,3},{3,2},{4,5},{5,4},{6,7},{7,6},{8,9},{9,8},{10,11... | collective-permute-start | bytes 9224 | tf_op jit(solution)/shard_map/ppermute | solution.py:32
  4.9 3.1 %collective-permute-start.1 = (f32[2,3,128]{2,1,0:T(4,128)S(1)}, f32[2,3,128]{2,1,0:T(4,128)S(1)}, u32[]{:S(2)}, u32[]{:S(2)}) collective-permute-start(f32[2,3,128]{2,1,0:T(4,128)S(1)} %pad_maximum_fusion), channel_id=1, source_target_pairs={{0,2},{1,3},{2,0},{3,1},{4,6},{5,7},{6,4},{7,5},{8,10},{9,11},{10,... | collective-permute-start | bytes 9224 | tf_op jit(solution)/shard_map/ppermute | solution.py:32
  4.9 3.3 %collective-permute-start.2 = (f32[2,3,128]{2,1,0:T(4,128)S(1)}, f32[2,3,128]{2,1,0:T(4,128)S(1)}, u32[]{:S(2)}, u32[]{:S(2)}) collective-permute-start(f32[2,3,128]{2,1,0:T(4,128)S(1)} %pad_maximum_fusion), channel_id=1, source_target_pairs={{0,3},{1,2},{2,1},{3,0},{4,7},{5,6},{6,5},{7,4},{8,11},{9,10},{10,... | collective-permute-start | bytes 9224 | tf_op jit(solution)/shard_map/ppermute | solution.py:32
  18.1 20.5 %all-to-all-start = ((bf16[16,192,128]{2,1,0:T(8,128)(2,1)}), bf16[16,192,128]{2,1,0:T(8,128)(2,1)}, u32[]{:S(2)}, u32[]{:S(2)}) async-start(bf16[16,192,128]{2,1,0:T(8,128)(2,1)} %pair_project.1.refs_0_), calls=%async_computation | async-start | bytes 1572864 | tf_op jit(solution)/shard_map/all_to_all | solution.py:671
  40.8 29.9 %all-to-all-start.1 = ((bf16[256,4,128]{2,1,0:T(4,128)(2,1)}), bf16[256,4,128]{2,1,0:T(4,128)(2,1)}, u32[]{:S(2)}, u32[]{:S(2)}) async-start(bf16[256,4,128]{2,1,0:T(4,128)(2,1)} %bitcast.36), calls=%async_computation.1 | async-start | bytes 524288 | tf_op jit(solution)/shard_map/all_to_all | solution.py:682
  55.4 7.0 %collective-permute-start.3 = (bf16[3,192,128]{2,1,0:T(8,128)(2,1)}, bf16[3,192,128]{2,1,0:T(8,128)(2,1)}, u32[]{:S(2)}, u32[]{:S(2)}) collective-permute-start(bf16[3,192,128]{2,1,0:T(8,128)(2,1)} %get-tuple-element.26.refs_1_), channel_id=1, source_target_pairs={{0,1},{1,0},{2,3},{3,2},{4,5},{5,4},{6,7},{7,6},{8,9},{9,8},{10,11... | collective-permute-start | bytes 442376 | tf_op jit(solution)/shard_map/ppermute | solution.py:32
  57.7 6.8 %collective-permute-start.4 = (bf16[3,192,128]{2,1,0:T(8,128)(2,1)}, bf16[3,192,128]{2,1,0:T(8,128)(2,1)}, u32[]{:S(2)}, u32[]{:S(2)}) collective-permute-start(bf16[3,192,128]{2,1,0:T(8,128)(2,1)} %get-tuple-element.26.refs_1_), channel_id=1, source_target_pairs={{0,2},{1,3},{2,0},{3,1},{4,6},{5,7},{6,4},{7,5},{8,10},{9,11},{10,... | collective-permute-start | bytes 442376 | tf_op jit(solution)/shard_map/ppermute | solution.py:32
  57.7 10.0 %collective-permute-start.5 = (bf16[3,192,128]{2,1,0:T(8,128)(2,1)}, bf16[3,192,128]{2,1,0:T(8,128)(2,1)}, u32[]{:S(2)}, u32[]{:S(2)}) collective-permute-start(bf16[3,192,128]{2,1,0:T(8,128)(2,1)} %get-tuple-element.26.refs_1_), channel_id=1, source_target_pairs={{0,3},{1,2},{2,1},{3,0},{4,7},{5,6},{6,5},{7,4},{8,11},{9,10},{10,... | collective-permute-start | bytes 442376 | tf_op jit(solution)/shard_map/ppermute | solution.py:32
  73.5 16.5 %all-to-all-start.2 = ((bf16[16,2,4,8,128]{4,3,2,1,0:T(8,128)(2,1)}), bf16[16,2,4,8,128]{4,3,2,1,0:T(8,128)(2,1)}, u32[]{:S(2)}, u32[]{:S(2)}) async-start(bf16[16,2,4,8,128]{4,3,2,1,0:T(8,128)(2,1)} %bitcast.38), calls=%async_computation.2 | async-start | bytes 524288 | tf_op jit(solution)/shard_map/all_to_all | solution.py:707
  77.9 7.4 %collective-permute-start.14 = (bf16[2,3,192,128]{3,2,1,0:T(8,128)(2,1)}, bf16[2,3,192,128]{3,2,1,0:T(8,128)(2,1)}, u32[]{:S(2)}, u32[]{:S(2)}) collective-permute-start(bf16[2,3,192,128]{3,2,1,0:T(8,128)(2,1)} %get-tuple-element.33.pair0), channel_id=1, source_target_pairs={{0,1},{1,0},{2,3},{3,2},{4,5},{5,4},{6,7},{7,6},{8,9},{9,8},{10,11... | collective-permute-start | bytes 884744 | tf_op jit(solution)/shard_map/ppermute | solution.py:32
  78.2 14.0 %collective-permute-start.15 = (bf16[2,3,192,128]{3,2,1,0:T(8,128)(2,1)}, bf16[2,3,192,128]{3,2,1,0:T(8,128)(2,1)}, u32[]{:S(2)}, u32[]{:S(2)}) collective-permute-start(bf16[2,3,192,128]{3,2,1,0:T(8,128)(2,1)} %get-tuple-element.33.pair0), channel_id=1, source_target_pairs={{0,2},{1,3},{2,0},{3,1},{4,6},{5,7},{6,4},{7,5},{8,10},{9,11},{10,... | collective-permute-start | bytes 884744 | tf_op jit(solution)/shard_map/ppermute | solution.py:32
  79.6 19.4 %collective-permute-start.16 = (bf16[2,3,192,128]{3,2,1,0:T(8,128)(2,1)}, bf16[2,3,192,128]{3,2,1,0:T(8,128)(2,1)}, u32[]{:S(2)}, u32[]{:S(2)}) collective-permute-start(bf16[2,3,192,128]{3,2,1,0:T(8,128)(2,1)} %get-tuple-element.33.pair0), channel_id=1, source_target_pairs={{0,3},{1,2},{2,1},{3,0},{4,7},{5,6},{6,5},{7,4},{8,11},{9,10},{10,... | collective-permute-start | bytes 884744 | tf_op jit(solution)/shard_map/ppermute | solution.py:32
  80.0 21.2 %collective-permute-start.7 = (bf16[1168,128]{1,0:T(8,128)(2,1)}, bf16[1168,128]{1,0:T(8,128)(2,1)}, u32[]{:S(2)}, u32[]{:S(2)}) collective-permute-start(bf16[1168,128]{1,0:T(8,128)(2,1)} %get-tuple-element.25.refs_0_.kv0), channel_id=1, source_target_pairs={{0,4},{4,0},{8,12},{12,8},{1,5},{5,1},{9,13},{13,9},{2,6},{6,2},{1... | collective-permute-start | bytes 897032 | tf_op jit(solution)/shard_map/ppermute | solution.py:32
  84.9 19.1 %collective-permute-start.12 = (bf16[2,3,192,128]{3,2,1,0:T(8,128)(2,1)}, bf16[2,3,192,128]{3,2,1,0:T(8,128)(2,1)}, u32[]{:S(2)}, u32[]{:S(2)}) collective-permute-start(bf16[2,3,192,128]{3,2,1,0:T(8,128)(2,1)} %get-tuple-element.32), channel_id=1, source_target_pairs={{0,1},{1,0},{2,3},{3,2},{4,5},{5,4},{6,7},{7,6},{8,9},{9,8},{10,11... | collective-permute-start | bytes 884744 | tf_op jit(solution)/shard_map/ppermute | solution.py:32
  90.0 16.5 %collective-permute-start.6 = (bf16[4,4,2,4,8,128]{5,4,3,2,1,0:T(8,128)(2,1)}, bf16[4,4,2,4,8,128]{5,4,3,2,1,0:T(8,128)(2,1)}, u32[]{:S(2)}, u32[]{:S(2)}) collective-permute-start(bf16[4,4,2,4,8,128]{5,4,3,2,1,0:T(8,128)(2,1)} %bitcast.16.bias0), channel_id=1, source_target_pairs={{0,16},{16,0},{32,48},{48,32},{64,80},{80,64},{96,112},{112,96},{1... | collective-permute-start | bytes 786440 | tf_op jit(solution)/shard_map/ppermute | solution.py:719
  92.3 22.7 %collective-permute-start.8 = (bf16[1168,128]{1,0:T(8,128)(2,1)}, bf16[1168,128]{1,0:T(8,128)(2,1)}, u32[]{:S(2)}, u32[]{:S(2)}) collective-permute-start(bf16[1168,128]{1,0:T(8,128)(2,1)} %get-tuple-element.25.refs_0_.kv0), channel_id=1, source_target_pairs={{0,8},{4,12},{8,0},{12,4},{1,9},{5,13},{9,1},{13,5},{2,10},{6,14},... | collective-permute-start | bytes 897032 | tf_op jit(solution)/shard_map/ppermute | solution.py:32
  99.1 15.9 %collective-permute-start.9 = (bf16[1168,128]{1,0:T(8,128)(2,1)}, bf16[1168,128]{1,0:T(8,128)(2,1)}, u32[]{:S(2)}, u32[]{:S(2)}) collective-permute-start(bf16[1168,128]{1,0:T(8,128)(2,1)} %get-tuple-element.25.refs_0_.kv0), channel_id=1, source_target_pairs={{0,12},{4,8},{8,4},{12,0},{1,13},{5,9},{9,5},{13,1},{2,14},{6,10},... | collective-permute-start | bytes 897032 | tf_op jit(solution)/shard_map/ppermute | solution.py:32
  101.3 13.7 %collective-permute-start.10 = (bf16[4,4,2,4,8,128]{5,4,3,2,1,0:T(8,128)(2,1)}, bf16[4,4,2,4,8,128]{5,4,3,2,1,0:T(8,128)(2,1)}, u32[]{:S(2)}, u32[]{:S(2)}) collective-permute-start(bf16[4,4,2,4,8,128]{5,4,3,2,1,0:T(8,128)(2,1)} %bitcast.16.bias0), channel_id=1, source_target_pairs={{0,32},{16,48},{32,0},{48,16},{64,96},{80,112},{96,64},{112,80},{1... | collective-permute-start | bytes 786440 | tf_op jit(solution)/shard_map/ppermute | solution.py:719
  104.0 12.9 %collective-permute-start.11 = (bf16[4,4,2,4,8,128]{5,4,3,2,1,0:T(8,128)(2,1)}, bf16[4,4,2,4,8,128]{5,4,3,2,1,0:T(8,128)(2,1)}, u32[]{:S(2)}, u32[]{:S(2)}) collective-permute-start(bf16[4,4,2,4,8,128]{5,4,3,2,1,0:T(8,128)(2,1)} %bitcast.16.bias0), channel_id=1, source_target_pairs={{0,48},{16,32},{32,16},{48,0},{64,112},{80,96},{96,80},{112,64},{1... | collective-permute-start | bytes 786440 | tf_op jit(solution)/shard_map/ppermute | solution.py:719
  106.6 8.4 %collective-permute-start.13 = (bf16[3,192,128]{2,1,0:T(8,128)(2,1)}, bf16[3,192,128]{2,1,0:T(8,128)(2,1)}, u32[]{:S(2)}, u32[]{:S(2)}) collective-permute-start(bf16[3,192,128]{2,1,0:T(8,128)(2,1)} %join.4), channel_id=1, source_target_pairs={{0,2},{1,3},{2,0},{3,1},{4,6},{5,7},{6,4},{7,5},{8,10},{9,11},{10,... | collective-permute-start | bytes 442376 | tf_op jit(solution)/shard_map/ppermute | solution.py:32
  106.7 24.1 %all-to-all-start.3 = ((bf16[16,8,8,128]{3,2,1,0:T(8,128)(2,1)}), bf16[16,8,8,128]{3,2,1,0:T(8,128)(2,1)}, u32[]{:S(2)}, u32[]{:S(2)}) async-start(bf16[16,8,8,128]{3,2,1,0:T(8,128)(2,1)} %bitcast.35), calls=%async_computation.3 | async-start | bytes 524288 | tf_op jit(solution)/shard_map/all_to_all | solution.py:723
  121.7 2.0 %collective-permute-start.17 = (bf16[2,3,192,128]{3,2,1,0:T(8,128)(2,1)}, bf16[2,3,192,128]{3,2,1,0:T(8,128)(2,1)}, u32[]{:S(2)}, u32[]{:S(2)}) collective-permute-start(bf16[2,3,192,128]{3,2,1,0:T(8,128)(2,1)} %get-tuple-element.35), channel_id=1, source_target_pairs={{0,1},{1,0},{2,3},{3,2},{4,5},{5,4},{6,7},{7,6},{8,9},{9,8},{10,11... | collective-permute-start | bytes 884744 | tf_op jit(solution)/shard_map/ppermute | solution.py:32
  125.4 5.4 %collective-permute-start.18 = (bf16[3,192,128]{2,1,0:T(8,128)(2,1)}, bf16[3,192,128]{2,1,0:T(8,128)(2,1)}, u32[]{:S(2)}, u32[]{:S(2)}) collective-permute-start(bf16[3,192,128]{2,1,0:T(8,128)(2,1)} %join.5), channel_id=1, source_target_pairs={{0,2},{1,3},{2,0},{3,1},{4,6},{5,7},{6,4},{7,5},{8,10},{9,11},{10,... | collective-permute-start | bytes 442376 | tf_op jit(solution)/shard_map/ppermute | solution.py:32
  146.2 9.8 %collective-permute-start.19 = (bf16[1168,128]{1,0:T(8,128)(2,1)}, bf16[1168,128]{1,0:T(8,128)(2,1)}, u32[]{:S(2)}, u32[]{:S(2)}) collective-permute-start(bf16[1168,128]{1,0:T(8,128)(2,1)} %get-tuple-element.40.kv0), channel_id=1, source_target_pairs={{0,4},{4,0},{8,12},{12,8},{1,5},{5,1},{9,13},{13,9},{2,6},{6,2},{1... | collective-permute-start | bytes 897032 | tf_op jit(solution)/shard_map/ppermute | solution.py:32
  146.2 3.8 %collective-permute-start.22 = (bf16[3,192,128]{2,1,0:T(8,128)(2,1)}, bf16[3,192,128]{2,1,0:T(8,128)(2,1)}, u32[]{:S(2)}, u32[]{:S(2)}) collective-permute-start(bf16[3,192,128]{2,1,0:T(8,128)(2,1)} %get-tuple-element.41.refs_1_), channel_id=1, source_target_pairs={{0,1},{1,0},{2,3},{3,2},{4,5},{5,4},{6,7},{7,6},{8,9},{9,8},{10,11... | collective-permute-start | bytes 442376 | tf_op jit(solution)/shard_map/ppermute | solution.py:32
  146.5 5.7 %collective-permute-start.23 = (bf16[3,192,128]{2,1,0:T(8,128)(2,1)}, bf16[3,192,128]{2,1,0:T(8,128)(2,1)}, u32[]{:S(2)}, u32[]{:S(2)}) collective-permute-start(bf16[3,192,128]{2,1,0:T(8,128)(2,1)} %get-tuple-element.41.refs_1_), channel_id=1, source_target_pairs={{0,2},{1,3},{2,0},{3,1},{4,6},{5,7},{6,4},{7,5},{8,10},{9,11},{10,... | collective-permute-start | bytes 442376 | tf_op jit(solution)/shard_map/ppermute | solution.py:32
  148.0 7.9 %collective-permute-start.24 = (bf16[3,192,128]{2,1,0:T(8,128)(2,1)}, bf16[3,192,128]{2,1,0:T(8,128)(2,1)}, u32[]{:S(2)}, u32[]{:S(2)}) collective-permute-start(bf16[3,192,128]{2,1,0:T(8,128)(2,1)} %get-tuple-element.41.refs_1_), channel_id=1, source_target_pairs={{0,3},{1,2},{2,1},{3,0},{4,7},{5,6},{6,5},{7,4},{8,11},{9,10},{10,... | collective-permute-start | bytes 442376 | tf_op jit(solution)/shard_map/ppermute | solution.py:32
  148.4 15.4 %collective-permute-start.20 = (bf16[1168,128]{1,0:T(8,128)(2,1)}, bf16[1168,128]{1,0:T(8,128)(2,1)}, u32[]{:S(2)}, u32[]{:S(2)}) collective-permute-start(bf16[1168,128]{1,0:T(8,128)(2,1)} %get-tuple-element.40.kv0), channel_id=1, source_target_pairs={{0,8},{4,12},{8,0},{12,4},{1,9},{5,13},{9,1},{13,5},{2,10},{6,14},... | collective-permute-start | bytes 897032 | tf_op jit(solution)/shard_map/ppermute | solution.py:32
  150.0 16.2 %collective-permute-start.21 = (bf16[1168,128]{1,0:T(8,128)(2,1)}, bf16[1168,128]{1,0:T(8,128)(2,1)}, u32[]{:S(2)}, u32[]{:S(2)}) collective-permute-start(bf16[1168,128]{1,0:T(8,128)(2,1)} %get-tuple-element.40.kv0), channel_id=1, source_target_pairs={{0,12},{4,8},{8,4},{12,0},{1,13},{5,9},{9,5},{13,1},{2,14},{6,10},... | collective-permute-start | bytes 897032 | tf_op jit(solution)/shard_map/ppermute | solution.py:32
  159.9 2.2 %collective-permute-start.25 = (bf16[2,3,192,128]{3,2,1,0:T(8,128)(2,1)}, bf16[2,3,192,128]{3,2,1,0:T(8,128)(2,1)}, u32[]{:S(2)}, u32[]{:S(2)}) collective-permute-start(bf16[2,3,192,128]{3,2,1,0:T(8,128)(2,1)} %get-tuple-element.43), channel_id=1, source_target_pairs={{0,1},{1,0},{2,3},{3,2},{4,5},{5,4},{6,7},{7,6},{8,9},{9,8},{10,11... | collective-permute-start | bytes 884744 | tf_op jit(solution)/shard_map/ppermute | solution.py:32
  170.8 2.8 %collective-permute-start.26 = (bf16[2,3,192,128]{3,2,1,0:T(8,128)(2,1)}, bf16[2,3,192,128]{3,2,1,0:T(8,128)(2,1)}, u32[]{:S(2)}, u32[]{:S(2)}) collective-permute-start(bf16[2,3,192,128]{3,2,1,0:T(8,128)(2,1)} %get-tuple-element.45), channel_id=1, source_target_pairs={{0,1},{1,0},{2,3},{3,2},{4,5},{5,4},{6,7},{7,6},{8,9},{9,8},{10,11... | collective-permute-start | bytes 884744 | tf_op jit(solution)/shard_map/ppermute | solution.py:32
  172.1 6.3 %collective-permute-start.28 = (bf16[3,192,128]{2,1,0:T(8,128)(2,1)}, bf16[3,192,128]{2,1,0:T(8,128)(2,1)}, u32[]{:S(2)}, u32[]{:S(2)}) collective-permute-start(bf16[3,192,128]{2,1,0:T(8,128)(2,1)} %join.6.refs_1_), channel_id=1, source_target_pairs={{0,2},{1,3},{2,0},{3,1},{4,6},{5,7},{6,4},{7,5},{8,10},{9,11},{10,... | collective-permute-start | bytes 442376 | tf_op jit(solution)/shard_map/ppermute | solution.py:32
  175.4 5.4 %collective-permute-start.27 = (bf16[3,192,128]{2,1,0:T(8,128)(2,1)}, bf16[3,192,128]{2,1,0:T(8,128)(2,1)}, u32[]{:S(2)}, u32[]{:S(2)}) collective-permute-start(bf16[3,192,128]{2,1,0:T(8,128)(2,1)} %join.7), channel_id=1, source_target_pairs={{0,2},{1,3},{2,0},{3,1},{4,6},{5,7},{6,4},{7,5},{8,10},{9,11},{10,... | collective-permute-start | bytes 442376 | tf_op jit(solution)/shard_map/ppermute | solution.py:32
